TPU v7x, 256 devices: a whole 4x4x8 slice. The times are simulated.
256 devices in a mesh: dp: 4 (over x), ctx: 64 (over z, y, core).
Axes of the slice: x: 4, y: 4, z: 8, core: 2. Of those that a mesh axis runs over, the one named last changes fastest.
Arguments:
- queries: bfloat16 [32768, 1024], P(('dp', 'ctx')), parts along dimension 0, may hold values from -6 to 6
- keys: bfloat16 [32768, 1024], P(('dp', 'ctx')), parts along dimension 0, may hold values from -6 to 6
- values: bfloat16 [32768, 1024], P(('dp', 'ctx')), parts along dimension 0, may hold values from -6 to 6
- out_grad: bfloat16 [32768, 1024], P(('dp', 'ctx')), parts along dimension 0, may hold values from -6 to 6
- offsets: int32 [24, 8], P('dp'), parts along dimension 0, may hold values from 0 to 31, as said below
Outputs:
- attended: bfloat16 [32768, 1024], P(('dp', 'ctx')), parts along dimension 0
- query_grad: bfloat16 [32768, 1024], P(('dp', 'ctx')), parts along dimension 0
- key_grad: bfloat16 [32768, 1024], P(('dp', 'ctx')), parts along dimension 0
- value_grad: bfloat16 [32768, 1024], P(('dp', 'ctx')), parts along dimension 0
There are 4 independent parts, one for each index of `dp`. A program takes and returns all parts, laid end to end along the dimension named above; each array names one. Nothing has to cross between parts.
Inputs may be any that keep to these rules, and one draw needn't show every extreme that they name: offsets[l, h] is below 2^l and equals offsets[5, h] modulo 2^l; the top level's offsets of the heads are distinct.
All inputs are finite; a program needn't handle non-finite values.
Results may differ from a plain program's by a relative error of at most 0.0049.
The roundings to bfloat16 on the way count: a program that leaves them out, or rounds other values in their place, can miss the bound.
Values may be sent and summed in bfloat16 or wider, within the bound.
No kernel may reach another device: no remote copies, remote signals or barrier semaphores. Data moves between devices by JAX's collectives and lax.ppermute only.
A program may use at most 128 MiB of HBM per device.

v0:
```python
import math

import jax
import jax.numpy as jnp
from jax import lax
from jax.experimental import pallas as pl
from jax.experimental.pallas import tpu as pltpu
from jax.sharding import PartitionSpec as P

HEADS = 8
WIDTH = 128
ROWS = 128
PLANE = HEADS * ROWS
DEPTH = 8
SEG = 256
SCALE = 1.0 / math.sqrt(WIDTH)
F32 = jnp.float32
BF16 = jnp.bfloat16


def nt(a, b):
    return lax.dot_general(a, b, (((1,), (1,)), ((), ())), preferred_element_type=F32)


def nn(a, b):
    return lax.dot_general(a, b, (((1,), (0,)), ((), ())), preferred_element_type=F32)


def tn(a, b):
    return lax.dot_general(a, b, (((0,), (0,)), ((), ())), preferred_element_type=F32)


def attend(q, k, v):
    scores = nt(q, k) * SCALE
    peak = jnp.max(scores, axis=1, keepdims=True)
    grown = jnp.exp(scores - peak)
    mass = jnp.sum(grown, axis=1, keepdims=True)
    weights = (grown * (1.0 / mass)).astype(BF16)
    return nn(weights, v), peak + jnp.log(mass)


def merge(out, total, more, more_total):
    peak = jnp.maximum(total, more_total)
    joined = peak + jnp.log(jnp.exp(total - peak) + jnp.exp(more_total - peak))
    return out * jnp.exp(total - joined) + more * jnp.exp(more_total - joined), joined


def wide(column, rows):
    return jnp.broadcast_to(column, (rows, WIDTH))


def chosen(offs):
    return (
        pl.ds(offs[5], 32, stride=32),
        pl.ds(offs[5] ^ 16, 32, stride=32),
        pl.ds(offs[4] ^ 8, 64, stride=16),
    )


def load_chosen(ref, offs):
    return jnp.concatenate([ref[s, :] for s in chosen(offs)], axis=0)


def store_chosen(ref, offs, rows):
    first, second, third = chosen(offs)
    ref[first, :] = rows[:32]
    ref[second, :] = rows[32:64]
    ref[third, :] = rows[64:]


def pick_kernel(offs, x, g, wide_rows):
    for t in range(4):
        wide_rows[...] = x[:, t].reshape(PLANE, WIDTH).astype(F32)
        g[t] = load_chosen(wide_rows, offs).astype(BF16)


def near_kernel(offs, x, o, t, qs, ks, vs):
    for index, ref in enumerate((qs, ks, vs)):
        ref[...] = x[:, index].reshape(PLANE, WIDTH).astype(F32)
    for s in range(4):
        q, k, v = (x[2 * s : 2 * s + 2, index].reshape(SEG, WIDTH) for index in range(3))
        out, total = attend(q, k, v)
        o[s * SEG : (s + 1) * SEG] = out
        t[s * SEG : (s + 1) * SEG] = wide(total, SEG)
    for level, begin in ((1, 0), (1, 512), (2, 0)):
        rows = pl.ds(offs[level] + begin, SEG, stride=2**level)
        q, k, v = (ref[rows, :].astype(BF16) for ref in (qs, ks, vs))
        out, total = attend(q, k, v)
        out, total = merge(o[rows, :], t[rows, :], out, wide(total, SEG))
        o[rows, :] = out
        t[rows, :] = total


def far_blocks(g, a1, a2, a3, index):
    own = g[index]
    three = jnp.concatenate([own, a1[index]], axis=0)
    four = jnp.concatenate([own[:64], a1[index, :64], a2[0, index], a2[1, index]], axis=0)
    five = jnp.concatenate(
        [own[:32], a1[index, :32], a2[0, index, :32], a2[1, index, :32]]
        + [a3[z, index] for z in range(4)],
        axis=0,
    )
    return three, four, five


def far_kernel(offs, x, g, a1, a2, a3, o_in, t_in, att, stats, message, o, t):
    keys, values = (far_blocks(g, a1, a2, a3, index) for index in (1, 2))
    out, total = load_chosen(o_in, offs), load_chosen(t_in, offs)
    for level in range(3):
        rows = 128 >> level
        more, more_total = attend(g[0][:rows], keys[level], values[level])
        part, part_total = merge(out[:rows], total[:rows], more, wide(more_total, rows))
        if level:
            part = jnp.concatenate([part, out[rows:]], axis=0)
            part_total = jnp.concatenate([part_total, total[rows:]], axis=0)
        out, total = part, part_total
    o[...] = o_in[...]
    t[...] = t_in[...]
    store_chosen(o, offs, out)
    store_chosen(t, offs, total)
    merged = o[...]
    att[...] = merged.astype(BF16).reshape(HEADS, ROWS, WIDTH)
    delta = jnp.sum(merged * x[:, 3].reshape(PLANE, WIDTH).astype(F32), axis=1, keepdims=True)
    lane = lax.broadcasted_iota(jnp.int32, (PLANE, WIDTH), 1)
    stats[...] = jnp.where(lane % 8 < 4, t[...], delta)
    message[...] = load_chosen(stats, offs).T[:8]


def score_parts(q, k, v, do, stat):
    chance = jnp.exp(nt(q, k) * SCALE - stat[:, 0:1])
    score = (chance * (nt(do, v) - stat[:, 4:5]) * SCALE).astype(BF16)
    return chance.astype(BF16), score


def back_kernel(offs, x, g, a1, a2, a3, stats, dq_out, dk, dv, qs, ks, vs, ds, dq):
    for index, ref in enumerate((qs, ks, vs, ds)):
        ref[...] = x[:, index].reshape(PLANE, WIDTH).astype(F32)
    for s in range(4):
        rows = slice(s * SEG, (s + 1) * SEG)
        q, k, v, do = (x[2 * s : 2 * s + 2, index].reshape(SEG, WIDTH) for index in range(4))
        chance, score = score_parts(q, k, v, do, stats[rows])
        dq[rows] = nn(score, k)
        dk[rows] = tn(score, q)
        dv[rows] = tn(chance, do)
    for level, begin in ((1, 0), (1, 512), (2, 0)):
        rows = pl.ds(offs[level] + begin, SEG, stride=2**level)
        q, k, v, do = (ref[rows, :].astype(BF16) for ref in (qs, ks, vs, ds))
        chance, score = score_parts(q, k, v, do, stats[rows, :])
        dq[rows, :] = dq[rows, :] + nn(score, k)
        dk[rows, :] = dk[rows, :] + tn(score, q)
        dv[rows, :] = dv[rows, :] + tn(chance, do)
    keys, values = (far_blocks(g, a1, a2, a3, index) for index in (1, 2))
    stat = load_chosen(stats, offs)
    total = load_chosen(dq, offs)
    for level in range(3):
        rows = 128 >> level
        _, score = score_parts(g[0][:rows], keys[level], values[level], g[3][:rows], stat[:rows])
        part = total[:rows] + nn(score, keys[level])
        total = jnp.concatenate([part, total[rows:]], axis=0) if level else part
    store_chosen(dq, offs, total)
    dq_out[...] = dq[...].astype(BF16).reshape(HEADS, ROWS, WIDTH)


def far_stats(m0, m1, m2, m3):
    lane = lax.broadcasted_iota(jnp.int32, (8, WIDTH), 1)

    def pair(a, b):
        return jnp.where(lane < 64, a, pltpu.roll(b, 64, 1))

    def four(a, b, c, d):
        return jnp.where(
            lane < 64,
            jnp.where(lane < 32, a, pltpu.roll(b, 32, 1)),
            jnp.where(lane < 96, pltpu.roll(c, 64, 1), pltpu.roll(d, 96, 1)),
        )

    three = jnp.concatenate([m0, m1], axis=1)
    wider = jnp.concatenate([pair(m0, m1), pair(m2[0], m2[1])], axis=1)
    widest = jnp.concatenate([four(m0, m1, m2[0], m2[1]), four(m3[0], m3[1], m3[2], m3[3])], axis=1)
    return three, wider, widest


def keys_kernel(offs, g, a1, a2, a3, m0, m1, m2, m3, dk_in, dv_in, dk_out, dv_out, dk, dv):
    queries, grads = (far_blocks(g, a1, a2, a3, index) for index in (0, 3))
    stats = far_stats(m0[...], m1[...], m2[...], m3[...])
    dk[...] = dk_in[...]
    dv[...] = dv_in[...]
    key_total, value_total = load_chosen(dk, offs), load_chosen(dv, offs)
    for level in range(3):
        rows = 128 >> level
        chance = jnp.exp(nt(g[1][:rows], queries[level]) * SCALE - stats[level][0:1])
        score = (chance * (nt(g[2][:rows], grads[level]) - stats[level][4:5]) * SCALE).astype(BF16)
        key_part = key_total[:rows] + nn(score, queries[level])
        value_part = value_total[:rows] + nn(chance.astype(BF16), grads[level])
        if level:
            key_part = jnp.concatenate([key_part, key_total[rows:]], axis=0)
            value_part = jnp.concatenate([value_part, value_total[rows:]], axis=0)
        key_total, value_total = key_part, value_part
    store_chosen(dk, offs, key_total)
    store_chosen(dv, offs, value_total)
    dk_out[...] = dk[...].astype(BF16).reshape(HEADS, ROWS, WIDTH)
    dv_out[...] = dv[...].astype(BF16).reshape(HEADS, ROWS, WIDTH)


def call(kernel, name, outs, scratch, *args):
    smem = pl.BlockSpec(memory_space=pltpu.SMEM)
    vmem = pl.BlockSpec(memory_space=pltpu.VMEM)
    return pl.pallas_call(
        kernel,
        name=name,
        out_shape=tuple(jax.ShapeDtypeStruct(shape, dtype) for shape, dtype in outs),
        in_specs=[smem] + [vmem] * (len(args) - 1),
        out_specs=(vmem,) * len(outs),
        scratch_shapes=[pltpu.VMEM(shape, F32) for shape in scratch],
        compiler_params=pltpu.CompilerParams(vmem_limit_bytes=40 * 2**20),
    )(*args)


def across(array, flip):
    moves = [(HEADS * z + i, HEADS * (z ^ flip) + i) for z in range(DEPTH) for i in range(HEADS)]
    return lax.ppermute(array, "ctx", moves)


def planes():
    return [[HEADS * z + i for i in range(HEADS)] for z in range(DEPTH)]


def shards(queries, keys, values, out_grad, offsets):
    head = lax.axis_index("ctx") % HEADS
    offs = lax.dynamic_index_in_dim(offsets, head, axis=1, keepdims=False)
    stacked = jnp.stack(
        [a.reshape(ROWS, HEADS, WIDTH).transpose(1, 0, 2) for a in (queries, keys, values, out_grad)],
        axis=1,
    )
    x = lax.all_to_all(stacked, "ctx", 0, 0, axis_index_groups=planes(), tiled=True)
    full = (PLANE, WIDTH)
    blocks = (HEADS, ROWS, WIDTH)
    (g,) = call(pick_kernel, "pick", [((4, ROWS, WIDTH), BF16)], [full], offs, x)
    a1 = across(g, 1)
    a2 = across(jnp.stack([g[:, :64], a1[:, :64]]), 3)
    a3 = across(jnp.concatenate([jnp.stack([g[:, :32], a1[:, :32]]), a2[:, :, :32]]), 7)
    o, t = call(near_kernel, "near", [(full, F32), (full, F32)], [full] * 3, offs, x)
    att, stats, m0 = call(
        far_kernel,
        "far",
        [(blocks, BF16), (full, F32), ((8, WIDTH), F32)],
        [full] * 2,
        offs, x, g, a1, a2, a3, o, t,
    )
    m1 = across(m0, 1)
    m2 = across(jnp.stack([m0, m1]), 3)
    m3 = across(jnp.concatenate([jnp.stack([m0, m1]), m2]), 7)
    dq, dk, dv = call(
        back_kernel,
        "back",
        [(blocks, BF16), (full, F32), (full, F32)],
        [full] * 5,
        offs, x, g, a1, a2, a3, stats,
    )
    dk, dv = call(
        keys_kernel,
        "keys",
        [(blocks, BF16), (blocks, BF16)],
        [full] * 2,
        offs, g, a1, a2, a3, m0, m1, m2, m3, dk, dv,
    )
    back = lax.all_to_all(
        jnp.stack([att, dq, dk, dv], axis=1), "ctx", 0, 0, axis_index_groups=planes(), tiled=True
    )
    return tuple(back[:, i].transpose(1, 0, 2).reshape(ROWS, HEADS * WIDTH) for i in range(4))


def solution(mesh):
    rows = P(("dp", "ctx"), None)
    return jax.shard_map(
        shards,
        mesh=mesh,
        in_specs=(rows,) * 4 + (P("dp", None),),
        out_specs=(rows,) * 4,
        check_vma=False,
    )
```

profile of v0, /device:TPU:1, one launch (start us, length us, event | category | flops | bytes accessed | tf_op | source)
XLA Modules:
  0.0 92.3 jit_solution(672447600460332083)
XLA Ops:
  0.6 0.0 copy-start
  0.6 1.1 %copy.31 = bf16[128,1024]{0,1:T(8,128)(2,1)S(1)} copy(bf16[128,1024]{1,0:T(8,128)(2,1)} %param.8) | data formatting | bytes 524288 | tf_op args[3]
  1.8 0.0 copy-start.1
  1.8 0.2 copy.32
  2.0 0.8 copy-done.1
  2.7 0.2 copy.25
  2.9 0.0 copy-start.2
  2.9 0.2 copy.26
  3.1 0.8 copy-done.2
  3.9 0.2 copy.27
  4.1 0.0 copy-start.3
  4.1 0.2 copy.28
  4.3 0.8 copy-done.3
  5.0 0.2 copy.29
  5.2 0.2 copy.30
  5.4 1.1 %pad_maximum_fusion = bf16[8,4,128,128]{3,2,1,0:T(8,128)(2,1)} fusion(bf16[8,1,128,128]{3,2,1,0:T(8,128)(2,1)S(1)} %bitcast.66, bf16[8,1,128,128]{3,2,1,0:T(8,128)(2,1)S(1)} %bitcast.69, bf16[8,1,128,128]{3,2,1,0:T(8,128)(2,1)S(1)} %bitcast.68, bf16[8,1,128,128]{3,2,1,0:T(8,128)(2,1)S(1)} %bitcast.67), kind=kLoop, calls=%fused_computation | loop fusion | flops 1572864 | bytes 2097152 | tf_op jit(solution)/shard_map/stack | solution.py:231
  6.5 6.7 %all-to-all-start = ((bf16[8,4,128,128]{3,2,1,0:T(8,128)(2,1)}), bf16[8,4,128,128]{3,2,1,0:T(8,128)(2,1)S(1)}, u32[]{:S(2)}, u32[]{:S(2)}) async-start(bf16[8,4,128,128]{3,2,1,0:T(8,128)(2,1)} %pad_maximum_fusion), calls=%async_computation | async-start | bytes 2097152 | tf_op jit(solution)/shard_map/all_to_all | solution.py:235
  13.2 0.0 copy-done
  13.2 0.2 dynamic-slice_reduce_fusion.offs
  13.4 14.9 %all-to-all-done.x = bf16[8,4,128,128]{3,2,1,0:T(8,128)(2,1)S(1)} async-done(((bf16[8,4,128,128]{3,2,1,0:T(8,128)(2,1)}), bf16[8,4,128,128]{3,2,1,0:T(8,128)(2,1)S(1)}, u32[]{:S(2)}, u32[]{:S(2)}) %all-to-all-start) | async-done | bytes 1048608 | tf_op jit(solution)/shard_map/all_to_all | solution.py:235
  28.3 0.9 pick.1.g
  29.2 1.0 %collective-permute-start = (bf16[4,128,128]{2,1,0:T(8,128)(2,1)S(1)}, bf16[4,128,128]{2,1,0:T(8,128)(2,1)S(1)}, u32[]{:S(2)}, u32[]{:S(2)}) collective-permute-start(bf16[4,128,128]{2,1,0:T(8,128)(2,1)S(1)} %pick.1.g), channel_id=1, source_target_pairs={{0,8},{1,9},{2,10},{3,11},{4,12},{5,13},{6,14},{7,15},{8,0},{9,1},... | collective-permute-start | bytes 393224 | tf_op jit(solution)/shard_map/ppermute | solution.py:221
  30.2 3.2 %collective-permute-done.a1 = bf16[4,128,128]{2,1,0:T(8,128)(2,1)S(1)} collective-permute-done((bf16[4,128,128]{2,1,0:T(8,128)(2,1)S(1)}, bf16[4,128,128]{2,1,0:T(8,128)(2,1)S(1)}, u32[]{:S(2)}, u32[]{:S(2)}) %collective-permute-start) | collective-permute-done | bytes 131104 | tf_op jit(solution)/shard_map/ppermute | solution.py:221
  33.5 3.7 %collective-permute-start.1 = (bf16[2,4,64,128]{3,2,1,0:T(8,128)(2,1)S(1)}, bf16[2,4,64,128]{3,2,1,0:T(8,128)(2,1)S(1)}, u32[]{:S(2)}, u32[]{:S(2)}) collective-permute-start(bf16[2,4,64,128]{3,2,1,0:T(8,128)(2,1)S(1)} %pad_maximum_fusion.2), channel_id=1, source_target_pairs={{0,24},{1,25},{2,26},{3,27},{4,28},{5,29},{6,30},{7,31},{8,16},{9,... | collective-permute-start | bytes 393224 | tf_op jit(solution)/shard_map/ppermute | solution.py:221
  37.2 2.5 %collective-permute-done.1.a2 = bf16[2,4,64,128]{3,2,1,0:T(8,128)(2,1)S(1)} collective-permute-done((bf16[2,4,64,128]{3,2,1,0:T(8,128)(2,1)S(1)}, bf16[2,4,64,128]{3,2,1,0:T(8,128)(2,1)S(1)}, u32[]{:S(2)}, u32[]{:S(2)}) %collective-permute-start.1) | collective-permute-done | bytes 131104 | tf_op jit(solution)/shard_map/ppermute | solution.py:221
  39.7 4.6 %collective-permute-start.2 = (bf16[4,4,32,128]{3,2,1,0:T(8,128)(2,1)S(1)}, bf16[4,4,32,128]{3,2,1,0:T(8,128)(2,1)S(1)}, u32[]{:S(2)}, u32[]{:S(2)}) collective-permute-start(bf16[4,4,32,128]{3,2,1,0:T(8,128)(2,1)S(1)} %pad_maximum_fusion.3), channel_id=1, source_target_pairs={{0,56},{1,57},{2,58},{3,59},{4,60},{5,61},{6,62},{7,63},{8,48},{9,... | collective-permute-start | bytes 393224 | tf_op jit(solution)/shard_map/ppermute | solution.py:221
  44.2 2.2 %near.1 = (f32[1024,128]{1,0:T(8,128)S(1)}, f32[1024,128]{1,0:T(8,128)S(1)}) custom-call(s32[6]{0:T(128)S(1)} %dynamic-slice_reduce_fusion.offs, bf16[8,4,128,128]{3,2,1,0:T(8,128)(2,1)S(1)} %all-to-all-done.x), custom_call_target="tpu_custom_call" | custom-call | tf_op jit(solution)/shard_map/near/pallas_call | solution.py:208
  46.5 0.5 collective-permute-done.2.a3
  47.0 1.7 %far.1 = (bf16[8,128,128]{2,1,0:T(8,128)(2,1)S(1)}, f32[1024,128]{1,0:T(8,128)S(1)}, f32[8,128]{1,0:T(8,128)S(1)}) custom-call(s32[6]{0:T(128)S(1)} %dynamic-slice_reduce_fusion.offs, bf16[8,4,128,128]{3,2,1,0:T(8,128)(2,1)S(1)} %all-to-all-done.x, bf16[4,128,128]{2,1,0:T(8,128)(2,1)S(1)} %pick.1.g, bf16[4,128,128]{2,1,0:T(8,128)(2,1)S(1)} %collective-permute-done.a1, ...), custom_call_target="tpu_custom_call" | custom-call | tf_op jit(solution)/shard_map/far/pallas_call | solution.py:208
  48.7 2.2 %collective-permute-start.3 = (f32[8,128]{1,0:T(8,128)S(1)}, f32[8,128]{1,0:T(8,128)S(1)}, u32[]{:S(2)}, u32[]{:S(2)}) collective-permute-start(f32[8,128]{1,0:T(8,128)S(1)} %get-tuple-element.19.m0), channel_id=1, source_target_pairs={{0,8},{1,9},{2,10},{3,11},{4,12},{5,13},{6,14},{7,15},{8,0},{9,1},... | collective-permute-start | bytes 12296 | tf_op jit(solution)/shard_map/ppermute | solution.py:221
  50.9 1.0 %collective-permute-done.3.m1 = f32[8,128]{1,0:T(8,128)S(1)} collective-permute-done((f32[8,128]{1,0:T(8,128)S(1)}, f32[8,128]{1,0:T(8,128)S(1)}, u32[]{:S(2)}, u32[]{:S(2)}) %collective-permute-start.3) | collective-permute-done | bytes 4128 | tf_op jit(solution)/shard_map/ppermute | solution.py:221
  51.9 1.2 %collective-permute-start.4 = (f32[2,8,128]{2,1,0:T(8,128)S(1)}, f32[2,8,128]{2,1,0:T(8,128)S(1)}, u32[]{:S(2)}, u32[]{:S(2)}) collective-permute-start(f32[2,8,128]{2,1,0:T(8,128)S(1)} %pad_maximum_fusion.5), channel_id=1, source_target_pairs={{0,24},{1,25},{2,26},{3,27},{4,28},{5,29},{6,30},{7,31},{8,16},{9,... | collective-permute-start | bytes 24584 | tf_op jit(solution)/shard_map/ppermute | solution.py:221
  53.2 3.1 %collective-permute-done.4.m2 = f32[2,8,128]{2,1,0:T(8,128)S(1)} collective-permute-done((f32[2,8,128]{2,1,0:T(8,128)S(1)}, f32[2,8,128]{2,1,0:T(8,128)S(1)}, u32[]{:S(2)}, u32[]{:S(2)}) %collective-permute-start.4) | collective-permute-done | bytes 8224 | tf_op jit(solution)/shard_map/ppermute | solution.py:221
  56.2 2.4 %collective-permute-start.5 = (f32[4,8,128]{2,1,0:T(8,128)S(1)}, f32[4,8,128]{2,1,0:T(8,128)S(1)}, u32[]{:S(2)}, u32[]{:S(2)}) collective-permute-start(f32[4,8,128]{2,1,0:T(8,128)S(1)} %pad_maximum_fusion.4), channel_id=1, source_target_pairs={{0,56},{1,57},{2,58},{3,59},{4,60},{5,61},{6,62},{7,63},{8,48},{9,... | collective-permute-start | bytes 49160 | tf_op jit(solution)/shard_map/ppermute | solution.py:221
  58.6 3.6 %back.1 = (bf16[8,128,128]{2,1,0:T(8,128)(2,1)S(1)}, f32[1024,128]{1,0:T(8,128)S(1)}, f32[1024,128]{1,0:T(8,128)S(1)}) custom-call(s32[6]{0:T(128)S(1)} %dynamic-slice_reduce_fusion.offs, bf16[8,4,128,128]{3,2,1,0:T(8,128)(2,1)S(1)} %all-to-all-done.x, bf16[4,128,128]{2,1,0:T(8,128)(2,1)S(1)} %pick.1.g, bf16[4,128,128]{2,1,0:T(8,128)(2,1)S(1)} %collective-permute-done.a1, ...), custom_call_target="tpu_custom_call" | custom-call | tf_op jit(solution)/shard_map/back/pallas_call | solution.py:208
  62.3 0.0 collective-permute-done.5.m3
  62.3 1.3 %keys.1 = (bf16[8,128,128]{2,1,0:T(8,128)(2,1)S(1)}, bf16[8,128,128]{2,1,0:T(8,128)(2,1)S(1)}) custom-call(s32[6]{0:T(128)S(1)} %dynamic-slice_reduce_fusion.offs, bf16[4,128,128]{2,1,0:T(8,128)(2,1)S(1)} %pick.1.g, bf16[4,128,128]{2,1,0:T(8,128)(2,1)S(1)} %collective-permute-done.a1, bf16[2,4,64,128]{3,2,1,0:T(8,128)(2,1)S(1)} %collective-permute-done.1.a2, ...), custom_call_target="tpu_custom_call" | custom-call | tf_op jit(solution)/shard_map/keys/pallas_call | solution.py:208
  63.6 0.1 pad_maximum_fusion.1
  63.7 0.1 copy.33
  63.9 24.2 %all_to_all.10 = bf16[8,4,128,128]{3,2,1,0:T(8,128)(2,1)S(1)} all-to-all(bf16[8,4,128,128]{3,2,1,0:T(8,128)(2,1)S(1)} %copy.33), channel_id=1, replica_groups={{0,1,2,3,4,5,6,7},{8,9,10,11,12,13,14,15},{16,17,18,19,20,21,22,23},{24..., dimensions={0} | all-to-all | bytes 2097152 | tf_op jit(solution)/shard_map/all_to_all | solution.py:267
  88.0 0.1 fusion
  88.1 0.2 copy.42
  88.3 0.9 copy.38
  89.2 0.2 copy.43
  89.4 0.9 copy.39
  90.2 0.2 copy.44
  90.4 0.9 copy.40
  91.3 0.2 copy.45
  91.5 0.9 copy.41
  (9 shorter events, 0.1 us)
Async XLA Ops:
  0.6 12.6 %copy-start = (s32[6,8]{1,0:T(8,128)S(1)}, s32[6,8]{1,0:T(8,128)}, u32[]{:S(2)}) copy-start(s32[6,8]{1,0:T(8,128)} %param.9) | copy-start | bytes 580
  1.8 1.0 %copy-start.1 = (bf16[128,1024]{1,0:T(8,128)(2,1)S(1)}, bf16[128,1024]{1,0:T(8,128)(2,1)}, u32[]{:S(2)}) copy-start(bf16[128,1024]{1,0:T(8,128)(2,1)} %param.5) | copy-start | bytes 786436
  2.9 1.0 %copy-start.2 = (bf16[128,1024]{1,0:T(8,128)(2,1)S(1)}, bf16[128,1024]{1,0:T(8,128)(2,1)}, u32[]{:S(2)}) copy-start(bf16[128,1024]{1,0:T(8,128)(2,1)} %param.6) | copy-start | bytes 786436
  4.1 1.0 %copy-start.3 = (bf16[128,1024]{1,0:T(8,128)(2,1)S(1)}, bf16[128,1024]{1,0:T(8,128)(2,1)}, u32[]{:S(2)}) copy-start(bf16[128,1024]{1,0:T(8,128)(2,1)} %param.7) | copy-start | bytes 786436
  6.5 21.8 %all-to-all-start = ((bf16[8,4,128,128]{3,2,1,0:T(8,128)(2,1)}), bf16[8,4,128,128]{3,2,1,0:T(8,128)(2,1)S(1)}, u32[]{:S(2)}, u32[]{:S(2)}) async-start(bf16[8,4,128,128]{3,2,1,0:T(8,128)(2,1)} %pad_maximum_fusion), calls=%async_computation | async-start | bytes 2097152 | tf_op jit(solution)/shard_map/all_to_all | solution.py:235
  29.2 4.2 %collective-permute-start = (bf16[4,128,128]{2,1,0:T(8,128)(2,1)S(1)}, bf16[4,128,128]{2,1,0:T(8,128)(2,1)S(1)}, u32[]{:S(2)}, u32[]{:S(2)}) collective-permute-start(bf16[4,128,128]{2,1,0:T(8,128)(2,1)S(1)} %pick.1.g), channel_id=1, source_target_pairs={{0,8},{1,9},{2,10},{3,11},{4,12},{5,13},{6,14},{7,15},{8,0},{9,1},... | collective-permute-start | bytes 393224 | tf_op jit(solution)/shard_map/ppermute | solution.py:221
  33.5 6.1 %collective-permute-start.1 = (bf16[2,4,64,128]{3,2,1,0:T(8,128)(2,1)S(1)}, bf16[2,4,64,128]{3,2,1,0:T(8,128)(2,1)S(1)}, u32[]{:S(2)}, u32[]{:S(2)}) collective-permute-start(bf16[2,4,64,128]{3,2,1,0:T(8,128)(2,1)S(1)} %pad_maximum_fusion.2), channel_id=1, source_target_pairs={{0,24},{1,25},{2,26},{3,27},{4,28},{5,29},{6,30},{7,31},{8,16},{9,... | collective-permute-start | bytes 393224 | tf_op jit(solution)/shard_map/ppermute | solution.py:221
  39.7 7.3 %collective-permute-start.2 = (bf16[4,4,32,128]{3,2,1,0:T(8,128)(2,1)S(1)}, bf16[4,4,32,128]{3,2,1,0:T(8,128)(2,1)S(1)}, u32[]{:S(2)}, u32[]{:S(2)}) collective-permute-start(bf16[4,4,32,128]{3,2,1,0:T(8,128)(2,1)S(1)} %pad_maximum_fusion.3), channel_id=1, source_target_pairs={{0,56},{1,57},{2,58},{3,59},{4,60},{5,61},{6,62},{7,63},{8,48},{9,... | collective-permute-start | bytes 393224 | tf_op jit(solution)/shard_map/ppermute | solution.py:221
  48.7 3.2 %collective-permute-start.3 = (f32[8,128]{1,0:T(8,128)S(1)}, f32[8,128]{1,0:T(8,128)S(1)}, u32[]{:S(2)}, u32[]{:S(2)}) collective-permute-start(f32[8,128]{1,0:T(8,128)S(1)} %get-tuple-element.19.m0), channel_id=1, source_target_pairs={{0,8},{1,9},{2,10},{3,11},{4,12},{5,13},{6,14},{7,15},{8,0},{9,1},... | collective-permute-start | bytes 12296 | tf_op jit(solution)/shard_map/ppermute | solution.py:221
  51.9 4.3 %collective-permute-start.4 = (f32[2,8,128]{2,1,0:T(8,128)S(1)}, f32[2,8,128]{2,1,0:T(8,128)S(1)}, u32[]{:S(2)}, u32[]{:S(2)}) collective-permute-start(f32[2,8,128]{2,1,0:T(8,128)S(1)} %pad_maximum_fusion.5), channel_id=1, source_target_pairs={{0,24},{1,25},{2,26},{3,27},{4,28},{5,29},{6,30},{7,31},{8,16},{9,... | collective-permute-start | bytes 24584 | tf_op jit(solution)/shard_map/ppermute | solution.py:221
  56.2 6.0 %collective-permute-start.5 = (f32[4,8,128]{2,1,0:T(8,128)S(1)}, f32[4,8,128]{2,1,0:T(8,128)S(1)}, u32[]{:S(2)}, u32[]{:S(2)}) collective-permute-start(f32[4,8,128]{2,1,0:T(8,128)S(1)} %pad_maximum_fusion.4), channel_id=1, source_target_pairs={{0,56},{1,57},{2,58},{3,59},{4,60},{5,61},{6,62},{7,63},{8,48},{9,... | collective-permute-start | bytes 49160 | tf_op jit(solution)/shard_map/ppermute | solution.py:221
where the time goes:
time: 92.6 us; the launch traced here: 92.3 us
  waiting for transfers between devices  25.2 us (27%)
  blocking collectives  24.2 us (26%)
  starting transfers between devices  21.8 us (24%)
  Pallas kernels  9.76 us (11%)
  local copies, waits for them, and re-layouts  9.22 us (10%)
  other arithmetic  1.28 us (1%)
    all_to_all x1, blocking collectives, shards(): lax.all_to_all(jnp.stack([att, dq, dk, dv], axis=1), 'ctx', 0, 0, axis_in...  24.2 us
    ppermute x6, starting transfers between devices, across(): return lax.ppermute(array, 'ctx', moves)  15.1 us
    all_to_all x1, waiting for transfers between devices, shards(): lax.all_to_all(stacked, 'ctx', 0, 0, axis_index_groups=planes(), tiled=True)  14.9 us
    ppermute x6, waiting for transfers between devices, across(): return lax.ppermute(array, 'ctx', moves)  10.3 us
    pallas_call x5, Pallas kernels, call(): pl.pallas_call(kernel, name=name, out_shape=tuple((jax.ShapeDtypeStruct(s...  9.76 us
    unnamed x20, local copies, waits for them, and re-layouts  8.09 us
    all_to_all x1, starting transfers between devices, shards(): lax.all_to_all(stacked, 'ctx', 0, 0, axis_index_groups=planes(), tiled=True)  6.7 us
  transfers between devices with their start and end apart: 7, of which 6 were waited for; matrix products, arithmetic and copies ran while one was open for 0% of the time, Pallas kernels for 6%

commit v1 on v0

v1 whole, which is shorter than its diff:
```python
import math

import jax
import jax.numpy as jnp
from jax import lax
from jax.experimental import pallas as pl
from jax.experimental.pallas import tpu as pltpu
from jax.sharding import PartitionSpec as P

HEADS = 8
WIDTH = 128
ROWS = 128
CHIP = 2 * ROWS
CHIPS = 4
PLANE = 2 * CHIPS
DEPTH = 8
SEG = 256
BODY = 4 * ROWS
MESSAGE = BODY + 32
SCALE = 1.0 / math.sqrt(WIDTH)
F32 = jnp.float32
BF16 = jnp.bfloat16


def nt(a, b):
    return lax.dot_general(a, b, (((1,), (1,)), ((), ())), preferred_element_type=F32)


def nn(a, b):
    return lax.dot_general(a, b, (((1,), (0,)), ((), ())), preferred_element_type=F32)


def tn(a, b):
    return lax.dot_general(a, b, (((0,), (0,)), ((), ())), preferred_element_type=F32)


def join(parts):
    return jnp.concatenate(parts, axis=0)


def attend(q, k, v):
    scores = nt(q, k) * SCALE
    peak = jnp.max(scores, axis=1, keepdims=True)
    grown = jnp.exp(scores - peak)
    mass = jnp.sum(grown, axis=1, keepdims=True)
    weights = (grown * (1.0 / mass)).astype(BF16)
    return nn(weights, v), peak + jnp.log(mass)


def dotted(a, b):
    return jnp.sum(a.astype(F32) * b, axis=1, keepdims=True)


def mixed(total, delta):
    rows = total.shape[0]
    lane = lax.broadcasted_iota(jnp.int32, (rows, WIDTH), 1)
    return jnp.where(lane % 8 < 4, total, delta)


def total_of(stat):
    return stat[:, 0:1]


def delta_of(stat):
    return stat[:, 4:5]


def combine(stat, total, delta):
    old = total_of(stat)
    peak = jnp.maximum(old, total)
    joined = peak + jnp.log(jnp.exp(old - peak) + jnp.exp(total - peak))
    kept, added = jnp.exp(old - joined), jnp.exp(total - joined)
    return mixed(joined, kept * delta_of(stat) + added * delta), kept, added


def pack(stat):
    flat = stat.T[:8]
    high = flat.astype(BF16).astype(F32)
    middle = (flat - high).astype(BF16).astype(F32)
    low = flat - high - middle
    return join([high, middle, low, jnp.zeros_like(low)]).astype(BF16)


def unpack(rows):
    terms = rows.astype(F32)
    flat = terms[:8] + terms[8:16] + terms[16:24]
    return join([flat] * 16).T


def score_parts(q, k, v, do, stat):
    chance = jnp.exp(nt(q, k) * SCALE - total_of(stat))
    score = (chance * (nt(do, v) - delta_of(stat)) * SCALE).astype(BF16)
    return chance.astype(BF16), score


def chosen(offs, head):
    return (
        (0, pl.ds(offs[5, head], 8, stride=32)),
        (8, pl.ds(offs[5, head] ^ 16, 8, stride=32)),
        (16, pl.ds(offs[4, head] ^ 8, 16, stride=16)),
        (32, pl.ds(offs[3, head] ^ 4, 32, stride=8)),
        (64, pl.ds(offs[2, head] ^ 2, 64, stride=4)),
    )


def load_chosen(ref, offs, head):
    return join([ref[rows, :] for _, rows in chosen(offs, head)])


def lanes(head):
    return pl.ds(pl.multiple_of(head * WIDTH, WIDTH), WIDTH)


def split_kernel(place, q, k, v, do, theirs):
    for y in range(CHIPS):
        for t, ref in enumerate((q, k, v, do)):
            theirs[y, t] = ref[:, lanes(2 * y + 1 - place[0])]


def chip_rows(place, step, raw, theirs):
    y = place[1] ^ step
    head = 2 * y + place[0]
    return head, [join([ref[:, lanes(head)], theirs[y, t]]) for t, ref in enumerate(raw)]


def chip_kernel(offs, place, q, k, v, do, theirs, m0, m1, m2, m3, outs, stats, work):
    for step, message in enumerate((m0, m1, m2, m3)):
        head, tensors = chip_rows(place, step, (q, k, v, do), theirs)
        out, total = attend(*tensors[:3])
        stat = mixed(total, dotted(tensors[3], out))
        outs[step] = out
        stats[step] = stat
        for t, rows in enumerate(tensors):
            work[t] = rows.astype(F32)
            message[t * ROWS : (t + 1) * ROWS] = load_chosen(work.at[t], offs, head).astype(BF16)
        work[4] = stat
        message[BODY:] = pack(load_chosen(work.at[4], offs, head))


def tensor(ref, t, rows=ROWS):
    return ref[t * ROWS : t * ROWS + rows]


def group(parts):
    return join(
        [p[:8] for p in parts] + [p[8:16] for p in parts] + [p[16:32] for p in parts]
    )


def ungroup(rows, chip):
    return join(
        [
            rows[8 * chip : 8 * chip + 8],
            rows[32 + 8 * chip : 40 + 8 * chip],
            rows[64 + 16 * chip : 80 + 16 * chip],
        ]
    )


def near_kernel(m0, m1, m2, m3, outs, stats, g):
    refs = (m0, m1, m2, m3)
    stat = [unpack(ref[BODY:]) for ref in refs]
    out = [None] * 4
    for pair in (0, 2):
        q, k, v, do = (join([tensor(refs[pair], t), tensor(refs[pair + 1], t)]) for t in range(4))
        more, total = attend(q, k, v)
        joined, _, added = combine(join(stat[pair : pair + 2]), total, dotted(do, more))
        more = more * added
        for chip in range(2):
            out[pair + chip] = more[chip * ROWS : (chip + 1) * ROWS]
            stat[pair + chip] = joined[chip * ROWS : (chip + 1) * ROWS]
    q, k, v, do = (join([tensor(ref, t, 64) for ref in refs]) for t in range(4))
    more, total = attend(q, k, v)
    joined, kept, added = combine(join([s[:64] for s in stat]), total, dotted(do, more))
    more = join([o[:64] for o in out]) * kept + more * added
    for chip in range(4):
        out[chip] = join([more[chip * 64 : (chip + 1) * 64], out[chip][64:]])
        stat[chip] = join([joined[chip * 64 : (chip + 1) * 64], stat[chip][64:]])
        outs[chip] = out[chip]
        stats[chip] = stat[chip]
    for t in range(4):
        rows = group([tensor(ref, t, 32).astype(F32) for ref in refs])
        g[t * ROWS : (t + 1) * ROWS] = rows.astype(BF16)
    g[BODY:] = pack(group(stat))


def far_kernel(g, a1, a2, a3, out_far, stats, message):
    refs = (g, a1, a2, a3)
    stat = [unpack(ref[BODY:]) for ref in refs]
    out = None
    for pair in (0, 2):
        q, k, v, do = (join([tensor(refs[pair], t), tensor(refs[pair + 1], t)]) for t in range(4))
        more, total = attend(q, k, v)
        joined, _, added = combine(join(stat[pair : pair + 2]), total, dotted(do, more))
        stat[pair], stat[pair + 1] = joined[:ROWS], joined[ROWS:]
        if pair == 0:
            out = (more * added)[:ROWS]
    q, k, v, do = (join([tensor(ref, t, 64) for ref in refs]) for t in range(4))
    more, total = attend(q, k, v)
    joined, kept, added = combine(join([s[:64] for s in stat]), total, dotted(do, more))
    out_far[...] = join([out[:64] * kept[:64] + more[:64] * added[:64], out[64:]])
    for z in range(4):
        stat[z] = join([joined[z * 64 : (z + 1) * 64], stat[z][64:]])
        stats[z] = stat[z]
    message[...] = join([s[:32] for s in stat]).T[:8]


def rest_kernel(
    m0, m1, m2, m3, outs, stats, g, a1, a2, a3, out_far, stats_far, far5, message5, c0, c1, c2, c3
):
    refs, fars = (m0, m1, m2, m3), (g, a1, a2, a3)
    own = [tensor(g, t) for t in range(4)]
    three = [join([tensor(g, t), tensor(a1, t)]) for t in range(4)]
    four = [join([tensor(ref, t, 64) for ref in fars]) for t in range(4)]
    five = [
        join([tensor(ref, t, 32) for ref in fars] + [far5[z, t] for z in range(4)])
        for t in range(4)
    ]
    far = [stats_far[z] for z in range(4)]
    more, total = attend(*five[:3])
    old = join([s[:32] for s in far] + [join([message5[...]] * 16).T])
    stat5, kept, added = combine(old, total, dotted(five[3], more))
    stat4 = join([join([stat5[32 * z : 32 * z + 32], far[z][32:64]]) for z in range(4)])
    stat3 = join([join([stat5[32 * z : 32 * z + 32], far[z][32:]]) for z in range(2)])
    own_stat = stat3[:ROWS]
    out = join([out_far[:32] * kept[:32] + more[:32] * added[:32], out_far[32:]])
    near = group([stats[chip] for chip in range(4)])
    out = out + group([outs[chip] for chip in range(4)]) * jnp.exp(
        total_of(near) - total_of(own_stat)
    )
    dq = dk = dv = None
    for level, (rows, gathered, stat) in enumerate(
        ((128, three, stat3), (64, four, stat4), (32, five, stat5))
    ):
        _, score = score_parts(
            own[0][:rows], gathered[1], gathered[2], own[3][:rows], own_stat[:rows]
        )
        queries = nn(score, gathered[1])
        chance, score = score_parts(
            gathered[0], own[1][:rows], own[2][:rows], gathered[3], stat
        )
        keys, values = tn(score, gathered[0]), tn(chance, gathered[3])
        if level == 0:
            dq, dk, dv = queries, keys, values
        else:
            dq, dk, dv = (
                join([whole[:rows] + part, whole[rows:]])
                for whole, part in ((dq, queries), (dk, keys), (dv, values))
            )
    stat = [join([ungroup(own_stat, chip), stats[chip, 32:]]) for chip in range(4)]
    sums = [None] * 4
    for pair in (0, 2):
        q, k, v, do = (join([tensor(refs[pair], t), tensor(refs[pair + 1], t)]) for t in range(4))
        chance, score = score_parts(q, k, v, do, join(stat[pair : pair + 2]))
        parts = nn(score, k), tn(score, q), tn(chance, do)
        for chip in range(2):
            sums[pair + chip] = [part[chip * ROWS : (chip + 1) * ROWS] for part in parts]
    q, k, v, do = (join([tensor(ref, t, 64) for ref in refs]) for t in range(4))
    chance, score = score_parts(q, k, v, do, join([s[:64] for s in stat]))
    parts = nn(score, k), tn(score, q), tn(chance, do)
    for chip, message in enumerate((c0, c1, c2, c3)):
        message[:ROWS] = join([ungroup(out, chip), outs[chip, 32:]]).astype(BF16)
        for t, (whole, part, top) in enumerate(zip(sums[chip], parts, (dq, dk, dv))):
            part = part[chip * 64 : (chip + 1) * 64]
            rows = join(
                [whole[:32] + part[:32] + ungroup(top, chip), whole[32:64] + part[32:], whole[64:]]
            )
            message[(t + 1) * ROWS : (t + 2) * ROWS] = rows.astype(BF16)
        message[BODY:] = pack(stat[chip])


def finish_kernel(
    offs, place, q, k, v, do, theirs, outs, stats, c0, c1, c2, c3, mine_out, theirs_out, work
):
    for step, message in enumerate((c0, c1, c2, c3)):
        head, tensors = chip_rows(place, step, (q, k, v, do), theirs)
        places = chosen(offs, head)
        work[4] = stats[step]
        final = unpack(message[BODY:])
        for begin, rows in places:
            work[4, rows, :] = final[begin : begin + rows.size]
        stat = work[4]
        work[0] = outs[step] * jnp.exp(total_of(stats[step]) - total_of(stat))
        chance, score = score_parts(*tensors, stat)
        work[1] = nn(score, tensors[1])
        work[2] = tn(score, tensors[0])
        work[3] = tn(chance, tensors[3])
        for t in range(4):
            part = tensor(message, t).astype(F32)
            for begin, rows in places:
                work[t, rows, :] = work[t, rows, :] + part[begin : begin + rows.size]
            mine_out[step, t] = work[t, :ROWS].astype(BF16)
            theirs_out[step, t] = work[t, ROWS:].astype(BF16)


def place_kernel(place, mine, theirs, att, dq, dk, dv):
    for step in range(CHIPS):
        head = 2 * (place[1] ^ step)
        for t, ref in enumerate((att, dq, dk, dv)):
            ref[:, lanes(head + place[0])] = mine[step, t]
            ref[:, lanes(head + 1 - place[0])] = theirs[step, t]


def call(kernel, name, scalars, outs, scratch, *args):
    smem = pl.BlockSpec(memory_space=pltpu.SMEM)
    vmem = pl.BlockSpec(memory_space=pltpu.VMEM)
    return pl.pallas_call(
        kernel,
        name=name,
        out_shape=tuple(jax.ShapeDtypeStruct(shape, dtype) for shape, dtype in outs),
        in_specs=[smem] * scalars + [vmem] * (len(args) - scalars),
        out_specs=(vmem,) * len(outs),
        scratch_shapes=[pltpu.VMEM(shape, F32) for shape in scratch],
        compiler_params=pltpu.CompilerParams(vmem_limit_bytes=40 * 2**20),
    )(*args)


def in_plane(array, flip):
    moves = [(PLANE * z + i, PLANE * z + (i ^ flip)) for z in range(DEPTH) for i in range(PLANE)]
    return lax.ppermute(array, "ctx", moves)


def across(array, flip):
    moves = [(PLANE * z + i, PLANE * (z ^ flip) + i) for z in range(DEPTH) for i in range(PLANE)]
    return lax.ppermute(array, "ctx", moves)


def shards(queries, keys, values, out_grad, offsets):
    spot = lax.axis_index("ctx") % PLANE
    place = jnp.stack([spot % 2, spot // 2])
    raw = (queries, keys, values, out_grad)
    half = ((CHIPS, 4, ROWS, WIDTH), BF16)
    message = ((MESSAGE, WIDTH), BF16)
    quads = ((4, ROWS, WIDTH), F32)
    chips = ((4, CHIP, WIDTH), F32)
    (theirs,) = call(split_kernel, "split", 1, [half], [], place, *raw)
    theirs = in_plane(theirs, 1)
    *sent, outs0, stats0 = call(
        chip_kernel, "chip", 2, [message] * 4 + [chips] * 2, [(5, CHIP, WIDTH)],
        offsets, place, *raw, theirs,
    )
    got = [sent[0]] + [in_plane(sent[step], 2 * step) for step in (1, 2, 3)]
    outs, stats, g = call(near_kernel, "near", 0, [quads, quads, message], [], *got)
    fars = [g] + [across(g, flip) for flip in (1, 2, 3)]
    top = jnp.stack([far[:BODY].reshape(4, ROWS, WIDTH)[:, :32] for far in fars])
    top = across(top, 7)
    out_far, stats_far, message5 = call(
        far_kernel, "far", 0, [((ROWS, WIDTH), F32), quads, ((8, WIDTH), F32)], [], *fars
    )
    message5 = across(message5, 7)
    back = call(
        rest_kernel, "rest", 0, [message] * 4, [],
        *got, outs, stats, *fars, out_far, stats_far, top, message5,
    )
    back = [back[0]] + [in_plane(back[step], 2 * step) for step in (1, 2, 3)]
    mine, theirs_out = call(
        finish_kernel, "finish", 2, [half, half], [(5, CHIP, WIDTH)],
        offsets, place, *raw, theirs, outs0, stats0, *back,
    )
    theirs_out = in_plane(theirs_out, 1)
    row = ((ROWS, HEADS * WIDTH), BF16)
    return call(place_kernel, "place", 1, [row] * 4, [], place, mine, theirs_out)


def solution(mesh):
    rows = P(("dp", "ctx"), None)
    return jax.shard_map(
        shards,
        mesh=mesh,
        in_specs=(rows,) * 4 + (P("dp", None),),
        out_specs=(rows,) * 4,
        check_vma=False,
    )
```

time: 92.6 us -> 74.6 us (0.81)
  blocking collectives: 24.2 us -> 0 us
  Pallas kernels: 9.76 us -> 16.2 us
  starting transfers between devices: 21.8 us -> 26.1 us
  local copies, waits for them, and re-layouts: 9.22 us -> 5.42 us
  other arithmetic: 1.28 us -> 0.1 us
    all_to_all x1 -> x0, blocking collectives: 24.2 us -> none  [shards(): lax.all_to_all(jnp.stack([att, dq, dk, dv], axis=1), 'ctx', 0, 0, axis_in...]
    ppermute x0 -> x8, starting transfers between devices: none -> 16 us  [in_plane(): return lax.ppermute(array, 'ctx', moves)]
    all_to_all x1 -> x0, waiting for transfers between devices: 14.9 us -> none  [shards(): lax.all_to_all(stacked, 'ctx', 0, 0, axis_index_groups=planes(), tiled=True)]
    ppermute x0 -> x8, waiting for transfers between devices: none -> 13.6 us  [in_plane(): return lax.ppermute(array, 'ctx', moves)]
    all_to_all x1 -> x0, starting transfers between devices: 6.7 us -> none  [shards(): lax.all_to_all(stacked, 'ctx', 0, 0, axis_index_groups=planes(), tiled=True)]
    pallas_call x5 -> x7, Pallas kernels: 9.76 us -> 16.2 us  [call(): pl.pallas_call(kernel, name=name, out_shape=tuple((jax.ShapeDtypeStruct(s...]
    ppermute x6 -> x5, starting transfers between devices: 15.1 us -> 10.1 us  [across(): return lax.ppermute(array, 'ctx', moves)]
    unnamed x20 -> x22, local copies, waits for them, and re-layouts: 8.09 us -> 4.48 us
  transfers between devices with their start and end apart: 7 -> 13, of which waited for: 6 -> 10; matrix products, arithmetic and copies ran while one was open for 0% -> 0% of each run, Pallas kernels for 6% -> 3%
where the time goes in v1:
time: 74.6 us; the launch traced here: 74.4 us
  starting transfers between devices  26.1 us (35%)
  waiting for transfers between devices  25.8 us (35%)
  Pallas kernels  16.2 us (22%)
  local copies, waits for them, and re-layouts  5.42 us (7%)
  between operations  0.8 us (1%)
    pallas_call x7, Pallas kernels, call(): pl.pallas_call(kernel, name=name, out_shape=tuple((jax.ShapeDtypeStruct(s...  16.2 us
    ppermute x8, starting transfers between devices, in_plane(): return lax.ppermute(array, 'ctx', moves)  16 us
    ppermute x8, waiting for transfers between devices, in_plane(): return lax.ppermute(array, 'ctx', moves)  13.6 us
    ppermute x5, waiting for transfers between devices, across(): return lax.ppermute(array, 'ctx', moves)  12.2 us
    ppermute x5, starting transfers between devices, across(): return lax.ppermute(array, 'ctx', moves)  10.1 us
    unnamed x22, local copies, waits for them, and re-layouts  4.48 us
  transfers between devices with their start and end apart: 13, of which 10 were waited for; matrix products, arithmetic and copies ran while one was open for 0% of the time, Pallas kernels for 3%

profile of v1, /device:TPU:1, one launch (start us, length us, event | category | flops | bytes accessed | tf_op | source)
XLA Modules:
  0.0 74.4 jit_solution(4875876366872556809)
XLA Ops:
  0.7 0.1 pad_add_fusion.place
  0.7 0.0 copy-start
  0.7 0.9 %copy-done = bf16[128,1024]{1,0:T(8,128)(2,1)S(1)} copy-done((bf16[128,1024]{1,0:T(8,128)(2,1)S(1)}, bf16[128,1024]{1,0:T(8,128)(2,1)}, u32[]{:S(2)}) %copy-start) | copy-done | bytes 262168
  1.7 0.0 copy-start.2
  1.7 0.9 %copy-done.2 = bf16[128,1024]{1,0:T(8,128)(2,1)S(1)} copy-done((bf16[128,1024]{1,0:T(8,128)(2,1)S(1)}, bf16[128,1024]{1,0:T(8,128)(2,1)}, u32[]{:S(2)}) %copy-start.2) | copy-done | bytes 262168
  2.6 0.0 copy-start.4
  2.6 0.9 %copy-done.4 = bf16[128,1024]{1,0:T(8,128)(2,1)S(1)} copy-done((bf16[128,1024]{1,0:T(8,128)(2,1)S(1)}, bf16[128,1024]{1,0:T(8,128)(2,1)}, u32[]{:S(2)}) %copy-start.4) | copy-done | bytes 262168
  3.6 0.0 copy-start.6
  3.6 0.9 %copy-done.6 = bf16[128,1024]{1,0:T(8,128)(2,1)S(1)} copy-done((bf16[128,1024]{1,0:T(8,128)(2,1)S(1)}, bf16[128,1024]{1,0:T(8,128)(2,1)}, u32[]{:S(2)}) %copy-start.6) | copy-done | bytes 262168
  4.5 0.0 copy-start.10
  4.5 0.7 split.1
  5.2 3.3 %collective-permute-start = (bf16[4,4,128,128]{3,2,1,0:T(8,128)(2,1)S(1)}, bf16[4,4,128,128]{3,2,1,0:T(8,128)(2,1)S(1)}, u32[]{:S(2)}, u32[]{:S(2)}) collective-permute-start(bf16[4,4,128,128]{3,2,1,0:T(8,128)(2,1)S(1)} %split.1), channel_id=1, source_target_pairs={{0,1},{1,0},{2,3},{3,2},{4,5},{5,4},{6,7},{7,6},{8,9},{9,8},{10,11... | collective-permute-start | bytes 1572872 | tf_op jit(solution)/shard_map/ppermute | solution.py:320
  8.6 1.5 %collective-permute-done.theirs = bf16[4,4,128,128]{3,2,1,0:T(8,128)(2,1)S(1)} collective-permute-done((bf16[4,4,128,128]{3,2,1,0:T(8,128)(2,1)S(1)}, bf16[4,4,128,128]{3,2,1,0:T(8,128)(2,1)S(1)}, u32[]{:S(2)}, u32[]{:S(2)}) %collective-permute-start) | collective-permute-done | bytes 524320 | tf_op jit(solution)/shard_map/ppermute | solution.py:320
  10.1 0.0 copy-done.10
  10.1 2.3 %chip.1 = (bf16[544,128]{1,0:T(8,128)(2,1)S(1)}, bf16[544,128]{1,0:T(8,128)(2,1)S(1)}, bf16[544,128]{1,0:T(8,128)(2,1)S(1)}, bf16[544,128]{1,0:T(8,128)(2,1)S(1)...) custom-call(s32[6,8]{1,0:T(8,128)S(1)} %copy-done.10, s32[2]{0:T(128)S(1)} %pad_add_fusion.place, ...), custom_call_target="tpu_custom_call" | custom-call | tf_op jit(solution)/shard_map/chip/pallas_call | solution.py:307
  12.4 0.1 collective-permute-start.1
  12.5 2.2 %collective-permute-start.2 = (bf16[544,128]{1,0:T(8,128)(2,1)S(1)}, bf16[544,128]{1,0:T(8,128)(2,1)S(1)}, u32[]{:S(2)}, u32[]{:S(2)}) collective-permute-start(bf16[544,128]{1,0:T(8,128)(2,1)S(1)} %get-tuple-element.26), channel_id=1, source_target_pairs={{0,4},{1,5},{2,6},{3,7},{4,0},{5,1},{6,2},{7,3},{8,12},{9,13},{10,... | collective-permute-start | bytes 417800 | tf_op jit(solution)/shard_map/ppermute | solution.py:320
  14.6 1.7 %collective-permute-start.3 = (bf16[544,128]{1,0:T(8,128)(2,1)S(1)}, bf16[544,128]{1,0:T(8,128)(2,1)S(1)}, u32[]{:S(2)}, u32[]{:S(2)}) collective-permute-start(bf16[544,128]{1,0:T(8,128)(2,1)S(1)} %get-tuple-element.27), channel_id=1, source_target_pairs={{0,6},{1,7},{2,4},{3,5},{4,2},{5,3},{6,0},{7,1},{8,14},{9,15},{10,... | collective-permute-start | bytes 417800 | tf_op jit(solution)/shard_map/ppermute | solution.py:320
  16.3 1.0 %collective-permute-done.1.m1 = bf16[544,128]{1,0:T(8,128)(2,1)S(1)} collective-permute-done((bf16[544,128]{1,0:T(8,128)(2,1)S(1)}, bf16[544,128]{1,0:T(8,128)(2,1)S(1)}, u32[]{:S(2)}, u32[]{:S(2)}) %collective-permute-start.1) | collective-permute-done | bytes 139296 | tf_op jit(solution)/shard_map/ppermute | solution.py:320
  17.3 3.7 %collective-permute-done.2.m2 = bf16[544,128]{1,0:T(8,128)(2,1)S(1)} collective-permute-done((bf16[544,128]{1,0:T(8,128)(2,1)S(1)}, bf16[544,128]{1,0:T(8,128)(2,1)S(1)}, u32[]{:S(2)}, u32[]{:S(2)}) %collective-permute-start.2) | collective-permute-done | bytes 139296 | tf_op jit(solution)/shard_map/ppermute | solution.py:320
  21.1 2.5 %collective-permute-done.3.m3 = bf16[544,128]{1,0:T(8,128)(2,1)S(1)} collective-permute-done((bf16[544,128]{1,0:T(8,128)(2,1)S(1)}, bf16[544,128]{1,0:T(8,128)(2,1)S(1)}, u32[]{:S(2)}, u32[]{:S(2)}) %collective-permute-start.3) | collective-permute-done | bytes 139296 | tf_op jit(solution)/shard_map/ppermute | solution.py:320
  23.6 2.6 %near.1 = (f32[4,128,128]{2,1,0:T(8,128)S(1)}, f32[4,128,128]{2,1,0:T(8,128)S(1)}, bf16[544,128]{1,0:T(8,128)(2,1)S(1)}) custom-call(bf16[544,128]{1,0:T(8,128)(2,1)S(1)} %get-tuple-element.24.m0, bf16[544,128]{1,0:T(8,128)(2,1)S(1)} %collective-permute-done.1.m1, bf16[544,128]{1,0:T(8,128)(2,1)S(1)} %collective-permute-done.2.m2, ...), custom_call_target="tpu_custom_call" | custom-call | tf_op jit(solution)/shard_map/near/pallas_call | solution.py:307
  26.1 4.4 %collective-permute-start.6 = (bf16[544,128]{1,0:T(8,128)(2,1)S(1)}, bf16[544,128]{1,0:T(8,128)(2,1)S(1)}, u32[]{:S(2)}, u32[]{:S(2)}) collective-permute-start(bf16[544,128]{1,0:T(8,128)(2,1)S(1)} %get-tuple-element.30.g), channel_id=1, source_target_pairs={{0,24},{1,25},{2,26},{3,27},{4,28},{5,29},{6,30},{7,31},{8,16},{9,... | collective-permute-start | bytes 417800 | tf_op jit(solution)/shard_map/ppermute | solution.py:325
  30.5 0.0 collective-permute-start.5
  30.5 0.5 collective-permute-start.4
  31.0 2.5 %collective-permute-done.6.a3 = bf16[544,128]{1,0:T(8,128)(2,1)S(1)} collective-permute-done((bf16[544,128]{1,0:T(8,128)(2,1)S(1)}, bf16[544,128]{1,0:T(8,128)(2,1)S(1)}, u32[]{:S(2)}, u32[]{:S(2)}) %collective-permute-start.6) | collective-permute-done | bytes 139296 | tf_op jit(solution)/shard_map/ppermute | solution.py:325
  33.5 0.0 copy-start.8
  33.5 0.7 copy-done.8
  34.2 6.7 %collective-permute-done.5.a2 = bf16[544,128]{1,0:T(8,128)(2,1)S(1)} collective-permute-done((bf16[544,128]{1,0:T(8,128)(2,1)S(1)}, bf16[544,128]{1,0:T(8,128)(2,1)S(1)}, u32[]{:S(2)}, u32[]{:S(2)}) %collective-permute-start.5) | collective-permute-done | bytes 139296 | tf_op jit(solution)/shard_map/ppermute | solution.py:325
  40.9 0.0 slice-start
  40.9 0.9 %slice-done = bf16[512,128]{1,0:T(8,128)(2,1)S(1)} async-done(((bf16[544,128]{1,0:T(8,128)(2,1)}), bf16[512,128]{1,0:T(8,128)(2,1)S(1)}, s32[]{:S(2)}) %slice-start) | async-done | bytes 131096 | tf_op jit(solution)/shard_map/slice | solution.py:345
  41.8 0.0 collective-permute-done.4.a1
  41.9 0.0 copy-start.9
  41.9 4.2 %collective-permute-start.7 = (bf16[4,4,32,128]{3,2,1,0:T(8,128)(2,1)S(1)}, bf16[4,4,32,128]{3,2,1,0:T(8,128)(2,1)S(1)}, u32[]{:S(2)}, u32[]{:S(2)}) collective-permute-start(bf16[4,4,32,128]{3,2,1,0:T(8,128)(2,1)S(1)} %pad_maximum_fusion), channel_id=1, source_target_pairs={{0,56},{1,57},{2,58},{3,59},{4,60},{5,61},{6,62},{7,63},{8,48},{9,... | collective-permute-start | bytes 393224 | tf_op jit(solution)/shard_map/ppermute | solution.py:325
  46.1 0.0 copy-done.9
  46.1 2.4 %far.1 = (f32[128,128]{1,0:T(8,128)S(1)}, f32[4,128,128]{2,1,0:T(8,128)S(1)}, f32[8,128]{1,0:T(8,128)S(1)}) custom-call(bf16[544,128]{1,0:T(8,128)(2,1)S(1)} %get-tuple-element.30.g, bf16[544,128]{1,0:T(8,128)(2,1)S(1)} %collective-permute-done.4.a1, bf16[544,128]{1,0:T(8,128)(2,1)S(1)} %collective-permute-done.5.a2, bf16[544,128]{1,0:T(8,128)(2,1)S(1)} %copy-done.9), custom_call_target="tpu_custom_call" | custom-call | tf_op jit(solution)/shard_map/far/pallas_call | solution.py:307
  48.5 1.0 %collective-permute-start.8 = (f32[8,128]{1,0:T(8,128)S(1)}, f32[8,128]{1,0:T(8,128)S(1)}, u32[]{:S(2)}, u32[]{:S(2)}) collective-permute-start(f32[8,128]{1,0:T(8,128)S(1)} %get-tuple-element.33), channel_id=1, source_target_pairs={{0,56},{1,57},{2,58},{3,59},{4,60},{5,61},{6,62},{7,63},{8,48},{9,... | collective-permute-start | bytes 12296 | tf_op jit(solution)/shard_map/ppermute | solution.py:325
  49.5 2.9 %collective-permute-done.8.message5 = f32[8,128]{1,0:T(8,128)S(1)} collective-permute-done((f32[8,128]{1,0:T(8,128)S(1)}, f32[8,128]{1,0:T(8,128)S(1)}, u32[]{:S(2)}, u32[]{:S(2)}) %collective-permute-start.8) | collective-permute-done | bytes 4128 | tf_op jit(solution)/shard_map/ppermute | solution.py:325
  52.4 0.0 collective-permute-done.7.far5
  52.4 0.0 copy-start.1
  52.4 0.0 copy-start.3
  52.4 0.0 copy-start.5
  52.4 0.0 copy-start.7
  52.5 3.0 %rest.1 = (bf16[544,128]{1,0:T(8,128)(2,1)S(1)}, bf16[544,128]{1,0:T(8,128)(2,1)S(1)}, bf16[544,128]{1,0:T(8,128)(2,1)S(1)}, bf16[544,128]{1,0:T(8,128)(2,1)S(1)}) custom-call(bf16[544,128]{1,0:T(8,128)(2,1)S(1)} %get-tuple-element.24.m0, bf16[544,128]{1,0:T(8,128)(2,1)S(1)} %collective-permute-done.1.m1, bf16[544,128]{1,0:T(8,128)(2,1)S(1)} %collective-permute-done.2.m2, ...), custom_call_target="tpu_custom_call" | custom-call | tf_op jit(solution)/shard_map/rest/pallas_call | solution.py:307
  55.5 0.1 collective-permute-start.9
  55.6 1.7 %collective-permute-start.10 = (bf16[544,128]{1,0:T(8,128)(2,1)S(1)}, bf16[544,128]{1,0:T(8,128)(2,1)S(1)}, u32[]{:S(2)}, u32[]{:S(2)}) collective-permute-start(bf16[544,128]{1,0:T(8,128)(2,1)S(1)} %get-tuple-element.36), channel_id=1, source_target_pairs={{0,4},{1,5},{2,6},{3,7},{4,0},{5,1},{6,2},{7,3},{8,12},{9,13},{10,... | collective-permute-start | bytes 417800 | tf_op jit(solution)/shard_map/ppermute | solution.py:320
  57.3 2.1 %collective-permute-start.11 = (bf16[544,128]{1,0:T(8,128)(2,1)S(1)}, bf16[544,128]{1,0:T(8,128)(2,1)S(1)}, u32[]{:S(2)}, u32[]{:S(2)}) collective-permute-start(bf16[544,128]{1,0:T(8,128)(2,1)S(1)} %get-tuple-element.37), channel_id=1, source_target_pairs={{0,6},{1,7},{2,4},{3,5},{4,2},{5,3},{6,0},{7,1},{8,14},{9,15},{10,... | collective-permute-start | bytes 417800 | tf_op jit(solution)/shard_map/ppermute | solution.py:320
  59.4 0.0 collective-permute-done.9.c1
  59.5 1.8 %collective-permute-done.10.c2 = bf16[544,128]{1,0:T(8,128)(2,1)S(1)} collective-permute-done((bf16[544,128]{1,0:T(8,128)(2,1)S(1)}, bf16[544,128]{1,0:T(8,128)(2,1)S(1)}, u32[]{:S(2)}, u32[]{:S(2)}) %collective-permute-start.10) | collective-permute-done | bytes 139296 | tf_op jit(solution)/shard_map/ppermute | solution.py:320
  61.3 1.5 %collective-permute-done.11.c3 = bf16[544,128]{1,0:T(8,128)(2,1)S(1)} collective-permute-done((bf16[544,128]{1,0:T(8,128)(2,1)S(1)}, bf16[544,128]{1,0:T(8,128)(2,1)S(1)}, u32[]{:S(2)}, u32[]{:S(2)}) %collective-permute-start.11) | collective-permute-done | bytes 139296 | tf_op jit(solution)/shard_map/ppermute | solution.py:320
  62.7 0.0 copy-done.1
  62.7 0.0 copy-done.3
  62.7 0.0 copy-done.5
  62.8 0.0 copy-done.7
  62.8 3.5 %finish.1 = (bf16[4,4,128,128]{3,2,1,0:T(8,128)(2,1)S(1)}, bf16[4,4,128,128]{3,2,1,0:T(8,128)(2,1)S(1)}) custom-call(s32[6,8]{1,0:T(8,128)S(1)} %copy-done.10, s32[2]{0:T(128)S(1)} %pad_add_fusion.place, bf16[128,1024]{1,0:T(8,128)(2,1)S(1)} %copy-done.1, bf16[128,1024]{1,0:T(8,128)(2,1)S(1)} %copy-done.3, bf16[128,1024]{1,0:T(8,128)(2,1)S(1)} %copy-done.5, ...), custom_call_target="tpu_custom_call" | custom-call | tf_op jit(solution)/shard_map/finish/pallas_call | solution.py:307
  66.3 4.8 %collective-permute-start.12 = (bf16[4,4,128,128]{3,2,1,0:T(8,128)(2,1)S(1)}, bf16[4,4,128,128]{3,2,1,0:T(8,128)(2,1)S(1)}, u32[]{:S(2)}, u32[]{:S(2)}) collective-permute-start(bf16[4,4,128,128]{3,2,1,0:T(8,128)(2,1)S(1)} %get-tuple-element.39), channel_id=1, source_target_pairs={{0,1},{1,0},{2,3},{3,2},{4,5},{5,4},{6,7},{7,6},{8,9},{9,8},{10,11... | collective-permute-start | bytes 1572872 | tf_op jit(solution)/shard_map/ppermute | solution.py:320
  71.1 1.5 %collective-permute-done.12.theirs = bf16[4,4,128,128]{3,2,1,0:T(8,128)(2,1)S(1)} collective-permute-done((bf16[4,4,128,128]{3,2,1,0:T(8,128)(2,1)S(1)}, bf16[4,4,128,128]{3,2,1,0:T(8,128)(2,1)S(1)}, u32[]{:S(2)}, u32[]{:S(2)}) %collective-permute-start.12) | collective-permute-done | bytes 524320 | tf_op jit(solution)/shard_map/ppermute | solution.py:320
  72.6 1.8 %place.1 = (bf16[128,1024]{1,0:T(8,128)(2,1)}, bf16[128,1024]{1,0:T(8,128)(2,1)}, bf16[128,1024]{1,0:T(8,128)(2,1)}, bf16[128,1024]{1,0:T(8,128)(2,1)}) custom-call(s32[2]{0:T(128)S(1)} %pad_add_fusion.place, bf16[4,4,128,128]{3,2,1,0:T(8,128)(2,1)S(1)} %get-tuple-element.38.mine, bf16[4,4,128,128]{3,2,1,0:T(8,128)(2,1)S(1)} %collective-permute-done.12.theirs), custom_call_target="tpu_custom_call" | custom-call | tf_op jit(solution)/shard_map/place/pallas_call | solution.py:307
  (6 shorter events, 0.1 us)
Async XLA Ops:
  0.7 1.0 %copy-start = (bf16[128,1024]{1,0:T(8,128)(2,1)S(1)}, bf16[128,1024]{1,0:T(8,128)(2,1)}, u32[]{:S(2)}) copy-start(bf16[128,1024]{1,0:T(8,128)(2,1)} %q.5) | copy-start | bytes 786436
  1.7 0.9 %copy-start.2 = (bf16[128,1024]{1,0:T(8,128)(2,1)S(1)}, bf16[128,1024]{1,0:T(8,128)(2,1)}, u32[]{:S(2)}) copy-start(bf16[128,1024]{1,0:T(8,128)(2,1)} %k.5) | copy-start | bytes 786436
  2.6 0.9 %copy-start.4 = (bf16[128,1024]{1,0:T(8,128)(2,1)S(1)}, bf16[128,1024]{1,0:T(8,128)(2,1)}, u32[]{:S(2)}) copy-start(bf16[128,1024]{1,0:T(8,128)(2,1)} %v.5) | copy-start | bytes 786436
  3.6 0.9 %copy-start.6 = (bf16[128,1024]{1,0:T(8,128)(2,1)S(1)}, bf16[128,1024]{1,0:T(8,128)(2,1)}, u32[]{:S(2)}) copy-start(bf16[128,1024]{1,0:T(8,128)(2,1)} %do.5) | copy-start | bytes 786436
  4.5 5.6 %copy-start.10 = (s32[6,8]{1,0:T(8,128)S(1)}, s32[6,8]{1,0:T(8,128)}, u32[]{:S(2)}) copy-start(s32[6,8]{1,0:T(8,128)} %offs.3) | copy-start | bytes 580
  5.2 4.9 %collective-permute-start = (bf16[4,4,128,128]{3,2,1,0:T(8,128)(2,1)S(1)}, bf16[4,4,128,128]{3,2,1,0:T(8,128)(2,1)S(1)}, u32[]{:S(2)}, u32[]{:S(2)}) collective-permute-start(bf16[4,4,128,128]{3,2,1,0:T(8,128)(2,1)S(1)} %split.1), channel_id=1, source_target_pairs={{0,1},{1,0},{2,3},{3,2},{4,5},{5,4},{6,7},{7,6},{8,9},{9,8},{10,11... | collective-permute-start | bytes 1572872 | tf_op jit(solution)/shard_map/ppermute | solution.py:320
  12.4 4.9 %collective-permute-start.1 = (bf16[544,128]{1,0:T(8,128)(2,1)S(1)}, bf16[544,128]{1,0:T(8,128)(2,1)S(1)}, u32[]{:S(2)}, u32[]{:S(2)}) collective-permute-start(bf16[544,128]{1,0:T(8,128)(2,1)S(1)} %get-tuple-element.25), channel_id=1, source_target_pairs={{0,2},{1,3},{2,0},{3,1},{4,6},{5,7},{6,4},{7,5},{8,10},{9,11},{10,... | collective-permute-start | bytes 417800 | tf_op jit(solution)/shard_map/ppermute | solution.py:320
  12.5 8.6 %collective-permute-start.2 = (bf16[544,128]{1,0:T(8,128)(2,1)S(1)}, bf16[544,128]{1,0:T(8,128)(2,1)S(1)}, u32[]{:S(2)}, u32[]{:S(2)}) collective-permute-start(bf16[544,128]{1,0:T(8,128)(2,1)S(1)} %get-tuple-element.26), channel_id=1, source_target_pairs={{0,4},{1,5},{2,6},{3,7},{4,0},{5,1},{6,2},{7,3},{8,12},{9,13},{10,... | collective-permute-start | bytes 417800 | tf_op jit(solution)/shard_map/ppermute | solution.py:320
  14.6 8.9 %collective-permute-start.3 = (bf16[544,128]{1,0:T(8,128)(2,1)S(1)}, bf16[544,128]{1,0:T(8,128)(2,1)S(1)}, u32[]{:S(2)}, u32[]{:S(2)}) collective-permute-start(bf16[544,128]{1,0:T(8,128)(2,1)S(1)} %get-tuple-element.27), channel_id=1, source_target_pairs={{0,6},{1,7},{2,4},{3,5},{4,2},{5,3},{6,0},{7,1},{8,14},{9,15},{10,... | collective-permute-start | bytes 417800 | tf_op jit(solution)/shard_map/ppermute | solution.py:320
  26.1 7.4 %collective-permute-start.6 = (bf16[544,128]{1,0:T(8,128)(2,1)S(1)}, bf16[544,128]{1,0:T(8,128)(2,1)S(1)}, u32[]{:S(2)}, u32[]{:S(2)}) collective-permute-start(bf16[544,128]{1,0:T(8,128)(2,1)S(1)} %get-tuple-element.30.g), channel_id=1, source_target_pairs={{0,24},{1,25},{2,26},{3,27},{4,28},{5,29},{6,30},{7,31},{8,16},{9,... | collective-permute-start | bytes 417800 | tf_op jit(solution)/shard_map/ppermute | solution.py:325
  30.5 10.4 %collective-permute-start.5 = (bf16[544,128]{1,0:T(8,128)(2,1)S(1)}, bf16[544,128]{1,0:T(8,128)(2,1)S(1)}, u32[]{:S(2)}, u32[]{:S(2)}) collective-permute-start(bf16[544,128]{1,0:T(8,128)(2,1)S(1)} %get-tuple-element.30.g), channel_id=1, source_target_pairs={{0,16},{1,17},{2,18},{3,19},{4,20},{5,21},{6,22},{7,23},{8,24},{9,... | collective-permute-start | bytes 417800 | tf_op jit(solution)/shard_map/ppermute | solution.py:325
  30.5 11.3 %collective-permute-start.4 = (bf16[544,128]{1,0:T(8,128)(2,1)S(1)}, bf16[544,128]{1,0:T(8,128)(2,1)S(1)}, u32[]{:S(2)}, u32[]{:S(2)}) collective-permute-start(bf16[544,128]{1,0:T(8,128)(2,1)S(1)} %get-tuple-element.30.g), channel_id=1, source_target_pairs={{0,8},{1,9},{2,10},{3,11},{4,12},{5,13},{6,14},{7,15},{8,0},{9,1},... | collective-permute-start | bytes 417800 | tf_op jit(solution)/shard_map/ppermute | solution.py:325
  33.5 0.7 copy-start.8
  40.9 0.9 %slice-start = ((bf16[544,128]{1,0:T(8,128)(2,1)}), bf16[512,128]{1,0:T(8,128)(2,1)S(1)}, s32[]{:S(2)}) async-start(bf16[544,128]{1,0:T(8,128)(2,1)} %copy-done.8), calls=%async_computation | async-start | bytes 262144 | tf_op jit(solution)/shard_map/slice | solution.py:345
  41.9 4.2 %copy-start.9 = (bf16[544,128]{1,0:T(8,128)(2,1)S(1)}, bf16[544,128]{1,0:T(8,128)(2,1)}, u32[]{:S(2)}) copy-start(bf16[544,128]{1,0:T(8,128)(2,1)} %copy-done.8) | copy-start | bytes 417796
  41.9 10.5 %collective-permute-start.7 = (bf16[4,4,32,128]{3,2,1,0:T(8,128)(2,1)S(1)}, bf16[4,4,32,128]{3,2,1,0:T(8,128)(2,1)S(1)}, u32[]{:S(2)}, u32[]{:S(2)}) collective-permute-start(bf16[4,4,32,128]{3,2,1,0:T(8,128)(2,1)S(1)} %pad_maximum_fusion), channel_id=1, source_target_pairs={{0,56},{1,57},{2,58},{3,59},{4,60},{5,61},{6,62},{7,63},{8,48},{9,... | collective-permute-start | bytes 393224 | tf_op jit(solution)/shard_map/ppermute | solution.py:325
  48.5 3.9 %collective-permute-start.8 = (f32[8,128]{1,0:T(8,128)S(1)}, f32[8,128]{1,0:T(8,128)S(1)}, u32[]{:S(2)}, u32[]{:S(2)}) collective-permute-start(f32[8,128]{1,0:T(8,128)S(1)} %get-tuple-element.33), channel_id=1, source_target_pairs={{0,56},{1,57},{2,58},{3,59},{4,60},{5,61},{6,62},{7,63},{8,48},{9,... | collective-permute-start | bytes 12296 | tf_op jit(solution)/shard_map/ppermute | solution.py:325
  52.4 10.3 %copy-start.1 = (bf16[128,1024]{1,0:T(8,128)(2,1)S(1)}, bf16[128,1024]{1,0:T(8,128)(2,1)}, u32[]{:S(2)}) copy-start(bf16[128,1024]{1,0:T(8,128)(2,1)} %q.5) | copy-start | bytes 786436
  52.4 10.3 %copy-start.3 = (bf16[128,1024]{1,0:T(8,128)(2,1)S(1)}, bf16[128,1024]{1,0:T(8,128)(2,1)}, u32[]{:S(2)}) copy-start(bf16[128,1024]{1,0:T(8,128)(2,1)} %k.5) | copy-start | bytes 786436
  52.4 10.3 %copy-start.5 = (bf16[128,1024]{1,0:T(8,128)(2,1)S(1)}, bf16[128,1024]{1,0:T(8,128)(2,1)}, u32[]{:S(2)}) copy-start(bf16[128,1024]{1,0:T(8,128)(2,1)} %v.5) | copy-start | bytes 786436
  52.4 10.3 %copy-start.7 = (bf16[128,1024]{1,0:T(8,128)(2,1)S(1)}, bf16[128,1024]{1,0:T(8,128)(2,1)}, u32[]{:S(2)}) copy-start(bf16[128,1024]{1,0:T(8,128)(2,1)} %do.5) | copy-start | bytes 786436
  55.5 4.0 %collective-permute-start.9 = (bf16[544,128]{1,0:T(8,128)(2,1)S(1)}, bf16[544,128]{1,0:T(8,128)(2,1)S(1)}, u32[]{:S(2)}, u32[]{:S(2)}) collective-permute-start(bf16[544,128]{1,0:T(8,128)(2,1)S(1)} %get-tuple-element.35), channel_id=1, source_target_pairs={{0,2},{1,3},{2,0},{3,1},{4,6},{5,7},{6,4},{7,5},{8,10},{9,11},{10,... | collective-permute-start | bytes 417800 | tf_op jit(solution)/shard_map/ppermute | solution.py:320
  55.6 5.7 %collective-permute-start.10 = (bf16[544,128]{1,0:T(8,128)(2,1)S(1)}, bf16[544,128]{1,0:T(8,128)(2,1)S(1)}, u32[]{:S(2)}, u32[]{:S(2)}) collective-permute-start(bf16[544,128]{1,0:T(8,128)(2,1)S(1)} %get-tuple-element.36), channel_id=1, source_target_pairs={{0,4},{1,5},{2,6},{3,7},{4,0},{5,1},{6,2},{7,3},{8,12},{9,13},{10,... | collective-permute-start | bytes 417800 | tf_op jit(solution)/shard_map/ppermute | solution.py:320
  57.3 5.4 %collective-permute-start.11 = (bf16[544,128]{1,0:T(8,128)(2,1)S(1)}, bf16[544,128]{1,0:T(8,128)(2,1)S(1)}, u32[]{:S(2)}, u32[]{:S(2)}) collective-permute-start(bf16[544,128]{1,0:T(8,128)(2,1)S(1)} %get-tuple-element.37), channel_id=1, source_target_pairs={{0,6},{1,7},{2,4},{3,5},{4,2},{5,3},{6,0},{7,1},{8,14},{9,15},{10,... | collective-permute-start | bytes 417800 | tf_op jit(solution)/shard_map/ppermute | solution.py:320
  66.3 6.3 %collective-permute-start.12 = (bf16[4,4,128,128]{3,2,1,0:T(8,128)(2,1)S(1)}, bf16[4,4,128,128]{3,2,1,0:T(8,128)(2,1)S(1)}, u32[]{:S(2)}, u32[]{:S(2)}) collective-permute-start(bf16[4,4,128,128]{3,2,1,0:T(8,128)(2,1)S(1)} %get-tuple-element.39), channel_id=1, source_target_pairs={{0,1},{1,0},{2,3},{3,2},{4,5},{5,4},{6,7},{7,6},{8,9},{9,8},{10,11... | collective-permute-start | bytes 1572872 | tf_op jit(solution)/shard_map/ppermute | solution.py:320

commit v2 on v1

--- a/solution.py
+++ b/solution.py
@@ -1,3 +1,4 @@
+import functools
 import math
 
 import jax
@@ -111,30 +112,55 @@
     return pl.ds(pl.multiple_of(head * WIDTH, WIDTH), WIDTH)
 
 
-def split_kernel(place, q, k, v, do, theirs):
-    for y in range(CHIPS):
-        for t, ref in enumerate((q, k, v, do)):
-            theirs[y, t] = ref[:, lanes(2 * y + 1 - place[0])]
-
-
-def chip_rows(place, step, raw, theirs):
-    y = place[1] ^ step
-    head = 2 * y + place[0]
-    return head, [join([ref[:, lanes(head)], theirs[y, t]]) for t, ref in enumerate(raw)]
-
-
-def chip_kernel(offs, place, q, k, v, do, theirs, m0, m1, m2, m3, outs, stats, work):
-    for step, message in enumerate((m0, m1, m2, m3)):
-        head, tensors = chip_rows(place, step, (q, k, v, do), theirs)
-        out, total = attend(*tensors[:3])
-        stat = mixed(total, dotted(tensors[3], out))
+def own_head(step):
+    spot = lax.axis_index("ctx") % PLANE
+    return spot ^ (2 * step)
+
+
+def other_head(step):
+    return own_head(step) ^ 1
+
+
+def split_kernel(q, k, v, do, q_in, k_in, v_in, do_in, theirs, sems):
+    inside = (q_in, k_in, v_in, do_in)
+    copies = [
+        pltpu.make_async_copy(ref, to, sems.at[t])
+        for t, (ref, to) in enumerate(zip((q, k, v, do), inside))
+    ]
+    for copy in copies:
+        copy.start()
+    for t, ref in enumerate(inside):
+        copies[t].wait()
+        for step in range(CHIPS):
+            theirs[step, t] = ref[:, lanes(other_head(step))]
+
+
+def chip_rows(step, raw, theirs):
+    head = own_head(step)
+    return [join([ref[:, lanes(head)], theirs[step, t]]) for t, ref in enumerate(raw)]
+
+
+def chip_kernel(
+    offs_left, q, k, v, do, theirs, m0, m1, m2, m3, outs, stats, work, offs, sem
+):
+    copy = pltpu.make_async_copy(offs_left, offs, sem.at[0])
+    copy.start()
+    tensors = [chip_rows(step, (q, k, v, do), theirs) for step in range(CHIPS)]
+    for step in range(CHIPS):
+        out, total = attend(*tensors[step][:3])
+        stat = mixed(total, dotted(tensors[step][3], out))
         outs[step] = out
         stats[step] = stat
-        for t, rows in enumerate(tensors):
-            work[t] = rows.astype(F32)
-            message[t * ROWS : (t + 1) * ROWS] = load_chosen(work.at[t], offs, head).astype(BF16)
-        work[4] = stat
-        message[BODY:] = pack(load_chosen(work.at[4], offs, head))
+        for t in range(4):
+            work[step, t] = tensors[step][t].astype(F32)
+        work[step, 4] = stat
+    copy.wait()
+    for step, message in enumerate((m0, m1, m2, m3)):
+        head = own_head(step)
+        for t in range(4):
+            picked = load_chosen(work.at[step, t], offs, head)
+            message[t * ROWS : (t + 1) * ROWS] = picked.astype(BF16)
+        message[BODY:] = pack(load_chosen(work.at[step, 4], offs, head))
 
 
 def tensor(ref, t, rows=ROWS):
@@ -157,7 +183,7 @@
     )
 
 
-def near_kernel(m0, m1, m2, m3, outs, stats, g):
+def near_kernel(m0, m1, m2, m3, outs, stats, g, g4):
     refs = (m0, m1, m2, m3)
     stat = [unpack(ref[BODY:]) for ref in refs]
     out = [None] * 4
@@ -180,48 +206,73 @@
         stats[chip] = stat[chip]
     for t in range(4):
         rows = group([tensor(ref, t, 32).astype(F32) for ref in refs])
-        g[t * ROWS : (t + 1) * ROWS] = rows.astype(BF16)
+        rows = rows.astype(BF16)
+        g[t * ROWS : (t + 1) * ROWS] = rows
+        g4[t] = rows[:64]
     g[BODY:] = pack(group(stat))
 
 
-def far_kernel(g, a1, a2, a3, out_far, stats, message):
-    refs = (g, a1, a2, a3)
-    stat = [unpack(ref[BODY:]) for ref in refs]
-    out = None
-    for pair in (0, 2):
-        q, k, v, do = (join([tensor(refs[pair], t), tensor(refs[pair + 1], t)]) for t in range(4))
-        more, total = attend(q, k, v)
-        joined, _, added = combine(join(stat[pair : pair + 2]), total, dotted(do, more))
-        stat[pair], stat[pair + 1] = joined[:ROWS], joined[ROWS:]
-        if pair == 0:
-            out = (more * added)[:ROWS]
-    q, k, v, do = (join([tensor(ref, t, 64) for ref in refs]) for t in range(4))
+def pair_kernel(g, a1, out3, stats, message):
+    refs = (g, a1)
+    q, k, v, do = (join([tensor(ref, t) for ref in refs]) for t in range(4))
     more, total = attend(q, k, v)
-    joined, kept, added = combine(join([s[:64] for s in stat]), total, dotted(do, more))
-    out_far[...] = join([out[:64] * kept[:64] + more[:64] * added[:64], out[64:]])
-    for z in range(4):
-        stat[z] = join([joined[z * 64 : (z + 1) * 64], stat[z][64:]])
-        stats[z] = stat[z]
-    message[...] = join([s[:32] for s in stat]).T[:8]
+    stat, _, added = combine(join([unpack(ref[BODY:]) for ref in refs]), total, dotted(do, more))
+    out3[...] = more[:ROWS] * added[:ROWS]
+    stats[0], stats[1] = stat[:ROWS], stat[ROWS:]
+    message[...] = join([stat[:64], stat[ROWS : ROWS + 64]]).T[:8]
+
+
+def top_kernel(g, a1, a3, a2, top):
+    for t in range(4):
+        top[0, t] = tensor(g, t, 32)
+        top[1, t] = tensor(a1, t, 32)
+        top[2, t] = a3[t, :32]
+        top[3, t] = a2[t, :32]
+
+
+def fours(g, a1, a3, a2):
+    return [join([tensor(g, t, 64), tensor(a1, t, 64), a3[t], a2[t]]) for t in range(4)]
+
+
+def spread(message):
+    return join([message[...]] * 16).T
+
+
+def quad_kernel(g, a1, a3, a2, out3, stats, message3, out_far, stats_far, message):
+    q, k, v, do = fours(g, a1, a3, a2)
+    more, total = attend(q, k, v)
+    old = join([stats[0, :64], stats[1, :64], spread(message3)])
+    stat, kept, added = combine(old, total, dotted(do, more))
+    out_far[...] = join([out3[:64] * kept[:64] + more[:64] * added[:64], out3[64:]])
+    stats_far[...] = stat
+    message[...] = join([stat[64 * z : 64 * z + 32] for z in range(4)]).T[:8]
 
 
 def rest_kernel(
-    m0, m1, m2, m3, outs, stats, g, a1, a2, a3, out_far, stats_far, far5, message5, c0, c1, c2, c3
+    m0, m1, m2, m3, outs, stats, g, a1, a3, a2, out_far, stats_three, stats_far, far5, message5,
+    c0, c1, c2, c3,
 ):
-    refs, fars = (m0, m1, m2, m3), (g, a1, a2, a3)
+    refs = (m0, m1, m2, m3)
     own = [tensor(g, t) for t in range(4)]
     three = [join([tensor(g, t), tensor(a1, t)]) for t in range(4)]
-    four = [join([tensor(ref, t, 64) for ref in fars]) for t in range(4)]
+    four = fours(g, a1, a3, a2)
     five = [
-        join([tensor(ref, t, 32) for ref in fars] + [far5[z, t] for z in range(4)])
+        join([four[t][64 * z : 64 * z + 32] for z in range(4)] + [far5[z, t] for z in range(4)])
         for t in range(4)
     ]
-    far = [stats_far[z] for z in range(4)]
     more, total = attend(*five[:3])
-    old = join([s[:32] for s in far] + [join([message5[...]] * 16).T])
+    old = join([stats_far[64 * z : 64 * z + 32] for z in range(4)] + [spread(message5)])
     stat5, kept, added = combine(old, total, dotted(five[3], more))
-    stat4 = join([join([stat5[32 * z : 32 * z + 32], far[z][32:64]]) for z in range(4)])
-    stat3 = join([join([stat5[32 * z : 32 * z + 32], far[z][32:]]) for z in range(2)])
+    stat4 = join(
+        [
+            rows
+            for z in range(4)
+            for rows in (stat5[32 * z : 32 * z + 32], stats_far[64 * z + 32 : 64 * z + 64])
+        ]
+    )
+    stat3 = join(
+        [rows for z in range(2) for rows in (stat4[64 * z : 64 * z + 64], stats_three[z, 64:])]
+    )
     own_stat = stat3[:ROWS]
     out = join([out_far[:32] * kept[:32] + more[:32] * added[:32], out_far[32:]])
     near = group([stats[chip] for chip in range(4)])
@@ -270,47 +321,61 @@
 
 
 def finish_kernel(
-    offs, place, q, k, v, do, theirs, outs, stats, c0, c1, c2, c3, mine_out, theirs_out, work
+    offs_left, q, k, v, do, theirs, outs, stats, c0, c1, c2, c3, mine_out, theirs_out,
+    work, offs, sem,
 ):
+    copy = pltpu.make_async_copy(offs_left, offs, sem.at[0])
+    copy.start()
+    copy.wait()
     for step, message in enumerate((c0, c1, c2, c3)):
-        head, tensors = chip_rows(place, step, (q, k, v, do), theirs)
-        places = chosen(offs, head)
-        work[4] = stats[step]
+        places = chosen(offs, own_head(step))
+        tensors = chip_rows(step, (q, k, v, do), theirs)
+        work[step, 4] = stats[step]
         final = unpack(message[BODY:])
         for begin, rows in places:
-            work[4, rows, :] = final[begin : begin + rows.size]
-        stat = work[4]
-        work[0] = outs[step] * jnp.exp(total_of(stats[step]) - total_of(stat))
+            work[step, 4, rows, :] = final[begin : begin + rows.size]
+        stat = work[step, 4]
+        work[step, 0] = outs[step] * jnp.exp(total_of(stats[step]) - total_of(stat))
         chance, score = score_parts(*tensors, stat)
-        work[1] = nn(score, tensors[1])
-        work[2] = tn(score, tensors[0])
-        work[3] = tn(chance, tensors[3])
+        work[step, 1] = nn(score, tensors[1])
+        work[step, 2] = tn(score, tensors[0])
+        work[step, 3] = tn(chance, tensors[3])
         for t in range(4):
             part = tensor(message, t).astype(F32)
             for begin, rows in places:
-                work[t, rows, :] = work[t, rows, :] + part[begin : begin + rows.size]
-            mine_out[step, t] = work[t, :ROWS].astype(BF16)
-            theirs_out[step, t] = work[t, ROWS:].astype(BF16)
-
-
-def place_kernel(place, mine, theirs, att, dq, dk, dv):
-    for step in range(CHIPS):
-        head = 2 * (place[1] ^ step)
-        for t, ref in enumerate((att, dq, dk, dv)):
-            ref[:, lanes(head + place[0])] = mine[step, t]
-            ref[:, lanes(head + 1 - place[0])] = theirs[step, t]
-
-
-def call(kernel, name, scalars, outs, scratch, *args):
-    smem = pl.BlockSpec(memory_space=pltpu.SMEM)
-    vmem = pl.BlockSpec(memory_space=pltpu.VMEM)
+                work[step, t, rows, :] = work[step, t, rows, :] + part[begin : begin + rows.size]
+            mine_out[step, t] = work[step, t, :ROWS].astype(BF16)
+            theirs_out[step, t] = work[step, t, ROWS:].astype(BF16)
+
+
+def place_kernel(mine, theirs, att, dq, dk, dv, rows, sems):
+    copies = [
+        pltpu.make_async_copy(rows.at[t], ref, sems.at[t])
+        for t, ref in enumerate((att, dq, dk, dv))
+    ]
+    for t in range(4):
+        for step in range(CHIPS):
+            rows[t, :, lanes(own_head(step))] = mine[step, t]
+            rows[t, :, lanes(other_head(step))] = theirs[step, t]
+        copies[t].start()
+    for copy in copies:
+        copy.wait()
+
+
+VMEM = pl.BlockSpec(memory_space=pltpu.VMEM)
+LEFT = pl.BlockSpec(memory_space=pltpu.HBM)
+
+
+def call(kernel, name, outs, *args, left=0, scratch=(), out_specs=None):
+    stay = [pltpu.with_memory_space_constraint(arg, pltpu.HBM) for arg in args[:left]]
+    args = (*stay, *args[left:])
     return pl.pallas_call(
         kernel,
         name=name,
         out_shape=tuple(jax.ShapeDtypeStruct(shape, dtype) for shape, dtype in outs),
-        in_specs=[smem] * scalars + [vmem] * (len(args) - scalars),
-        out_specs=(vmem,) * len(outs),
-        scratch_shapes=[pltpu.VMEM(shape, F32) for shape in scratch],
+        in_specs=[LEFT] * left + [VMEM] * (len(args) - left),
+        out_specs=out_specs or (VMEM,) * len(outs),
+        scratch_shapes=scratch,
         compiler_params=pltpu.CompilerParams(vmem_limit_bytes=40 * 2**20),
     )(*args)
 
@@ -326,40 +391,56 @@
 
 
 def shards(queries, keys, values, out_grad, offsets):
-    spot = lax.axis_index("ctx") % PLANE
-    place = jnp.stack([spot % 2, spot // 2])
-    raw = (queries, keys, values, out_grad)
+    whole = ((ROWS, HEADS * WIDTH), BF16)
     half = ((CHIPS, 4, ROWS, WIDTH), BF16)
     message = ((MESSAGE, WIDTH), BF16)
+    flat = ((8, WIDTH), F32)
+    rows = ((ROWS, WIDTH), F32)
     quads = ((4, ROWS, WIDTH), F32)
-    chips = ((4, CHIP, WIDTH), F32)
-    (theirs,) = call(split_kernel, "split", 1, [half], [], place, *raw)
+    chips = ((CHIPS, CHIP, WIDTH), F32)
+    fetched = [pltpu.SMEM((6, HEADS), jnp.int32), pltpu.SemaphoreType.DMA((1,))]
+    work = [pltpu.VMEM((CHIPS, 5, CHIP, WIDTH), F32)] + fetched
+    *raw, theirs = call(
+        split_kernel, "split", [whole] * 4 + [half], queries, keys, values, out_grad,
+        left=4, scratch=[pltpu.SemaphoreType.DMA((4,))],
+    )
     theirs = in_plane(theirs, 1)
     *sent, outs0, stats0 = call(
-        chip_kernel, "chip", 2, [message] * 4 + [chips] * 2, [(5, CHIP, WIDTH)],
-        offsets, place, *raw, theirs,
+        chip_kernel, "chip", [message] * 4 + [chips] * 2, offsets, *raw, theirs,
+        left=1, scratch=work,
     )
     got = [sent[0]] + [in_plane(sent[step], 2 * step) for step in (1, 2, 3)]
-    outs, stats, g = call(near_kernel, "near", 0, [quads, quads, message], [], *got)
-    fars = [g] + [across(g, flip) for flip in (1, 2, 3)]
-    top = jnp.stack([far[:BODY].reshape(4, ROWS, WIDTH)[:, :32] for far in fars])
+    outs, stats, g, g4 = call(
+        near_kernel, "near", [quads, quads, message, ((4, 64, WIDTH), BF16)], *got
+    )
+    a1 = across(g, 1)
+    a3 = across(g4, 3)
+    a2 = across(g4, 2)
+    out3, stats3, message3 = call(
+        pair_kernel, "pair", [rows, ((2, ROWS, WIDTH), F32), flat], g, a1
+    )
+    a3, a2, message3 = lax.optimization_barrier((a3, a2, across(message3, 3)))
+    fars = (g, a1, a3, a2)
+    (top,) = call(top_kernel, "top", [((4, 4, 32, WIDTH), BF16)], *fars)
     top = across(top, 7)
     out_far, stats_far, message5 = call(
-        far_kernel, "far", 0, [((ROWS, WIDTH), F32), quads, ((8, WIDTH), F32)], [], *fars
+        quad_kernel, "quad", [rows, ((SEG, WIDTH), F32), flat], *fars, out3, stats3, message3
     )
     message5 = across(message5, 7)
     back = call(
-        rest_kernel, "rest", 0, [message] * 4, [],
-        *got, outs, stats, *fars, out_far, stats_far, top, message5,
+        rest_kernel, "rest", [message] * 4,
+        *got, outs, stats, *fars, out_far, stats3, stats_far, top, message5,
     )
     back = [back[0]] + [in_plane(back[step], 2 * step) for step in (1, 2, 3)]
-    mine, theirs_out = call(
-        finish_kernel, "finish", 2, [half, half], [(5, CHIP, WIDTH)],
-        offsets, place, *raw, theirs, outs0, stats0, *back,
-    )
-    theirs_out = in_plane(theirs_out, 1)
-    row = ((ROWS, HEADS * WIDTH), BF16)
-    return call(place_kernel, "place", 1, [row] * 4, [], place, mine, theirs_out)
+    mine, theirs = call(
+        finish_kernel, "finish", [half, half], offsets, *raw, theirs, outs0, stats0, *back,
+        left=1, scratch=work,
+    )
+    theirs = in_plane(theirs, 1)
+    return call(
+        place_kernel, "place", [whole] * 4, mine, theirs, out_specs=(LEFT,) * 4,
+        scratch=[pltpu.VMEM((4, ROWS, HEADS * WIDTH), BF16), pltpu.SemaphoreType.DMA((4,))],
+    )
 
 
 def solution(mesh):

time: 74.6 us -> 65.5 us (0.88)
  waiting for transfers between devices: 25.8 us -> 19.2 us
  local copies, waits for them, and re-layouts: 5.42 us -> 0 us
  starting transfers between devices: 26.1 us -> 30.4 us
  Pallas kernels: 16.2 us -> 14.9 us
    ppermute x5 -> x6, waiting for transfers between devices: 12.2 us -> 5.7 us  [across(): return lax.ppermute(array, 'ctx', moves)]
    unnamed x22 -> x0, local copies, waits for them, and re-layouts: 4.48 us -> none
    ppermute x5 -> x6, starting transfers between devices: 10.1 us -> 13.3 us  [across(): return lax.ppermute(array, 'ctx', moves)]
    pallas_call x7 -> x9, Pallas kernels: 16.2 us -> 14.9 us  [call(): pl.pallas_call(kernel, name=name, out_shape=tuple((jax.ShapeDtypeStruct(s...]
    ppermute x8, starting transfers between devices: 16 us -> 17.1 us  [in_plane(): return lax.ppermute(array, 'ctx', moves)]
    slice x5 -> x0, local copies, waits for them, and re-layouts: 0.92 us -> none  [shards(): far[:BODY].reshape(4, ROWS, WIDTH)[:, :32]]
  transfers between devices with their start and end apart: 13 -> 14, of which waited for: 10 -> 9; matrix products, arithmetic and copies ran while one was open for 0% -> 0% of each run, Pallas kernels for 3% -> 2%
where the time goes in v2:
time: 65.5 us; the launch traced here: 65.3 us
  starting transfers between devices  30.4 us (46%)
  waiting for transfers between devices  19.2 us (29%)
  Pallas kernels  14.9 us (23%)
  between operations  0.86 us (1%)
    ppermute x8, starting transfers between devices, in_plane(): return lax.ppermute(array, 'ctx', moves)  17.1 us
    pallas_call x9, Pallas kernels, call(): pl.pallas_call(kernel, name=name, out_shape=tuple((jax.ShapeDtypeStruct(s...  14.9 us
    ppermute x8, waiting for transfers between devices, in_plane(): return lax.ppermute(array, 'ctx', moves)  13.5 us
    ppermute x6, starting transfers between devices, across(): return lax.ppermute(array, 'ctx', moves)  13.3 us
    ppermute x6, waiting for transfers between devices, across(): return lax.ppermute(array, 'ctx', moves)  5.7 us
  transfers between devices with their start and end apart: 14, of which 9 were waited for; matrix products, arithmetic and copies ran while one was open for 0% of the time, Pallas kernels for 2%

profile of v2, /device:TPU:1, one launch (start us, length us, event | category | flops | bytes accessed | tf_op | source)
XLA Modules:
  0.0 65.3 jit_solution(6226578812727845620)
XLA Ops:
  0.6 1.3 %split.1 = (bf16[128,1024]{1,0:T(8,128)(2,1)S(1)}, bf16[128,1024]{1,0:T(8,128)(2,1)S(1)}, bf16[128,1024]{1,0:T(8,128)(2,1)S(1)}, bf16[128,1024]{1,0:T(8,128)(2,1)S(1)}, bf16[4,4,128,128]{3,2,1,0:T(8,128)(2,1)S(1)}) custom-call(bf16[128,1024]{1,0:T(8,128)(2,1)} %q.1, bf16[128,1024]{1,0:T(8,128)(2,1)} %k.1, bf16[128,1024]{1,0:T(8,128)(2,1)} %v.1, ...), custom_call_target="tpu_custom_call" | custom-call | tf_op jit(solution)/shard_map/split/pallas_call | solution.py:372
  1.9 3.3 %collective-permute-start = (bf16[4,4,128,128]{3,2,1,0:T(8,128)(2,1)S(1)}, bf16[4,4,128,128]{3,2,1,0:T(8,128)(2,1)S(1)}, u32[]{:S(2)}, u32[]{:S(2)}) collective-permute-start(bf16[4,4,128,128]{3,2,1,0:T(8,128)(2,1)S(1)} %get-tuple-element.38), channel_id=1, source_target_pairs={{0,1},{1,0},{2,3},{3,2},{4,5},{5,4},{6,7},{7,6},{8,9},{9,8},{10,11... | collective-permute-start | bytes 1572872 | tf_op jit(solution)/shard_map/ppermute | solution.py:385
  5.2 1.5 %collective-permute-done.theirs = bf16[4,4,128,128]{3,2,1,0:T(8,128)(2,1)S(1)} collective-permute-done((bf16[4,4,128,128]{3,2,1,0:T(8,128)(2,1)S(1)}, bf16[4,4,128,128]{3,2,1,0:T(8,128)(2,1)S(1)}, u32[]{:S(2)}, u32[]{:S(2)}) %collective-permute-start) | collective-permute-done | bytes 524320 | tf_op jit(solution)/shard_map/ppermute | solution.py:385
  6.8 1.8 %chip.1 = (bf16[544,128]{1,0:T(8,128)(2,1)S(1)}, bf16[544,128]{1,0:T(8,128)(2,1)S(1)}, bf16[544,128]{1,0:T(8,128)(2,1)S(1)}, bf16[544,128]{1,0:T(8,128)(2,1)S(1)...) custom-call(s32[6,8]{1,0:T(8,128)} %offs_left.3, bf16[128,1024]{1,0:T(8,128)(2,1)S(1)} %get-tuple-element.34.q, ...), custom_call_target="tpu_custom_call" | custom-call | tf_op jit(solution)/shard_map/chip/pallas_call | solution.py:372
  8.5 0.1 collective-permute-start.1
  8.6 2.2 %collective-permute-start.2 = (bf16[544,128]{1,0:T(8,128)(2,1)S(1)}, bf16[544,128]{1,0:T(8,128)(2,1)S(1)}, u32[]{:S(2)}, u32[]{:S(2)}) collective-permute-start(bf16[544,128]{1,0:T(8,128)(2,1)S(1)} %get-tuple-element.43), channel_id=1, source_target_pairs={{0,4},{1,5},{2,6},{3,7},{4,0},{5,1},{6,2},{7,3},{8,12},{9,13},{10,... | collective-permute-start | bytes 417800 | tf_op jit(solution)/shard_map/ppermute | solution.py:385
  10.8 1.7 %collective-permute-start.3 = (bf16[544,128]{1,0:T(8,128)(2,1)S(1)}, bf16[544,128]{1,0:T(8,128)(2,1)S(1)}, u32[]{:S(2)}, u32[]{:S(2)}) collective-permute-start(bf16[544,128]{1,0:T(8,128)(2,1)S(1)} %get-tuple-element.44), channel_id=1, source_target_pairs={{0,6},{1,7},{2,4},{3,5},{4,2},{5,3},{6,0},{7,1},{8,14},{9,15},{10,... | collective-permute-start | bytes 417800 | tf_op jit(solution)/shard_map/ppermute | solution.py:385
  12.5 1.0 %collective-permute-done.1.m1 = bf16[544,128]{1,0:T(8,128)(2,1)S(1)} collective-permute-done((bf16[544,128]{1,0:T(8,128)(2,1)S(1)}, bf16[544,128]{1,0:T(8,128)(2,1)S(1)}, u32[]{:S(2)}, u32[]{:S(2)}) %collective-permute-start.1) | collective-permute-done | bytes 139296 | tf_op jit(solution)/shard_map/ppermute | solution.py:385
  13.5 3.8 %collective-permute-done.2.m2 = bf16[544,128]{1,0:T(8,128)(2,1)S(1)} collective-permute-done((bf16[544,128]{1,0:T(8,128)(2,1)S(1)}, bf16[544,128]{1,0:T(8,128)(2,1)S(1)}, u32[]{:S(2)}, u32[]{:S(2)}) %collective-permute-start.2) | collective-permute-done | bytes 139296 | tf_op jit(solution)/shard_map/ppermute | solution.py:385
  17.3 2.5 %collective-permute-done.3.m3 = bf16[544,128]{1,0:T(8,128)(2,1)S(1)} collective-permute-done((bf16[544,128]{1,0:T(8,128)(2,1)S(1)}, bf16[544,128]{1,0:T(8,128)(2,1)S(1)}, u32[]{:S(2)}, u32[]{:S(2)}) %collective-permute-start.3) | collective-permute-done | bytes 139296 | tf_op jit(solution)/shard_map/ppermute | solution.py:385
  19.7 2.6 %near.1 = (f32[4,128,128]{2,1,0:T(8,128)S(1)}, f32[4,128,128]{2,1,0:T(8,128)S(1)}, bf16[544,128]{1,0:T(8,128)(2,1)S(1)}, bf16[4,64,128]{2,1,0:T(8,128)(2,1)S(1)}) custom-call(bf16[544,128]{1,0:T(8,128)(2,1)S(1)} %get-tuple-element.41.m0, bf16[544,128]{1,0:T(8,128)(2,1)S(1)} %collective-permute-done.1.m1, bf16[544,128]{1,0:T(8,128)(2,1)S(1)} %collective-permute-done.2.m2, ...), custom_call_target="tpu_custom_call" | custom-call | tf_op jit(solution)/shard_map/near/pallas_call | solution.py:372
  22.3 1.7 %collective-permute-start.4 = (bf16[544,128]{1,0:T(8,128)(2,1)S(1)}, bf16[544,128]{1,0:T(8,128)(2,1)S(1)}, u32[]{:S(2)}, u32[]{:S(2)}) collective-permute-start(bf16[544,128]{1,0:T(8,128)(2,1)S(1)} %get-tuple-element.47.g), channel_id=1, source_target_pairs={{0,8},{1,9},{2,10},{3,11},{4,12},{5,13},{6,14},{7,15},{8,0},{9,1},... | collective-permute-start | bytes 417800 | tf_op jit(solution)/shard_map/ppermute | solution.py:390
  24.0 3.0 %collective-permute-start.6 = (bf16[4,64,128]{2,1,0:T(8,128)(2,1)S(1)}, bf16[4,64,128]{2,1,0:T(8,128)(2,1)S(1)}, u32[]{:S(2)}, u32[]{:S(2)}) collective-permute-start(bf16[4,64,128]{2,1,0:T(8,128)(2,1)S(1)} %get-tuple-element.48), channel_id=1, source_target_pairs={{0,16},{1,17},{2,18},{3,19},{4,20},{5,21},{6,22},{7,23},{8,24},{9,... | collective-permute-start | bytes 196616 | tf_op jit(solution)/shard_map/ppermute | solution.py:390
  27.0 0.0 collective-permute-start.5
  27.0 0.0 collective-permute-done.4.a1
  27.0 0.8 %pair.1 = (f32[128,128]{1,0:T(8,128)S(1)}, f32[2,128,128]{2,1,0:T(8,128)S(1)}, f32[8,128]{1,0:T(8,128)S(1)}) custom-call(bf16[544,128]{1,0:T(8,128)(2,1)S(1)} %get-tuple-element.47.g, bf16[544,128]{1,0:T(8,128)(2,1)S(1)} %collective-permute-done.4.a1), custom_call_target="tpu_custom_call" | custom-call | tf_op jit(solution)/shard_map/pair/pallas_call | solution.py:372
  27.8 5.0 %collective-permute-start.7 = (f32[8,128]{1,0:T(8,128)S(1)}, f32[8,128]{1,0:T(8,128)S(1)}, u32[]{:S(2)}, u32[]{:S(2)}) collective-permute-start(f32[8,128]{1,0:T(8,128)S(1)} %get-tuple-element.49), channel_id=1, source_target_pairs={{0,24},{1,25},{2,26},{3,27},{4,28},{5,29},{6,30},{7,31},{8,16},{9,... | collective-permute-start | bytes 12296 | tf_op jit(solution)/shard_map/ppermute | solution.py:390
  32.8 0.0 collective-permute-done.6.a2
  32.8 0.0 collective-permute-done.5.a3
  32.8 1.3 %collective-permute-done.7.message3 = f32[8,128]{1,0:T(8,128)S(1)} collective-permute-done((f32[8,128]{1,0:T(8,128)S(1)}, f32[8,128]{1,0:T(8,128)S(1)}, u32[]{:S(2)}, u32[]{:S(2)}) %collective-permute-start.7) | collective-permute-done | bytes 4128 | tf_op jit(solution)/shard_map/ppermute | solution.py:390
  34.1 3.4 %collective-permute-start.8 = (bf16[4,4,32,128]{3,2,1,0:T(8,128)(2,1)S(1)}, bf16[4,4,32,128]{3,2,1,0:T(8,128)(2,1)S(1)}, u32[]{:S(2)}, u32[]{:S(2)}) collective-permute-start(bf16[4,4,32,128]{3,2,1,0:T(8,128)(2,1)S(1)} %top.1), channel_id=1, source_target_pairs={{0,56},{1,57},{2,58},{3,59},{4,60},{5,61},{6,62},{7,63},{8,48},{9,... | collective-permute-start | bytes 393224 | tf_op jit(solution)/shard_map/ppermute | solution.py:390
  37.5 0.8 %quad.1 = (f32[128,128]{1,0:T(8,128)S(1)}, f32[256,128]{1,0:T(8,128)S(1)}, f32[8,128]{1,0:T(8,128)S(1)}) custom-call(bf16[544,128]{1,0:T(8,128)(2,1)S(1)} %get-tuple-element.47.g, bf16[544,128]{1,0:T(8,128)(2,1)S(1)} %collective-permute-done.4.a1, bf16[4,64,128]{2,1,0:T(8,128)(2,1)S(1)} %collective-permute-done.5.a3, ...), custom_call_target="tpu_custom_call" | custom-call | tf_op jit(solution)/shard_map/quad/pallas_call | solution.py:372
  38.3 0.3 collective-permute-start.9
  38.5 4.4 %collective-permute-done.9.message5 = f32[8,128]{1,0:T(8,128)S(1)} collective-permute-done((f32[8,128]{1,0:T(8,128)S(1)}, f32[8,128]{1,0:T(8,128)S(1)}, u32[]{:S(2)}, u32[]{:S(2)}) %collective-permute-start.9) | collective-permute-done | bytes 4128 | tf_op jit(solution)/shard_map/ppermute | solution.py:390
  42.9 0.0 collective-permute-done.8.far5
  42.9 3.0 %rest.1 = (bf16[544,128]{1,0:T(8,128)(2,1)S(1)}, bf16[544,128]{1,0:T(8,128)(2,1)S(1)}, bf16[544,128]{1,0:T(8,128)(2,1)S(1)}, bf16[544,128]{1,0:T(8,128)(2,1)S(1)}) custom-call(bf16[544,128]{1,0:T(8,128)(2,1)S(1)} %get-tuple-element.41.m0, bf16[544,128]{1,0:T(8,128)(2,1)S(1)} %collective-permute-done.1.m1, bf16[544,128]{1,0:T(8,128)(2,1)S(1)} %collective-permute-done.2.m2, ...), custom_call_target="tpu_custom_call" | custom-call | tf_op jit(solution)/shard_map/rest/pallas_call | solution.py:372
  46.0 0.1 collective-permute-start.10
  46.1 1.5 %collective-permute-start.11 = (bf16[544,128]{1,0:T(8,128)(2,1)S(1)}, bf16[544,128]{1,0:T(8,128)(2,1)S(1)}, u32[]{:S(2)}, u32[]{:S(2)}) collective-permute-start(bf16[544,128]{1,0:T(8,128)(2,1)S(1)} %get-tuple-element.60), channel_id=1, source_target_pairs={{0,4},{1,5},{2,6},{3,7},{4,0},{5,1},{6,2},{7,3},{8,12},{9,13},{10,... | collective-permute-start | bytes 417800 | tf_op jit(solution)/shard_map/ppermute | solution.py:385
  47.6 2.3 %collective-permute-start.12 = (bf16[544,128]{1,0:T(8,128)(2,1)S(1)}, bf16[544,128]{1,0:T(8,128)(2,1)S(1)}, u32[]{:S(2)}, u32[]{:S(2)}) collective-permute-start(bf16[544,128]{1,0:T(8,128)(2,1)S(1)} %get-tuple-element.61), channel_id=1, source_target_pairs={{0,6},{1,7},{2,4},{3,5},{4,2},{5,3},{6,0},{7,1},{8,14},{9,15},{10,... | collective-permute-start | bytes 417800 | tf_op jit(solution)/shard_map/ppermute | solution.py:385
  49.9 0.0 collective-permute-done.10.c1
  50.0 1.6 %collective-permute-done.11.c2 = bf16[544,128]{1,0:T(8,128)(2,1)S(1)} collective-permute-done((bf16[544,128]{1,0:T(8,128)(2,1)S(1)}, bf16[544,128]{1,0:T(8,128)(2,1)S(1)}, u32[]{:S(2)}, u32[]{:S(2)}) %collective-permute-start.11) | collective-permute-done | bytes 139296 | tf_op jit(solution)/shard_map/ppermute | solution.py:385
  51.6 1.5 %collective-permute-done.12.c3 = bf16[544,128]{1,0:T(8,128)(2,1)S(1)} collective-permute-done((bf16[544,128]{1,0:T(8,128)(2,1)S(1)}, bf16[544,128]{1,0:T(8,128)(2,1)S(1)}, u32[]{:S(2)}, u32[]{:S(2)}) %collective-permute-start.12) | collective-permute-done | bytes 139296 | tf_op jit(solution)/shard_map/ppermute | solution.py:385
  53.1 3.6 %finish.1 = (bf16[4,4,128,128]{3,2,1,0:T(8,128)(2,1)S(1)}, bf16[4,4,128,128]{3,2,1,0:T(8,128)(2,1)S(1)}) custom-call(s32[6,8]{1,0:T(8,128)} %offs_left.3, bf16[128,1024]{1,0:T(8,128)(2,1)S(1)} %get-tuple-element.34.q, bf16[128,1024]{1,0:T(8,128)(2,1)S(1)} %get-tuple-element.35.k, bf16[128,1024]{1,0:T(8,128)(2,1)S(1)} %get-tuple-element.36.v, ...), custom_call_target="tpu_custom_call" | custom-call | tf_op jit(solution)/shard_map/finish/pallas_call | solution.py:372
  56.7 5.9 %collective-permute-start.13 = (bf16[4,4,128,128]{3,2,1,0:T(8,128)(2,1)S(1)}, bf16[4,4,128,128]{3,2,1,0:T(8,128)(2,1)S(1)}, u32[]{:S(2)}, u32[]{:S(2)}) collective-permute-start(bf16[4,4,128,128]{3,2,1,0:T(8,128)(2,1)S(1)} %get-tuple-element.63), channel_id=1, source_target_pairs={{0,1},{1,0},{2,3},{3,2},{4,5},{5,4},{6,7},{7,6},{8,9},{9,8},{10,11... | collective-permute-start | bytes 1572872 | tf_op jit(solution)/shard_map/ppermute | solution.py:385
  62.6 1.5 %collective-permute-done.13.theirs = bf16[4,4,128,128]{3,2,1,0:T(8,128)(2,1)S(1)} collective-permute-done((bf16[4,4,128,128]{3,2,1,0:T(8,128)(2,1)S(1)}, bf16[4,4,128,128]{3,2,1,0:T(8,128)(2,1)S(1)}, u32[]{:S(2)}, u32[]{:S(2)}) %collective-permute-start.13) | collective-permute-done | bytes 524320 | tf_op jit(solution)/shard_map/ppermute | solution.py:385
  64.1 1.1 %place.1 = (bf16[128,1024]{1,0:T(8,128)(2,1)}, bf16[128,1024]{1,0:T(8,128)(2,1)}, bf16[128,1024]{1,0:T(8,128)(2,1)}, bf16[128,1024]{1,0:T(8,128)(2,1)}) custom-call(bf16[4,4,128,128]{3,2,1,0:T(8,128)(2,1)S(1)} %get-tuple-element.62.mine, bf16[4,4,128,128]{3,2,1,0:T(8,128)(2,1)S(1)} %collective-permute-done.13.theirs), custom_call_target="tpu_custom_call" | custom-call | tf_op jit(solution)/shard_map/place/pallas_call | solution.py:372
  (1 shorter events, 0.0 us)
Async XLA Ops:
  1.9 4.9 %collective-permute-start = (bf16[4,4,128,128]{3,2,1,0:T(8,128)(2,1)S(1)}, bf16[4,4,128,128]{3,2,1,0:T(8,128)(2,1)S(1)}, u32[]{:S(2)}, u32[]{:S(2)}) collective-permute-start(bf16[4,4,128,128]{3,2,1,0:T(8,128)(2,1)S(1)} %get-tuple-element.38), channel_id=1, source_target_pairs={{0,1},{1,0},{2,3},{3,2},{4,5},{5,4},{6,7},{7,6},{8,9},{9,8},{10,11... | collective-permute-start | bytes 1572872 | tf_op jit(solution)/shard_map/ppermute | solution.py:385
  8.5 5.0 %collective-permute-start.1 = (bf16[544,128]{1,0:T(8,128)(2,1)S(1)}, bf16[544,128]{1,0:T(8,128)(2,1)S(1)}, u32[]{:S(2)}, u32[]{:S(2)}) collective-permute-start(bf16[544,128]{1,0:T(8,128)(2,1)S(1)} %get-tuple-element.42), channel_id=1, source_target_pairs={{0,2},{1,3},{2,0},{3,1},{4,6},{5,7},{6,4},{7,5},{8,10},{9,11},{10,... | collective-permute-start | bytes 417800 | tf_op jit(solution)/shard_map/ppermute | solution.py:385
  8.6 8.6 %collective-permute-start.2 = (bf16[544,128]{1,0:T(8,128)(2,1)S(1)}, bf16[544,128]{1,0:T(8,128)(2,1)S(1)}, u32[]{:S(2)}, u32[]{:S(2)}) collective-permute-start(bf16[544,128]{1,0:T(8,128)(2,1)S(1)} %get-tuple-element.43), channel_id=1, source_target_pairs={{0,4},{1,5},{2,6},{3,7},{4,0},{5,1},{6,2},{7,3},{8,12},{9,13},{10,... | collective-permute-start | bytes 417800 | tf_op jit(solution)/shard_map/ppermute | solution.py:385
  10.8 8.9 %collective-permute-start.3 = (bf16[544,128]{1,0:T(8,128)(2,1)S(1)}, bf16[544,128]{1,0:T(8,128)(2,1)S(1)}, u32[]{:S(2)}, u32[]{:S(2)}) collective-permute-start(bf16[544,128]{1,0:T(8,128)(2,1)S(1)} %get-tuple-element.44), channel_id=1, source_target_pairs={{0,6},{1,7},{2,4},{3,5},{4,2},{5,3},{6,0},{7,1},{8,14},{9,15},{10,... | collective-permute-start | bytes 417800 | tf_op jit(solution)/shard_map/ppermute | solution.py:385
  22.3 4.7 %collective-permute-start.4 = (bf16[544,128]{1,0:T(8,128)(2,1)S(1)}, bf16[544,128]{1,0:T(8,128)(2,1)S(1)}, u32[]{:S(2)}, u32[]{:S(2)}) collective-permute-start(bf16[544,128]{1,0:T(8,128)(2,1)S(1)} %get-tuple-element.47.g), channel_id=1, source_target_pairs={{0,8},{1,9},{2,10},{3,11},{4,12},{5,13},{6,14},{7,15},{8,0},{9,1},... | collective-permute-start | bytes 417800 | tf_op jit(solution)/shard_map/ppermute | solution.py:390
  24.0 8.8 %collective-permute-start.6 = (bf16[4,64,128]{2,1,0:T(8,128)(2,1)S(1)}, bf16[4,64,128]{2,1,0:T(8,128)(2,1)S(1)}, u32[]{:S(2)}, u32[]{:S(2)}) collective-permute-start(bf16[4,64,128]{2,1,0:T(8,128)(2,1)S(1)} %get-tuple-element.48), channel_id=1, source_target_pairs={{0,16},{1,17},{2,18},{3,19},{4,20},{5,21},{6,22},{7,23},{8,24},{9,... | collective-permute-start | bytes 196616 | tf_op jit(solution)/shard_map/ppermute | solution.py:390
  27.0 5.8 %collective-permute-start.5 = (bf16[4,64,128]{2,1,0:T(8,128)(2,1)S(1)}, bf16[4,64,128]{2,1,0:T(8,128)(2,1)S(1)}, u32[]{:S(2)}, u32[]{:S(2)}) collective-permute-start(bf16[4,64,128]{2,1,0:T(8,128)(2,1)S(1)} %get-tuple-element.48), channel_id=1, source_target_pairs={{0,24},{1,25},{2,26},{3,27},{4,28},{5,29},{6,30},{7,31},{8,16},{9,... | collective-permute-start | bytes 196616 | tf_op jit(solution)/shard_map/ppermute | solution.py:390
  27.8 6.3 %collective-permute-start.7 = (f32[8,128]{1,0:T(8,128)S(1)}, f32[8,128]{1,0:T(8,128)S(1)}, u32[]{:S(2)}, u32[]{:S(2)}) collective-permute-start(f32[8,128]{1,0:T(8,128)S(1)} %get-tuple-element.49), channel_id=1, source_target_pairs={{0,24},{1,25},{2,26},{3,27},{4,28},{5,29},{6,30},{7,31},{8,16},{9,... | collective-permute-start | bytes 12296 | tf_op jit(solution)/shard_map/ppermute | solution.py:390
  34.1 8.8 %collective-permute-start.8 = (bf16[4,4,32,128]{3,2,1,0:T(8,128)(2,1)S(1)}, bf16[4,4,32,128]{3,2,1,0:T(8,128)(2,1)S(1)}, u32[]{:S(2)}, u32[]{:S(2)}) collective-permute-start(bf16[4,4,32,128]{3,2,1,0:T(8,128)(2,1)S(1)} %top.1), channel_id=1, source_target_pairs={{0,56},{1,57},{2,58},{3,59},{4,60},{5,61},{6,62},{7,63},{8,48},{9,... | collective-permute-start | bytes 393224 | tf_op jit(solution)/shard_map/ppermute | solution.py:390
  38.3 4.7 %collective-permute-start.9 = (f32[8,128]{1,0:T(8,128)S(1)}, f32[8,128]{1,0:T(8,128)S(1)}, u32[]{:S(2)}, u32[]{:S(2)}) collective-permute-start(f32[8,128]{1,0:T(8,128)S(1)} %get-tuple-element.57), channel_id=1, source_target_pairs={{0,56},{1,57},{2,58},{3,59},{4,60},{5,61},{6,62},{7,63},{8,48},{9,... | collective-permute-start | bytes 12296 | tf_op jit(solution)/shard_map/ppermute | solution.py:390
  46.0 4.0 %collective-permute-start.10 = (bf16[544,128]{1,0:T(8,128)(2,1)S(1)}, bf16[544,128]{1,0:T(8,128)(2,1)S(1)}, u32[]{:S(2)}, u32[]{:S(2)}) collective-permute-start(bf16[544,128]{1,0:T(8,128)(2,1)S(1)} %get-tuple-element.59), channel_id=1, source_target_pairs={{0,2},{1,3},{2,0},{3,1},{4,6},{5,7},{6,4},{7,5},{8,10},{9,11},{10,... | collective-permute-start | bytes 417800 | tf_op jit(solution)/shard_map/ppermute | solution.py:385
  46.1 5.5 %collective-permute-start.11 = (bf16[544,128]{1,0:T(8,128)(2,1)S(1)}, bf16[544,128]{1,0:T(8,128)(2,1)S(1)}, u32[]{:S(2)}, u32[]{:S(2)}) collective-permute-start(bf16[544,128]{1,0:T(8,128)(2,1)S(1)} %get-tuple-element.60), channel_id=1, source_target_pairs={{0,4},{1,5},{2,6},{3,7},{4,0},{5,1},{6,2},{7,3},{8,12},{9,13},{10,... | collective-permute-start | bytes 417800 | tf_op jit(solution)/shard_map/ppermute | solution.py:385
  47.6 5.4 %collective-permute-start.12 = (bf16[544,128]{1,0:T(8,128)(2,1)S(1)}, bf16[544,128]{1,0:T(8,128)(2,1)S(1)}, u32[]{:S(2)}, u32[]{:S(2)}) collective-permute-start(bf16[544,128]{1,0:T(8,128)(2,1)S(1)} %get-tuple-element.61), channel_id=1, source_target_pairs={{0,6},{1,7},{2,4},{3,5},{4,2},{5,3},{6,0},{7,1},{8,14},{9,15},{10,... | collective-permute-start | bytes 417800 | tf_op jit(solution)/shard_map/ppermute | solution.py:385
  56.7 7.4 %collective-permute-start.13 = (bf16[4,4,128,128]{3,2,1,0:T(8,128)(2,1)S(1)}, bf16[4,4,128,128]{3,2,1,0:T(8,128)(2,1)S(1)}, u32[]{:S(2)}, u32[]{:S(2)}) collective-permute-start(bf16[4,4,128,128]{3,2,1,0:T(8,128)(2,1)S(1)} %get-tuple-element.63), channel_id=1, source_target_pairs={{0,1},{1,0},{2,3},{3,2},{4,5},{5,4},{6,7},{7,6},{8,9},{9,8},{10,11... | collective-permute-start | bytes 1572872 | tf_op jit(solution)/shard_map/ppermute | solution.py:385

commit v3 on v2

v3 whole, which is shorter than its diff:
```python
import functools
import math

import jax
import jax.numpy as jnp
from jax import lax
from jax.experimental import pallas as pl
from jax.experimental.pallas import tpu as pltpu
from jax.sharding import PartitionSpec as P

HEADS = 8
WIDTH = 128
ROWS = 128
CHIP = 2 * ROWS
CHIPS = 4
PLANE = 2 * CHIPS
DEPTH = 8
SEG = 256
BODY = 4 * ROWS
MESSAGE = BODY + 32
SCALE = 1.0 / math.sqrt(WIDTH)
F32 = jnp.float32
BF16 = jnp.bfloat16


def nt(a, b):
    return lax.dot_general(a, b, (((1,), (1,)), ((), ())), preferred_element_type=F32)


def nn(a, b):
    return lax.dot_general(a, b, (((1,), (0,)), ((), ())), preferred_element_type=F32)


def tn(a, b):
    return lax.dot_general(a, b, (((0,), (0,)), ((), ())), preferred_element_type=F32)


def join(parts):
    return jnp.concatenate(parts, axis=0)


def attend(*blocks):
    scores = [nt(q, k) * SCALE for q, k, _ in blocks]
    peaks = [jnp.max(s, axis=1, keepdims=True) for s in scores]
    grown = [jnp.exp(s - peak) for s, peak in zip(scores, peaks)]
    masses = [jnp.sum(g, axis=1, keepdims=True) for g in grown]
    weights = [(g * (1.0 / mass)).astype(BF16) for g, mass in zip(grown, masses)]
    outs = [nn(w, v) for w, (_, _, v) in zip(weights, blocks)]
    return [(o, wide(peak + jnp.log(mass))) for o, peak, mass in zip(outs, peaks, masses)]


def dotted(a, b):
    return wide(jnp.sum(a.astype(F32) * b, axis=1, keepdims=True))


def wide(column):
    return jnp.broadcast_to(column, (column.shape[0], WIDTH))


def across_lanes(column):
    return jnp.concatenate([column, column], axis=1)


def rows_of(stat, begin, end):
    return [column[begin:end] for column in stat]


def stack(stats):
    return [join([stat[i] for stat in stats]) for i in range(2)]


def combine(stat, total, delta):
    peak = jnp.maximum(stat[0], total)
    kept, added = jnp.exp(stat[0] - peak), jnp.exp(total - peak)
    mass = kept + added
    share = 1.0 / mass
    kept, added = kept * share, added * share
    return [peak + jnp.log(mass), kept * stat[1] + added * delta], kept, added


def flatten(stat):
    lane = lax.broadcasted_iota(jnp.int32, (1, WIDTH), 1)
    return jnp.where(lane & 4 == 0, stat[0], stat[1]).T[:8]


def unflatten(flat):
    return [jnp.broadcast_to(flat[i : i + 1], (WIDTH, flat.shape[1])).T for i in (0, 4)]


def three_terms(values):
    high = values.astype(BF16).astype(F32)
    middle = (values - high).astype(BF16).astype(F32)
    return [term.astype(BF16) for term in (high, middle, values - high - middle)]


def pack(stat):
    flat = flatten(stat)
    return join([term.astype(F32) for term in three_terms(flat)] + [jnp.zeros_like(flat)]).astype(BF16)


def unpack(rows):
    terms = rows.astype(F32)
    return unflatten(terms[:8] + terms[8:16] + terms[16:24])


def products(blocks):
    return [nt(q, k) for q, k, _, _ in blocks], [nt(do, v) for _, _, v, do in blocks]


def fit(column, columns):
    return across_lanes(column) if columns == SEG else column[:, :columns]


def scored(scores, grads, stats):
    chances = [
        jnp.exp(s * SCALE - fit(stat[0], s.shape[1])) for s, stat in zip(scores, stats)
    ]
    parts = [
        (chance * (grad - fit(stat[1], grad.shape[1])) * SCALE).astype(BF16)
        for chance, grad, stat in zip(chances, grads, stats)
    ]
    return [(chance.astype(BF16), part) for chance, part in zip(chances, parts)]


def position(offs, head, i):
    place = (offs[2, head] ^ 2) + 4 * (i - 64)
    for below, level, flip, begin in ((64, 3, 4, 32), (32, 4, 8, 16), (16, 5, 16, 8), (8, 5, 0, 0)):
        stride = 32 if level == 5 else 2**level
        place = jnp.where(i < below, (offs[level, head] ^ flip) + stride * (i - begin), place)
    return place


def picking(offs, head):
    i = lax.broadcasted_iota(jnp.int32, (ROWS, WIDTH), 0)
    lane = lax.broadcasted_iota(jnp.int32, (ROWS, WIDTH), 1)
    place = position(offs, head, i)
    hits = [jnp.where(place == lane + begin, 1.0, 0.0).astype(BF16) for begin in (0, WIDTH)]
    return jnp.concatenate(hits, axis=1)


def placing(offs, head):
    place = position(offs, head, lax.broadcasted_iota(jnp.int32, (1, WIDTH), 1))
    row = lax.broadcasted_iota(jnp.int32, (CHIP, WIDTH), 0)
    return jnp.where(row == place, 1.0, 0.0).astype(BF16)


def side_by_side(parts):
    return jnp.concatenate(parts, axis=1)


def lanes(head):
    return pl.ds(pl.multiple_of(head * WIDTH, WIDTH), WIDTH)


def own_head(step):
    spot = lax.axis_index("ctx") % PLANE
    return spot ^ (2 * step)


def other_head(step):
    return own_head(step) ^ 1


def split_kernel(q, k, v, do, q_in, k_in, v_in, do_in, theirs, sems):
    inside = (q_in, k_in, v_in, do_in)
    copies = [
        pltpu.make_async_copy(ref, to, sems.at[t])
        for t, (ref, to) in enumerate(zip((q, k, v, do), inside))
    ]
    for copy in copies:
        copy.start()
    for t, ref in enumerate(inside):
        copies[t].wait()
        for step in range(CHIPS):
            theirs[step, t] = ref[:, lanes(other_head(step))]


def chip_rows(step, raw, theirs):
    head = own_head(step)
    return [join([ref[:, lanes(head)], theirs[step, t]]) for t, ref in enumerate(raw)]


def maps_kernel(offs_left, picks, places, offs, sem):
    copy = pltpu.make_async_copy(offs_left, offs, sem.at[0])
    copy.start()
    copy.wait()
    for step in range(CHIPS):
        picks[step] = picking(offs, own_head(step))
        places[step] = placing(offs, own_head(step))


def chip_kernel(q, k, v, do, theirs, picks, m0, m1, m2, m3, outs, stats):
    messages = (m0, m1, m2, m3)
    tensors = [chip_rows(step, (q, k, v, do), theirs) for step in range(CHIPS)]
    found = attend(*(rows[:3] for rows in tensors))
    picked = [nn(picks[step], side_by_side(tensors[step])) for step in range(CHIPS)]
    deltas = [dotted(tensors[step][3], found[step][0]) for step in range(CHIPS)]
    for step, message in enumerate(messages):
        for t in range(4):
            rows = picked[step][:, t * WIDTH : (t + 1) * WIDTH]
            message[t * ROWS : (t + 1) * ROWS] = rows.astype(BF16)
    lane = lax.broadcasted_iota(jnp.int32, (1, WIDTH), 1)
    for step, message in enumerate(messages):
        out, total = found[step]
        outs[step] = out
        stats[step, 0] = total
        stats[step, 1] = deltas[step]
        flat = jnp.where(lane & 4 == 0, total, deltas[step]).T[:8]
        flat = nt(join([term.astype(F32) for term in three_terms(flat)]).astype(BF16), picks[step])
        message[BODY:] = join([flat, jnp.zeros((8, WIDTH), F32)]).astype(BF16)


def alone_kernel(places, stats, others):
    for step in range(CHIPS):
        alone = 1.0 - nn(places[step], jnp.ones((ROWS, WIDTH), BF16))
        for i in range(2):
            others[step, i] = stats[step, i] * alone


def tensor(ref, t, rows=ROWS):
    return ref[t * ROWS : t * ROWS + rows]


def group(parts):
    return join(
        [p[:8] for p in parts] + [p[8:16] for p in parts] + [p[16:32] for p in parts]
    )


def ungroup(rows, chip):
    return join(
        [
            rows[8 * chip : 8 * chip + 8],
            rows[32 + 8 * chip : 40 + 8 * chip],
            rows[64 + 16 * chip : 80 + 16 * chip],
        ]
    )


def near_kernel(m0, m1, m2, m3, outs, stats, g, g4):
    refs = (m0, m1, m2, m3)
    stat = [unpack(ref[BODY:]) for ref in refs]
    out = [None] * 4
    blocks = [
        [join([tensor(refs[pair], t), tensor(refs[pair + 1], t)]) for t in range(4)]
        for pair in (0, 2)
    ]
    blocks.append([join([tensor(ref, t, 64) for ref in refs]) for t in range(4)])
    found = attend(*(block[:3] for block in blocks))
    deltas = [dotted(block[3], more) for block, (more, _) in zip(blocks, found)]
    for pair in (0, 2):
        more, total = found[pair // 2]
        joined, _, added = combine(stack(stat[pair : pair + 2]), total, deltas[pair // 2])
        more = more * added
        for chip in range(2):
            out[pair + chip] = more[chip * ROWS : (chip + 1) * ROWS]
            stat[pair + chip] = rows_of(joined, chip * ROWS, (chip + 1) * ROWS)
    more, total = found[2]
    joined, kept, added = combine(stack([rows_of(s, 0, 64) for s in stat]), total, deltas[2])
    more = join([o[:64] for o in out]) * kept + more * added
    for chip in range(4):
        out[chip] = join([more[chip * 64 : (chip + 1) * 64], out[chip][64:]])
        stat[chip] = stack(
            [rows_of(joined, chip * 64, (chip + 1) * 64), rows_of(stat[chip], 64, ROWS)]
        )
        outs[chip] = out[chip]
        stats[chip, 0], stats[chip, 1] = stat[chip]
    for t in range(4):
        rows = group([tensor(ref, t, 32).astype(F32) for ref in refs])
        rows = rows.astype(BF16)
        g[t * ROWS : (t + 1) * ROWS] = rows
        g4[t] = rows[:64]
    g[BODY:] = pack([group([s[i] for s in stat]) for i in range(2)])


def below_kernel(m0, m1, m2, m3, stats, sums):
    refs = (m0, m1, m2, m3)
    stat = [[stats[chip, i] for i in range(2)] for chip in range(4)]
    tensors = [[tensor(ref, t) for t in range(4)] for ref in refs]
    blocks, block_stats = [], []
    for pair in (0, 2):
        k, v = (join([tensors[pair][t], tensors[pair + 1][t]]) for t in (1, 2))
        q, do = (join([tensors[pair][t][32:], tensors[pair + 1][t][32:]]) for t in (0, 3))
        blocks.append((q, k, v, do))
        block_stats.append(stack([rows_of(s, 32, ROWS) for s in stat[pair : pair + 2]]))
    k, v = (join([rows[t][:64] for rows in tensors]) for t in (1, 2))
    q, do = (join([rows[t][32:64] for rows in tensors]) for t in (0, 3))
    blocks.append((q, k, v, do))
    block_stats.append(stack([rows_of(s, 32, 64) for s in stat]))
    found = scored(*products(blocks), block_stats)
    dqs = [nn(score, block[1]) for (_, score), block in zip(found, blocks)]
    dks = [tn(score, block[0]) for (_, score), block in zip(found, blocks)]
    dvs = [tn(chance, block[3]) for (chance, _), block in zip(found, blocks)]
    whole = [
        [
            dqs[chip // 2][chip % 2 * 96 : chip % 2 * 96 + 96],
            dks[chip // 2][chip % 2 * ROWS : chip % 2 * ROWS + ROWS],
            dvs[chip // 2][chip % 2 * ROWS : chip % 2 * ROWS + ROWS],
        ]
        for chip in range(4)
    ]
    parts = dqs[2], dks[2], dvs[2]
    for chip in range(4):
        sums[chip, 0, :32] = jnp.zeros((32, WIDTH), F32)
        sums[chip, 0, 32:64] = whole[chip][0][:32] + parts[0][chip * 32 : (chip + 1) * 32]
        sums[chip, 0, 64:] = whole[chip][0][32:]
        for i in (1, 2):
            sums[chip, i, :64] = whole[chip][i][:64] + parts[i][chip * 64 : (chip + 1) * 64]
            sums[chip, i, 64:] = whole[chip][i][64:]


def pair_kernel(g, a1, out3, stats, message):
    refs = (g, a1)
    q, k, v, do = (join([tensor(ref, t) for ref in refs]) for t in range(4))
    ((more, total),) = attend((q, k, v))
    stat, _, added = combine(stack([unpack(ref[BODY:]) for ref in refs]), total, dotted(do, more))
    out3[...] = more[:ROWS] * added[:ROWS]
    stats[0], stats[1] = stat
    message[...] = flatten(stack([rows_of(stat, 0, 64), rows_of(stat, ROWS, ROWS + 64)]))


def top_kernel(g, a1, a3, a2, top):
    for t in range(4):
        top[0, t] = tensor(g, t, 32)
        top[1, t] = tensor(a1, t, 32)
        top[2, t] = a3[t, :32]
        top[3, t] = a2[t, :32]


def fours(g, a1, a3, a2):
    return [join([tensor(g, t, 64), tensor(a1, t, 64), a3[t], a2[t]]) for t in range(4)]


def quad_kernel(g, a1, a3, a2, out3, stats, message3, out_far, stats_far, message):
    q, k, v, do = fours(g, a1, a3, a2)
    ((more, total),) = attend((q, k, v))
    old = [join([stats[i, :64], stats[i, ROWS : ROWS + 64]]) for i in range(2)]
    old = stack([old, unflatten(message3[...])])
    stat, kept, added = combine(old, total, dotted(do, more))
    out_far[...] = join([out3[:64] * kept[:64] + more[:64] * added[:64], out3[64:]])
    stats_far[0], stats_far[1] = stat
    message[...] = flatten(stack([rows_of(stat, 64 * z, 64 * z + 32) for z in range(4)]))


def rest_kernel(
    m0, m1, m2, m3, outs, stats, below, g, a1, a3, a2, out_far, stats_three, stats_far, far5,
    message5, c0, c1, c2, c3,
):
    refs = (m0, m1, m2, m3)
    own = [tensor(g, t) for t in range(4)]
    three = [join([tensor(g, t), tensor(a1, t)]) for t in range(4)]
    four = fours(g, a1, a3, a2)
    five = [
        join([four[t][64 * z : 64 * z + 32] for z in range(4)] + [far5[z, t] for z in range(4)])
        for t in range(4)
    ]
    blocks = []
    for rows, gathered in ((128, three), (64, four), (32, five)):
        mine = [part[:rows] for part in own]
        blocks.append((mine[0], gathered[1], gathered[2], mine[3]))
        blocks.append((gathered[0], mine[1], mine[2], gathered[3]))
    for pair in (0, 2):
        k, v = (join([tensor(refs[pair], t), tensor(refs[pair + 1], t)]) for t in (1, 2))
        q, do = (join([tensor(refs[pair], t, 32), tensor(refs[pair + 1], t, 32)]) for t in (0, 3))
        blocks.append((q, k, v, do))
    k, v = (join([tensor(ref, t, 64) for ref in refs]) for t in (1, 2))
    q, do = (join([tensor(ref, t, 32) for ref in refs]) for t in (0, 3))
    blocks.append((q, k, v, do))
    ((more, total),) = attend(five[:3])
    scores, grads = products(blocks)
    four_stat = [stats_far[0], stats_far[1]]
    three_stat = [stats_three[0], stats_three[1]]
    old = stack(
        [rows_of(four_stat, 64 * z, 64 * z + 32) for z in range(4)] + [unflatten(message5[...])]
    )
    stat5, kept, added = combine(old, total, dotted(five[3], more))
    stat4 = stack(
        [
            rows
            for z in range(4)
            for rows in (
                rows_of(stat5, 32 * z, 32 * z + 32),
                rows_of(four_stat, 64 * z + 32, 64 * z + 64),
            )
        ]
    )
    stat3 = stack(
        [
            rows
            for z in range(2)
            for rows in (
                rows_of(stat4, 64 * z, 64 * z + 64),
                rows_of(three_stat, ROWS * z + 64, ROWS * z + ROWS),
            )
        ]
    )
    own_stat = rows_of(stat3, 0, ROWS)
    out = join([out_far[:32] * kept[:32] + more[:32] * added[:32], out_far[32:]])
    near = group([stats[chip, 0] for chip in range(4)])
    out = out + group([outs[chip] for chip in range(4)]) * jnp.exp(near - own_stat[0])
    stat = [[ungroup(own_stat[i], chip) for i in range(2)] for chip in range(4)]
    block_stats = []
    for rows, gathered in ((128, stat3), (64, stat4), (32, stat5)):
        block_stats += [rows_of(own_stat, 0, rows), gathered]
    block_stats += [stack(stat[:2]), stack(stat[2:]), stack(stat)]
    found = scored(scores, grads, block_stats)
    dqs = [nn(found[i][1], blocks[i][1]) for i in (0, 2, 4, 6, 7, 8)]
    dks = [tn(found[i][1], blocks[i][0]) for i in (1, 3, 5, 6, 7, 8)]
    dvs = [tn(found[i][0], blocks[i][3]) for i in (1, 3, 5, 6, 7, 8)]
    dq, dk, dv = (
        join([f[:32] + g[:32] + h, f[32:64] + g[32:], f[64:]]) for f, g, h, *_ in (dqs, dks, dvs)
    )
    sums = [
        [
            dqs[3 + chip // 2][chip % 2 * 32 : chip % 2 * 32 + 32],
            dks[3 + chip // 2][chip % 2 * ROWS : chip % 2 * ROWS + ROWS],
            dvs[3 + chip // 2][chip % 2 * ROWS : chip % 2 * ROWS + ROWS],
        ]
        for chip in range(4)
    ]
    parts = dqs[5], dks[5], dvs[5]
    for chip, message in enumerate((c0, c1, c2, c3)):
        message[:ROWS] = join([ungroup(out, chip), outs[chip, 32:]]).astype(BF16)
        rows = sums[chip][0] + parts[0][chip * 32 : (chip + 1) * 32] + ungroup(dq, chip)
        message[ROWS : 2 * ROWS] = join([rows, below[chip, 0, 32:]]).astype(BF16)
        for i, top in ((1, dk), (2, dv)):
            whole = below[chip, i] + sums[chip][i]
            part = parts[i][chip * 64 : (chip + 1) * 64]
            rows = join([whole[:32] + part[:32] + ungroup(top, chip), whole[32:64] + part[32:], whole[64:]])
            message[(i + 1) * ROWS : (i + 2) * ROWS] = rows.astype(BF16)
        message[BODY:] = pack(
            [join([stat[chip][i], stats[chip, i, 32:]]) for i in range(2)]
        )


def finish_kernel(steps, q, k, v, do, theirs, places, outs, stats, others, c0, c1, *refs):
    mine_out, theirs_out = refs[-2:]
    messages = (c0, c1)
    tensors = [chip_rows(step, (q, k, v, do), theirs) for step in steps]
    scores, grads = products(tensors)
    terms = [nt(message[BODY:], places[step]) for step, message in zip(steps, messages)]
    finals = [unflatten(rows[:8] + rows[8:16] + rows[16:24]) for rows in terms]
    stat = [[others[step, i] + final[i] for i in range(2)] for step, final in zip(steps, finals)]
    back = [
        nn(places[step], side_by_side([tensor(message, t) for t in range(4)]))
        for step, message in zip(steps, messages)
    ]
    found = scored(scores, grads, stat)
    own = [
        [outs[step] * jnp.exp(stats[step, 0] - stat[slot][0]) for slot, step in enumerate(steps)],
        [nn(score, rows[1]) for (_, score), rows in zip(found, tensors)],
        [tn(score, rows[0]) for (_, score), rows in zip(found, tensors)],
        [tn(chance, rows[3]) for (chance, _), rows in zip(found, tensors)],
    ]
    for slot in range(2):
        for t in range(4):
            rows = own[t][slot] + back[slot][:, t * WIDTH : (t + 1) * WIDTH]
            mine_out[slot, t] = rows[:ROWS].astype(BF16)
            theirs_out[slot, t] = rows[ROWS:].astype(BF16)


def place_kernel(mine0, mine1, theirs0, theirs1, att, dq, dk, dv, rows, sems):
    copies = [
        pltpu.make_async_copy(rows.at[t], ref, sems.at[t])
        for t, ref in enumerate((att, dq, dk, dv))
    ]
    for t in range(4):
        for step in range(CHIPS):
            mine, theirs = ((mine0, theirs0), (mine1, theirs1))[step // 2]
            rows[t, :, lanes(own_head(step))] = mine[step % 2, t]
            rows[t, :, lanes(other_head(step))] = theirs[step % 2, t]
        copies[t].start()
    for copy in copies:
        copy.wait()


VMEM = pl.BlockSpec(memory_space=pltpu.VMEM)
LEFT = pl.BlockSpec(memory_space=pltpu.HBM)


def call(kernel, name, outs, *args, left=0, scratch=(), out_specs=None):
    stay = [pltpu.with_memory_space_constraint(arg, pltpu.HBM) for arg in args[:left]]
    args = (*stay, *args[left:])
    return pl.pallas_call(
        kernel,
        name=name,
        out_shape=tuple(jax.ShapeDtypeStruct(shape, dtype) for shape, dtype in outs),
        in_specs=[LEFT] * left + [VMEM] * (len(args) - left),
        out_specs=out_specs or (VMEM,) * len(outs),
        scratch_shapes=scratch,
        compiler_params=pltpu.CompilerParams(vmem_limit_bytes=40 * 2**20),
    )(*args)


def in_plane(array, flip):
    moves = [(PLANE * z + i, PLANE * z + (i ^ flip)) for z in range(DEPTH) for i in range(PLANE)]
    return lax.ppermute(array, "ctx", moves)


def across(array, flip):
    moves = [(PLANE * z + i, PLANE * (z ^ flip) + i) for z in range(DEPTH) for i in range(PLANE)]
    return lax.ppermute(array, "ctx", moves)


def shards(queries, keys, values, out_grad, offsets):
    whole = ((ROWS, HEADS * WIDTH), BF16)
    half = ((CHIPS, 4, ROWS, WIDTH), BF16)
    pairs = ((2, 4, ROWS, WIDTH), BF16)
    message = ((MESSAGE, WIDTH), BF16)
    flat = ((8, WIDTH), F32)
    rows = ((ROWS, WIDTH), F32)
    quads = ((4, ROWS, WIDTH), F32)
    quad_stats = ((4, 2, ROWS, WIDTH), F32)
    chips = ((CHIPS, CHIP, WIDTH), F32)
    chip_stats = ((CHIPS, 2, CHIP, WIDTH), F32)
    seg_stats = ((2, SEG, WIDTH), F32)
    *raw, theirs = call(
        split_kernel, "split", [whole] * 4 + [half], queries, keys, values, out_grad,
        left=4, scratch=[pltpu.SemaphoreType.DMA((4,))],
    )
    theirs = in_plane(theirs, 1)
    picks, places = call(
        maps_kernel, "maps", [((CHIPS, ROWS, CHIP), BF16), ((CHIPS, CHIP, ROWS), BF16)], offsets,
        left=1, scratch=[pltpu.SMEM((6, HEADS), jnp.int32), pltpu.SemaphoreType.DMA((1,))],
    )
    *sent, outs0, stats0 = call(
        chip_kernel, "chip", [message] * 4 + [chips, chip_stats], *raw, theirs, picks
    )
    (others,) = call(alone_kernel, "alone", [chip_stats], places, stats0)
    got = [sent[0]] + [in_plane(sent[step], 2 * step) for step in (1, 2, 3)]
    outs, stats, g, g4 = call(
        near_kernel, "near", [quads, quad_stats, message, ((4, 64, WIDTH), BF16)], *got
    )
    (below,) = call(below_kernel, "below", [((4, 3, ROWS, WIDTH), F32)], *got, stats)
    a1 = across(g, 1)
    a3 = across(g4, 3)
    a2 = across(g4, 2)
    out3, stats3, message3 = call(
        pair_kernel, "pair", [rows, seg_stats, flat], g, a1
    )
    a3, a2, message3 = lax.optimization_barrier((a3, a2, across(message3, 3)))
    fars = (g, a1, a3, a2)
    (top,) = call(top_kernel, "top", [((4, 4, 32, WIDTH), BF16)], *fars)
    top = across(top, 7)
    out_far, stats_far, message5 = call(
        quad_kernel, "quad", [rows, seg_stats, flat], *fars, out3, stats3, message3
    )
    message5 = across(message5, 7)
    back = call(
        rest_kernel, "rest", [message] * 4,
        *got, outs, stats, below, *fars, out_far, stats3, stats_far, top, message5,
    )
    back = [back[0]] + [in_plane(back[step], 2 * step) for step in (1, 2, 3)]
    halves, after = [], ()
    for steps in ((0, 1), (2, 3)):
        mine, other = call(
            functools.partial(finish_kernel, steps), "finish", [pairs, pairs],
            *raw, theirs, places, outs0, stats0, others, *(back[step] for step in steps), *after,
        )
        after = (mine,)
        halves.append((mine, in_plane(other, 1)))
    (mine0, theirs0), (mine1, theirs1) = halves
    return call(
        place_kernel, "place", [whole] * 4, mine0, mine1, theirs0, theirs1, out_specs=(LEFT,) * 4,
        scratch=[pltpu.VMEM((4, ROWS, HEADS * WIDTH), BF16), pltpu.SemaphoreType.DMA((4,))],
    )


def solution(mesh):
    rows = P(("dp", "ctx"), None)
    return jax.shard_map(
        shards,
        mesh=mesh,
        in_specs=(rows,) * 4 + (P("dp", None),),
        out_specs=(rows,) * 4,
        check_vma=False,
    )
```

time: 65.5 us -> 58.1 us (0.89)
  Pallas kernels: 14.9 us -> 10.7 us
  waiting for transfers between devices: 19.2 us -> 16 us
    pallas_call x9 -> x13, Pallas kernels: 14.9 us -> 10.7 us  [call(): pl.pallas_call(kernel, name=name, out_shape=tuple((jax.ShapeDtypeStruct(s...]
    ppermute x8 -> x9, waiting for transfers between devices: 13.5 us -> 11.3 us  [in_plane(): return lax.ppermute(array, 'ctx', moves)]
    ppermute x6, waiting for transfers between devices: 5.7 us -> 4.69 us  [across(): return lax.ppermute(array, 'ctx', moves)]
    ppermute x8 -> x9, starting transfers between devices: 17.1 us -> 17.3 us  [in_plane(): return lax.ppermute(array, 'ctx', moves)]
  transfers between devices with their start and end apart: 14 -> 15, of which waited for: 9 -> 11; matrix products, arithmetic and copies ran while one was open for 0% -> 0% of each run, Pallas kernels for 2% -> 7%
where the time goes in v3:
time: 58.1 us; the launch traced here: 58 us
  starting transfers between devices  30.4 us (52%)
  waiting for transfers between devices  16 us (28%)
  Pallas kernels  10.7 us (18%)
  between operations  0.88 us (2%)
    ppermute x9, starting transfers between devices, in_plane(): return lax.ppermute(array, 'ctx', moves)  17.3 us
    ppermute x6, starting transfers between devices, across(): return lax.ppermute(array, 'ctx', moves)  13.1 us
    ppermute x9, waiting for transfers between devices, in_plane(): return lax.ppermute(array, 'ctx', moves)  11.3 us
    pallas_call x13, Pallas kernels, call(): pl.pallas_call(kernel, name=name, out_shape=tuple((jax.ShapeDtypeStruct(s...  10.7 us
    ppermute x6, waiting for transfers between devices, across(): return lax.ppermute(array, 'ctx', moves)  4.69 us
  transfers between devices with their start and end apart: 15, of which 11 were waited for; matrix products, arithmetic and copies ran while one was open for 0% of the time, Pallas kernels for 7%

profile of v3, /device:TPU:1, one launch (start us, length us, event | category | flops | bytes accessed | tf_op | source)
XLA Modules:
  0.0 58.0 jit_solution(18075286688045176037)
XLA Ops:
  0.6 1.3 %split.1 = (bf16[128,1024]{1,0:T(8,128)(2,1)S(1)}, bf16[128,1024]{1,0:T(8,128)(2,1)S(1)}, bf16[128,1024]{1,0:T(8,128)(2,1)S(1)}, bf16[128,1024]{1,0:T(8,128)(2,1)S(1)}, bf16[4,4,128,128]{3,2,1,0:T(8,128)(2,1)S(1)}) custom-call(bf16[128,1024]{1,0:T(8,128)(2,1)} %q.1, bf16[128,1024]{1,0:T(8,128)(2,1)} %k.1, bf16[128,1024]{1,0:T(8,128)(2,1)} %v.1, ...), custom_call_target="tpu_custom_call" | custom-call | tf_op jit(solution)/shard_map/split/pallas_call | solution.py:484
  1.9 3.3 %collective-permute-start = (bf16[4,4,128,128]{3,2,1,0:T(8,128)(2,1)S(1)}, bf16[4,4,128,128]{3,2,1,0:T(8,128)(2,1)S(1)}, u32[]{:S(2)}, u32[]{:S(2)}) collective-permute-start(bf16[4,4,128,128]{3,2,1,0:T(8,128)(2,1)S(1)} %get-tuple-element.42), channel_id=1, source_target_pairs={{0,1},{1,0},{2,3},{3,2},{4,5},{5,4},{6,7},{7,6},{8,9},{9,8},{10,11... | collective-permute-start | bytes 1572872 | tf_op jit(solution)/shard_map/ppermute | solution.py:497
  5.2 0.8 %maps.1 = (bf16[4,128,256]{2,1,0:T(8,128)(2,1)S(1)}, bf16[4,256,128]{2,1,0:T(8,128)(2,1)S(1)}) custom-call(s32[6,8]{1,0:T(8,128)} %offs_left.1), custom_call_target="tpu_custom_call" | custom-call | tf_op jit(solution)/shard_map/maps/pallas_call | solution.py:484
  6.1 0.7 %collective-permute-done.theirs = bf16[4,4,128,128]{3,2,1,0:T(8,128)(2,1)S(1)} collective-permute-done((bf16[4,4,128,128]{3,2,1,0:T(8,128)(2,1)S(1)}, bf16[4,4,128,128]{3,2,1,0:T(8,128)(2,1)S(1)}, u32[]{:S(2)}, u32[]{:S(2)}) %collective-permute-start) | collective-permute-done | bytes 524320 | tf_op jit(solution)/shard_map/ppermute | solution.py:497
  6.8 1.1 %chip.1 = (bf16[544,128]{1,0:T(8,128)(2,1)S(1)}, bf16[544,128]{1,0:T(8,128)(2,1)S(1)}, bf16[544,128]{1,0:T(8,128)(2,1)S(1)}, bf16[544,128]{1,0:T(8,128)(2,1)S(1)...) custom-call(bf16[128,1024]{1,0:T(8,128)(2,1)S(1)} %get-tuple-element.38.q, ...), custom_call_target="tpu_custom_call" | custom-call | tf_op jit(solution)/shard_map/chip/pallas_call | solution.py:484
  7.9 0.1 collective-permute-start.1
  8.0 2.2 %collective-permute-start.2 = (bf16[544,128]{1,0:T(8,128)(2,1)S(1)}, bf16[544,128]{1,0:T(8,128)(2,1)S(1)}, u32[]{:S(2)}, u32[]{:S(2)}) collective-permute-start(bf16[544,128]{1,0:T(8,128)(2,1)S(1)} %get-tuple-element.49), channel_id=1, source_target_pairs={{0,4},{1,5},{2,6},{3,7},{4,0},{5,1},{6,2},{7,3},{8,12},{9,13},{10,... | collective-permute-start | bytes 417800 | tf_op jit(solution)/shard_map/ppermute | solution.py:497
  10.1 1.7 %collective-permute-start.3 = (bf16[544,128]{1,0:T(8,128)(2,1)S(1)}, bf16[544,128]{1,0:T(8,128)(2,1)S(1)}, u32[]{:S(2)}, u32[]{:S(2)}) collective-permute-start(bf16[544,128]{1,0:T(8,128)(2,1)S(1)} %get-tuple-element.50), channel_id=1, source_target_pairs={{0,6},{1,7},{2,4},{3,5},{4,2},{5,3},{6,0},{7,1},{8,14},{9,15},{10,... | collective-permute-start | bytes 417800 | tf_op jit(solution)/shard_map/ppermute | solution.py:497
  11.8 1.0 %collective-permute-done.1.m1 = bf16[544,128]{1,0:T(8,128)(2,1)S(1)} collective-permute-done((bf16[544,128]{1,0:T(8,128)(2,1)S(1)}, bf16[544,128]{1,0:T(8,128)(2,1)S(1)}, u32[]{:S(2)}, u32[]{:S(2)}) %collective-permute-start.1) | collective-permute-done | bytes 139296 | tf_op jit(solution)/shard_map/ppermute | solution.py:497
  12.8 3.7 %collective-permute-done.2.m2 = bf16[544,128]{1,0:T(8,128)(2,1)S(1)} collective-permute-done((bf16[544,128]{1,0:T(8,128)(2,1)S(1)}, bf16[544,128]{1,0:T(8,128)(2,1)S(1)}, u32[]{:S(2)}, u32[]{:S(2)}) %collective-permute-start.2) | collective-permute-done | bytes 139296 | tf_op jit(solution)/shard_map/ppermute | solution.py:497
  16.6 2.5 %collective-permute-done.3.m3 = bf16[544,128]{1,0:T(8,128)(2,1)S(1)} collective-permute-done((bf16[544,128]{1,0:T(8,128)(2,1)S(1)}, bf16[544,128]{1,0:T(8,128)(2,1)S(1)}, u32[]{:S(2)}, u32[]{:S(2)}) %collective-permute-start.3) | collective-permute-done | bytes 139296 | tf_op jit(solution)/shard_map/ppermute | solution.py:497
  19.1 1.0 %near.1 = (f32[4,128,128]{2,1,0:T(8,128)S(1)}, f32[4,2,128,128]{3,2,1,0:T(8,128)S(1)}, bf16[544,128]{1,0:T(8,128)(2,1)S(1)}, bf16[4,64,128]{2,1,0:T(8,128)(2,1)S(1)}) custom-call(bf16[544,128]{1,0:T(8,128)(2,1)S(1)} %get-tuple-element.47.m0, bf16[544,128]{1,0:T(8,128)(2,1)S(1)} %collective-permute-done.1.m1, bf16[544,128]{1,0:T(8,128)(2,1)S(1)} %collective-permute-done.2.m2, ...), custom_call_target="tpu_custom_call" | custom-call | tf_op jit(solution)/shard_map/near/pallas_call | solution.py:484
  20.0 1.7 %collective-permute-start.4 = (bf16[544,128]{1,0:T(8,128)(2,1)S(1)}, bf16[544,128]{1,0:T(8,128)(2,1)S(1)}, u32[]{:S(2)}, u32[]{:S(2)}) collective-permute-start(bf16[544,128]{1,0:T(8,128)(2,1)S(1)} %get-tuple-element.53.g), channel_id=1, source_target_pairs={{0,8},{1,9},{2,10},{3,11},{4,12},{5,13},{6,14},{7,15},{8,0},{9,1},... | collective-permute-start | bytes 417800 | tf_op jit(solution)/shard_map/ppermute | solution.py:502
  21.7 3.0 %collective-permute-start.6 = (bf16[4,64,128]{2,1,0:T(8,128)(2,1)S(1)}, bf16[4,64,128]{2,1,0:T(8,128)(2,1)S(1)}, u32[]{:S(2)}, u32[]{:S(2)}) collective-permute-start(bf16[4,64,128]{2,1,0:T(8,128)(2,1)S(1)} %get-tuple-element.54), channel_id=1, source_target_pairs={{0,16},{1,17},{2,18},{3,19},{4,20},{5,21},{6,22},{7,23},{8,24},{9,... | collective-permute-start | bytes 196616 | tf_op jit(solution)/shard_map/ppermute | solution.py:502
  24.7 0.0 collective-permute-start.5
  24.7 0.0 collective-permute-done.4.a1
  24.7 0.6 %pair.1 = (f32[128,128]{1,0:T(8,128)S(1)}, f32[2,256,128]{2,1,0:T(8,128)S(1)}, f32[8,128]{1,0:T(8,128)S(1)}) custom-call(bf16[544,128]{1,0:T(8,128)(2,1)S(1)} %get-tuple-element.53.g, bf16[544,128]{1,0:T(8,128)(2,1)S(1)} %collective-permute-done.4.a1), custom_call_target="tpu_custom_call" | custom-call | tf_op jit(solution)/shard_map/pair/pallas_call | solution.py:484
  25.4 5.0 %collective-permute-start.7 = (f32[8,128]{1,0:T(8,128)S(1)}, f32[8,128]{1,0:T(8,128)S(1)}, u32[]{:S(2)}, u32[]{:S(2)}) collective-permute-start(f32[8,128]{1,0:T(8,128)S(1)} %get-tuple-element.55), channel_id=1, source_target_pairs={{0,24},{1,25},{2,26},{3,27},{4,28},{5,29},{6,30},{7,31},{8,16},{9,... | collective-permute-start | bytes 12296 | tf_op jit(solution)/shard_map/ppermute | solution.py:502
  30.4 0.0 collective-permute-done.6.a2
  30.4 0.1 collective-permute-done.5.a3
  30.5 1.2 %collective-permute-done.7.message3 = f32[8,128]{1,0:T(8,128)S(1)} collective-permute-done((f32[8,128]{1,0:T(8,128)S(1)}, f32[8,128]{1,0:T(8,128)S(1)}, u32[]{:S(2)}, u32[]{:S(2)}) %collective-permute-start.7) | collective-permute-done | bytes 4128 | tf_op jit(solution)/shard_map/ppermute | solution.py:502
  31.7 3.3 %collective-permute-start.8 = (bf16[4,4,32,128]{3,2,1,0:T(8,128)(2,1)S(1)}, bf16[4,4,32,128]{3,2,1,0:T(8,128)(2,1)S(1)}, u32[]{:S(2)}, u32[]{:S(2)}) collective-permute-start(bf16[4,4,32,128]{3,2,1,0:T(8,128)(2,1)S(1)} %top.1), channel_id=1, source_target_pairs={{0,56},{1,57},{2,58},{3,59},{4,60},{5,61},{6,62},{7,63},{8,48},{9,... | collective-permute-start | bytes 393224 | tf_op jit(solution)/shard_map/ppermute | solution.py:502
  35.0 0.6 %quad.1 = (f32[128,128]{1,0:T(8,128)S(1)}, f32[2,256,128]{2,1,0:T(8,128)S(1)}, f32[8,128]{1,0:T(8,128)S(1)}) custom-call(bf16[544,128]{1,0:T(8,128)(2,1)S(1)} %get-tuple-element.53.g, bf16[544,128]{1,0:T(8,128)(2,1)S(1)} %collective-permute-done.4.a1, bf16[4,64,128]{2,1,0:T(8,128)(2,1)S(1)} %collective-permute-done.5.a3, ...), custom_call_target="tpu_custom_call" | custom-call | tf_op jit(solution)/shard_map/quad/pallas_call | solution.py:484
  35.7 0.1 collective-permute-start.9
  35.8 0.7 %below.1 = f32[4,3,128,128]{3,2,1,0:T(8,128)S(1)} custom-call(bf16[544,128]{1,0:T(8,128)(2,1)S(1)} %get-tuple-element.47.m0, bf16[544,128]{1,0:T(8,128)(2,1)S(1)} %collective-permute-done.1.m1, bf16[544,128]{1,0:T(8,128)(2,1)S(1)} %collective-permute-done.2.m2, bf16[544,128]{1,0:T(8,128)(2,1)S(1)} %collective-permute-done.3.m3, ...), custom_call_target="tpu_custom_call" | custom-call | tf_op jit(solution)/shard_map/below/pallas_call | solution.py:484
  36.5 3.4 %collective-permute-done.9.message5 = f32[8,128]{1,0:T(8,128)S(1)} collective-permute-done((f32[8,128]{1,0:T(8,128)S(1)}, f32[8,128]{1,0:T(8,128)S(1)}, u32[]{:S(2)}, u32[]{:S(2)}) %collective-permute-start.9) | collective-permute-done | bytes 4128 | tf_op jit(solution)/shard_map/ppermute | solution.py:502
  39.8 0.0 collective-permute-done.8.far5
  39.8 1.3 %rest.1 = (bf16[544,128]{1,0:T(8,128)(2,1)S(1)}, bf16[544,128]{1,0:T(8,128)(2,1)S(1)}, bf16[544,128]{1,0:T(8,128)(2,1)S(1)}, bf16[544,128]{1,0:T(8,128)(2,1)S(1)}) custom-call(bf16[544,128]{1,0:T(8,128)(2,1)S(1)} %get-tuple-element.47.m0, bf16[544,128]{1,0:T(8,128)(2,1)S(1)} %collective-permute-done.1.m1, bf16[544,128]{1,0:T(8,128)(2,1)S(1)} %collective-permute-done.2.m2, ...), custom_call_target="tpu_custom_call" | custom-call | tf_op jit(solution)/shard_map/rest/pallas_call | solution.py:484
  41.1 0.1 collective-permute-start.10
  41.2 1.4 %collective-permute-start.11 = (bf16[544,128]{1,0:T(8,128)(2,1)S(1)}, bf16[544,128]{1,0:T(8,128)(2,1)S(1)}, u32[]{:S(2)}, u32[]{:S(2)}) collective-permute-start(bf16[544,128]{1,0:T(8,128)(2,1)S(1)} %get-tuple-element.67), channel_id=1, source_target_pairs={{0,4},{1,5},{2,6},{3,7},{4,0},{5,1},{6,2},{7,3},{8,12},{9,13},{10,... | collective-permute-start | bytes 417800 | tf_op jit(solution)/shard_map/ppermute | solution.py:497
  42.6 2.5 %collective-permute-start.12 = (bf16[544,128]{1,0:T(8,128)(2,1)S(1)}, bf16[544,128]{1,0:T(8,128)(2,1)S(1)}, u32[]{:S(2)}, u32[]{:S(2)}) collective-permute-start(bf16[544,128]{1,0:T(8,128)(2,1)S(1)} %get-tuple-element.68), channel_id=1, source_target_pairs={{0,6},{1,7},{2,4},{3,5},{4,2},{5,3},{6,0},{7,1},{8,14},{9,15},{10,... | collective-permute-start | bytes 417800 | tf_op jit(solution)/shard_map/ppermute | solution.py:497
  45.1 0.2 alone.1.others
  45.3 0.0 collective-permute-done.10.c1
  45.3 1.0 %finish.2 = (bf16[2,4,128,128]{3,2,1,0:T(8,128)(2,1)S(1)}, bf16[2,4,128,128]{3,2,1,0:T(8,128)(2,1)S(1)}) custom-call(bf16[128,1024]{1,0:T(8,128)(2,1)S(1)} %get-tuple-element.38.q, bf16[128,1024]{1,0:T(8,128)(2,1)S(1)} %get-tuple-element.39.k, bf16[128,1024]{1,0:T(8,128)(2,1)S(1)} %get-tuple-element.40.v, bf16[128,1024]{1,0:T(8,128)(2,1)S(1)} %get-tuple-element.41.do, ...), custom_call_target="tpu_custom_call" | custom-call | tf_op jit(solution)/shard_map/finish/pallas_call | solution.py:484
  46.3 0.5 collective-permute-done.11.c0
  46.8 1.4 %collective-permute-done.12.c1 = bf16[544,128]{1,0:T(8,128)(2,1)S(1)} collective-permute-done((bf16[544,128]{1,0:T(8,128)(2,1)S(1)}, bf16[544,128]{1,0:T(8,128)(2,1)S(1)}, u32[]{:S(2)}, u32[]{:S(2)}) %collective-permute-start.12) | collective-permute-done | bytes 139296 | tf_op jit(solution)/shard_map/ppermute | solution.py:497
  48.2 1.0 %finish.3 = (bf16[2,4,128,128]{3,2,1,0:T(8,128)(2,1)S(1)}, bf16[2,4,128,128]{3,2,1,0:T(8,128)(2,1)S(1)}) custom-call(bf16[128,1024]{1,0:T(8,128)(2,1)S(1)} %get-tuple-element.38.q, bf16[128,1024]{1,0:T(8,128)(2,1)S(1)} %get-tuple-element.39.k, bf16[128,1024]{1,0:T(8,128)(2,1)S(1)} %get-tuple-element.40.v, bf16[128,1024]{1,0:T(8,128)(2,1)S(1)} %get-tuple-element.41.do, ...), custom_call_target="tpu_custom_call" | custom-call | tf_op jit(solution)/shard_map/finish/pallas_call | solution.py:484
  49.2 6.1 %collective-permute-start.14 = (bf16[2,4,128,128]{3,2,1,0:T(8,128)(2,1)S(1)}, bf16[2,4,128,128]{3,2,1,0:T(8,128)(2,1)S(1)}, u32[]{:S(2)}, u32[]{:S(2)}) collective-permute-start(bf16[2,4,128,128]{3,2,1,0:T(8,128)(2,1)S(1)} %get-tuple-element.71), channel_id=1, source_target_pairs={{0,1},{1,0},{2,3},{3,2},{4,5},{5,4},{6,7},{7,6},{8,9},{9,8},{10,11... | collective-permute-start | bytes 786440 | tf_op jit(solution)/shard_map/ppermute | solution.py:497
  55.2 0.1 collective-permute-start.13
  55.3 1.1 %collective-permute-done.14.theirs1 = bf16[2,4,128,128]{3,2,1,0:T(8,128)(2,1)S(1)} collective-permute-done((bf16[2,4,128,128]{3,2,1,0:T(8,128)(2,1)S(1)}, bf16[2,4,128,128]{3,2,1,0:T(8,128)(2,1)S(1)}, u32[]{:S(2)}, u32[]{:S(2)}) %collective-permute-start.14) | collective-permute-done | bytes 262176 | tf_op jit(solution)/shard_map/ppermute | solution.py:497
  56.4 0.4 collective-permute-done.13.theirs0
  56.8 1.1 %place.1 = (bf16[128,1024]{1,0:T(8,128)(2,1)}, bf16[128,1024]{1,0:T(8,128)(2,1)}, bf16[128,1024]{1,0:T(8,128)(2,1)}, bf16[128,1024]{1,0:T(8,128)(2,1)}) custom-call(bf16[2,4,128,128]{3,2,1,0:T(8,128)(2,1)S(1)} %get-tuple-element.66.refs_0_.mine0, bf16[2,4,128,128]{3,2,1,0:T(8,128)(2,1)S(1)} %get-tuple-element.69.mine1, ...), custom_call_target="tpu_custom_call" | custom-call | tf_op jit(solution)/shard_map/place/pallas_call | solution.py:484
  (1 shorter events, 0.0 us)
Async XLA Ops:
  1.9 4.9 %collective-permute-start = (bf16[4,4,128,128]{3,2,1,0:T(8,128)(2,1)S(1)}, bf16[4,4,128,128]{3,2,1,0:T(8,128)(2,1)S(1)}, u32[]{:S(2)}, u32[]{:S(2)}) collective-permute-start(bf16[4,4,128,128]{3,2,1,0:T(8,128)(2,1)S(1)} %get-tuple-element.42), channel_id=1, source_target_pairs={{0,1},{1,0},{2,3},{3,2},{4,5},{5,4},{6,7},{7,6},{8,9},{9,8},{10,11... | collective-permute-start | bytes 1572872 | tf_op jit(solution)/shard_map/ppermute | solution.py:497
  7.9 4.9 %collective-permute-start.1 = (bf16[544,128]{1,0:T(8,128)(2,1)S(1)}, bf16[544,128]{1,0:T(8,128)(2,1)S(1)}, u32[]{:S(2)}, u32[]{:S(2)}) collective-permute-start(bf16[544,128]{1,0:T(8,128)(2,1)S(1)} %get-tuple-element.48), channel_id=1, source_target_pairs={{0,2},{1,3},{2,0},{3,1},{4,6},{5,7},{6,4},{7,5},{8,10},{9,11},{10,... | collective-permute-start | bytes 417800 | tf_op jit(solution)/shard_map/ppermute | solution.py:497
  8.0 8.6 %collective-permute-start.2 = (bf16[544,128]{1,0:T(8,128)(2,1)S(1)}, bf16[544,128]{1,0:T(8,128)(2,1)S(1)}, u32[]{:S(2)}, u32[]{:S(2)}) collective-permute-start(bf16[544,128]{1,0:T(8,128)(2,1)S(1)} %get-tuple-element.49), channel_id=1, source_target_pairs={{0,4},{1,5},{2,6},{3,7},{4,0},{5,1},{6,2},{7,3},{8,12},{9,13},{10,... | collective-permute-start | bytes 417800 | tf_op jit(solution)/shard_map/ppermute | solution.py:497
  10.1 8.9 %collective-permute-start.3 = (bf16[544,128]{1,0:T(8,128)(2,1)S(1)}, bf16[544,128]{1,0:T(8,128)(2,1)S(1)}, u32[]{:S(2)}, u32[]{:S(2)}) collective-permute-start(bf16[544,128]{1,0:T(8,128)(2,1)S(1)} %get-tuple-element.50), channel_id=1, source_target_pairs={{0,6},{1,7},{2,4},{3,5},{4,2},{5,3},{6,0},{7,1},{8,14},{9,15},{10,... | collective-permute-start | bytes 417800 | tf_op jit(solution)/shard_map/ppermute | solution.py:497
  20.0 4.7 %collective-permute-start.4 = (bf16[544,128]{1,0:T(8,128)(2,1)S(1)}, bf16[544,128]{1,0:T(8,128)(2,1)S(1)}, u32[]{:S(2)}, u32[]{:S(2)}) collective-permute-start(bf16[544,128]{1,0:T(8,128)(2,1)S(1)} %get-tuple-element.53.g), channel_id=1, source_target_pairs={{0,8},{1,9},{2,10},{3,11},{4,12},{5,13},{6,14},{7,15},{8,0},{9,1},... | collective-permute-start | bytes 417800 | tf_op jit(solution)/shard_map/ppermute | solution.py:502
  21.7 8.6 %collective-permute-start.6 = (bf16[4,64,128]{2,1,0:T(8,128)(2,1)S(1)}, bf16[4,64,128]{2,1,0:T(8,128)(2,1)S(1)}, u32[]{:S(2)}, u32[]{:S(2)}) collective-permute-start(bf16[4,64,128]{2,1,0:T(8,128)(2,1)S(1)} %get-tuple-element.54), channel_id=1, source_target_pairs={{0,16},{1,17},{2,18},{3,19},{4,20},{5,21},{6,22},{7,23},{8,24},{9,... | collective-permute-start | bytes 196616 | tf_op jit(solution)/shard_map/ppermute | solution.py:502
  24.7 5.8 %collective-permute-start.5 = (bf16[4,64,128]{2,1,0:T(8,128)(2,1)S(1)}, bf16[4,64,128]{2,1,0:T(8,128)(2,1)S(1)}, u32[]{:S(2)}, u32[]{:S(2)}) collective-permute-start(bf16[4,64,128]{2,1,0:T(8,128)(2,1)S(1)} %get-tuple-element.54), channel_id=1, source_target_pairs={{0,24},{1,25},{2,26},{3,27},{4,28},{5,29},{6,30},{7,31},{8,16},{9,... | collective-permute-start | bytes 196616 | tf_op jit(solution)/shard_map/ppermute | solution.py:502
  25.4 6.3 %collective-permute-start.7 = (f32[8,128]{1,0:T(8,128)S(1)}, f32[8,128]{1,0:T(8,128)S(1)}, u32[]{:S(2)}, u32[]{:S(2)}) collective-permute-start(f32[8,128]{1,0:T(8,128)S(1)} %get-tuple-element.55), channel_id=1, source_target_pairs={{0,24},{1,25},{2,26},{3,27},{4,28},{5,29},{6,30},{7,31},{8,16},{9,... | collective-permute-start | bytes 12296 | tf_op jit(solution)/shard_map/ppermute | solution.py:502
  31.7 8.1 %collective-permute-start.8 = (bf16[4,4,32,128]{3,2,1,0:T(8,128)(2,1)S(1)}, bf16[4,4,32,128]{3,2,1,0:T(8,128)(2,1)S(1)}, u32[]{:S(2)}, u32[]{:S(2)}) collective-permute-start(bf16[4,4,32,128]{3,2,1,0:T(8,128)(2,1)S(1)} %top.1), channel_id=1, source_target_pairs={{0,56},{1,57},{2,58},{3,59},{4,60},{5,61},{6,62},{7,63},{8,48},{9,... | collective-permute-start | bytes 393224 | tf_op jit(solution)/shard_map/ppermute | solution.py:502
  35.7 4.1 %collective-permute-start.9 = (f32[8,128]{1,0:T(8,128)S(1)}, f32[8,128]{1,0:T(8,128)S(1)}, u32[]{:S(2)}, u32[]{:S(2)}) collective-permute-start(f32[8,128]{1,0:T(8,128)S(1)} %get-tuple-element.63), channel_id=1, source_target_pairs={{0,56},{1,57},{2,58},{3,59},{4,60},{5,61},{6,62},{7,63},{8,48},{9,... | collective-permute-start | bytes 12296 | tf_op jit(solution)/shard_map/ppermute | solution.py:502
  41.1 4.2 %collective-permute-start.10 = (bf16[544,128]{1,0:T(8,128)(2,1)S(1)}, bf16[544,128]{1,0:T(8,128)(2,1)S(1)}, u32[]{:S(2)}, u32[]{:S(2)}) collective-permute-start(bf16[544,128]{1,0:T(8,128)(2,1)S(1)} %get-tuple-element.65), channel_id=1, source_target_pairs={{0,2},{1,3},{2,0},{3,1},{4,6},{5,7},{6,4},{7,5},{8,10},{9,11},{10,... | collective-permute-start | bytes 417800 | tf_op jit(solution)/shard_map/ppermute | solution.py:497
  41.2 5.6 %collective-permute-start.11 = (bf16[544,128]{1,0:T(8,128)(2,1)S(1)}, bf16[544,128]{1,0:T(8,128)(2,1)S(1)}, u32[]{:S(2)}, u32[]{:S(2)}) collective-permute-start(bf16[544,128]{1,0:T(8,128)(2,1)S(1)} %get-tuple-element.67), channel_id=1, source_target_pairs={{0,4},{1,5},{2,6},{3,7},{4,0},{5,1},{6,2},{7,3},{8,12},{9,13},{10,... | collective-permute-start | bytes 417800 | tf_op jit(solution)/shard_map/ppermute | solution.py:497
  42.6 5.6 %collective-permute-start.12 = (bf16[544,128]{1,0:T(8,128)(2,1)S(1)}, bf16[544,128]{1,0:T(8,128)(2,1)S(1)}, u32[]{:S(2)}, u32[]{:S(2)}) collective-permute-start(bf16[544,128]{1,0:T(8,128)(2,1)S(1)} %get-tuple-element.68), channel_id=1, source_target_pairs={{0,6},{1,7},{2,4},{3,5},{4,2},{5,3},{6,0},{7,1},{8,14},{9,15},{10,... | collective-permute-start | bytes 417800 | tf_op jit(solution)/shard_map/ppermute | solution.py:497
  49.2 7.2 %collective-permute-start.14 = (bf16[2,4,128,128]{3,2,1,0:T(8,128)(2,1)S(1)}, bf16[2,4,128,128]{3,2,1,0:T(8,128)(2,1)S(1)}, u32[]{:S(2)}, u32[]{:S(2)}) collective-permute-start(bf16[2,4,128,128]{3,2,1,0:T(8,128)(2,1)S(1)} %get-tuple-element.71), channel_id=1, source_target_pairs={{0,1},{1,0},{2,3},{3,2},{4,5},{5,4},{6,7},{7,6},{8,9},{9,8},{10,11... | collective-permute-start | bytes 786440 | tf_op jit(solution)/shard_map/ppermute | solution.py:497
  55.2 1.5 %collective-permute-start.13 = (bf16[2,4,128,128]{3,2,1,0:T(8,128)(2,1)S(1)}, bf16[2,4,128,128]{3,2,1,0:T(8,128)(2,1)S(1)}, u32[]{:S(2)}, u32[]{:S(2)}) collective-permute-start(bf16[2,4,128,128]{3,2,1,0:T(8,128)(2,1)S(1)} %get-tuple-element.70), channel_id=1, source_target_pairs={{0,1},{1,0},{2,3},{3,2},{4,5},{5,4},{6,7},{7,6},{8,9},{9,8},{10,11... | collective-permute-start | bytes 786440 | tf_op jit(solution)/shard_map/ppermute | solution.py:497

commit v4 on v3

--- a/solution.py
+++ b/solution.py
@@ -459,16 +459,23 @@
             theirs_out[slot, t] = rows[ROWS:].astype(BF16)
 
 
-def place_kernel(mine0, mine1, theirs0, theirs1, att, dq, dk, dv, rows, sems):
+def early_kernel(mine0, theirs0, rows):
+    for t in range(4):
+        for slot in range(2):
+            rows[t, :, lanes(own_head(slot))] = mine0[slot, t]
+            rows[t, :, lanes(other_head(slot))] = theirs0[slot, t]
+
+
+def place_kernel(early, mine1, theirs1, att, dq, dk, dv, rows, sems):
     copies = [
         pltpu.make_async_copy(rows.at[t], ref, sems.at[t])
         for t, ref in enumerate((att, dq, dk, dv))
     ]
     for t in range(4):
-        for step in range(CHIPS):
-            mine, theirs = ((mine0, theirs0), (mine1, theirs1))[step // 2]
-            rows[t, :, lanes(own_head(step))] = mine[step % 2, t]
-            rows[t, :, lanes(other_head(step))] = theirs[step % 2, t]
+        rows[t] = early[t]
+        for slot in range(2):
+            rows[t, :, lanes(own_head(2 + slot))] = mine1[slot, t]
+            rows[t, :, lanes(other_head(2 + slot))] = theirs1[slot, t]
         copies[t].start()
     for copy in copies:
         copy.wait()
@@ -541,11 +548,11 @@
     a3, a2, message3 = lax.optimization_barrier((a3, a2, across(message3, 3)))
     fars = (g, a1, a3, a2)
     (top,) = call(top_kernel, "top", [((4, 4, 32, WIDTH), BF16)], *fars)
-    top = across(top, 7)
+    top = across(top, 6)
     out_far, stats_far, message5 = call(
         quad_kernel, "quad", [rows, seg_stats, flat], *fars, out3, stats3, message3
     )
-    message5 = across(message5, 7)
+    message5 = across(message5, 6)
     back = call(
         rest_kernel, "rest", [message] * 4,
         *got, outs, stats, below, *fars, out_far, stats3, stats_far, top, message5,
@@ -560,8 +567,9 @@
         after = (mine,)
         halves.append((mine, in_plane(other, 1)))
     (mine0, theirs0), (mine1, theirs1) = halves
+    (early,) = call(early_kernel, "early", [((4, ROWS, HEADS * WIDTH), BF16)], mine0, theirs0)
     return call(
-        place_kernel, "place", [whole] * 4, mine0, mine1, theirs0, theirs1, out_specs=(LEFT,) * 4,
+        place_kernel, "place", [whole] * 4, early, mine1, theirs1, out_specs=(LEFT,) * 4,
         scratch=[pltpu.VMEM((4, ROWS, HEADS * WIDTH), BF16), pltpu.SemaphoreType.DMA((4,))],
     )
 

time: 58.1 us -> 57.9 us (level)
  waiting for transfers between devices: 16 us -> 12.5 us
  starting transfers between devices: 30.4 us -> 33.6 us
    ppermute x9, starting transfers between devices: 17.3 us -> 20.1 us  [in_plane(): return lax.ppermute(array, 'ctx', moves)]
    ppermute x9, waiting for transfers between devices: 11.3 us -> 8.97 us  [in_plane(): return lax.ppermute(array, 'ctx', moves)]
    ppermute x6, waiting for transfers between devices: 4.69 us -> 3.55 us  [across(): return lax.ppermute(array, 'ctx', moves)]
    pallas_call x13 -> x14, Pallas kernels: 10.7 us -> 10.8 us  [call(): pl.pallas_call(kernel, name=name, out_shape=tuple((jax.ShapeDtypeStruct(s...]
  transfers between devices with their start and end apart: 15 -> 15, of which waited for: 11 -> 8; matrix products, arithmetic and copies ran while one was open for 0% -> 0% of each run, Pallas kernels for 7% -> 9%
where the time goes in v4:
time: 57.9 us; the launch traced here: 57.7 us
  starting transfers between devices  33.6 us (58%)
  waiting for transfers between devices  12.5 us (22%)
  Pallas kernels  10.8 us (19%)
  between operations  0.89 us (2%)
    ppermute x9, starting transfers between devices, in_plane(): return lax.ppermute(array, 'ctx', moves)  20.1 us
    ppermute x6, starting transfers between devices, across(): return lax.ppermute(array, 'ctx', moves)  13.4 us
    pallas_call x14, Pallas kernels, call(): pl.pallas_call(kernel, name=name, out_shape=tuple((jax.ShapeDtypeStruct(s...  10.8 us
    ppermute x9, waiting for transfers between devices, in_plane(): return lax.ppermute(array, 'ctx', moves)  8.97 us
    ppermute x6, waiting for transfers between devices, across(): return lax.ppermute(array, 'ctx', moves)  3.55 us
  transfers between devices with their start and end apart: 15, of which 8 were waited for; matrix products, arithmetic and copies ran while one was open for 0% of the time, Pallas kernels for 9%

profile of v4, /device:TPU:1, one launch (start us, length us, event | category | flops | bytes accessed | tf_op | source)
XLA Modules:
  0.0 57.7 jit_solution(16945344161641585673)
XLA Ops:
  0.6 1.3 %split.1 = (bf16[128,1024]{1,0:T(8,128)(2,1)S(1)}, bf16[128,1024]{1,0:T(8,128)(2,1)S(1)}, bf16[128,1024]{1,0:T(8,128)(2,1)S(1)}, bf16[128,1024]{1,0:T(8,128)(2,1)S(1)}, bf16[4,4,128,128]{3,2,1,0:T(8,128)(2,1)S(1)}) custom-call(bf16[128,1024]{1,0:T(8,128)(2,1)} %q.1, bf16[128,1024]{1,0:T(8,128)(2,1)} %k.1, bf16[128,1024]{1,0:T(8,128)(2,1)} %v.1, ...), custom_call_target="tpu_custom_call" | custom-call | tf_op jit(solution)/shard_map/split/pallas_call | solution.py:491
  1.9 3.3 %collective-permute-start = (bf16[4,4,128,128]{3,2,1,0:T(8,128)(2,1)S(1)}, bf16[4,4,128,128]{3,2,1,0:T(8,128)(2,1)S(1)}, u32[]{:S(2)}, u32[]{:S(2)}) collective-permute-start(bf16[4,4,128,128]{3,2,1,0:T(8,128)(2,1)S(1)} %get-tuple-element.42), channel_id=1, source_target_pairs={{0,1},{1,0},{2,3},{3,2},{4,5},{5,4},{6,7},{7,6},{8,9},{9,8},{10,11... | collective-permute-start | bytes 1572872 | tf_op jit(solution)/shard_map/ppermute | solution.py:504
  5.2 0.8 %maps.1 = (bf16[4,128,256]{2,1,0:T(8,128)(2,1)S(1)}, bf16[4,256,128]{2,1,0:T(8,128)(2,1)S(1)}) custom-call(s32[6,8]{1,0:T(8,128)} %offs_left.1), custom_call_target="tpu_custom_call" | custom-call | tf_op jit(solution)/shard_map/maps/pallas_call | solution.py:491
  6.1 0.7 %collective-permute-done.theirs = bf16[4,4,128,128]{3,2,1,0:T(8,128)(2,1)S(1)} collective-permute-done((bf16[4,4,128,128]{3,2,1,0:T(8,128)(2,1)S(1)}, bf16[4,4,128,128]{3,2,1,0:T(8,128)(2,1)S(1)}, u32[]{:S(2)}, u32[]{:S(2)}) %collective-permute-start) | collective-permute-done | bytes 524320 | tf_op jit(solution)/shard_map/ppermute | solution.py:504
  6.8 1.1 %chip.1 = (bf16[544,128]{1,0:T(8,128)(2,1)S(1)}, bf16[544,128]{1,0:T(8,128)(2,1)S(1)}, bf16[544,128]{1,0:T(8,128)(2,1)S(1)}, bf16[544,128]{1,0:T(8,128)(2,1)S(1)...) custom-call(bf16[128,1024]{1,0:T(8,128)(2,1)S(1)} %get-tuple-element.38.q, ...), custom_call_target="tpu_custom_call" | custom-call | tf_op jit(solution)/shard_map/chip/pallas_call | solution.py:491
  7.9 0.1 collective-permute-start.1
  8.0 2.2 %collective-permute-start.2 = (bf16[544,128]{1,0:T(8,128)(2,1)S(1)}, bf16[544,128]{1,0:T(8,128)(2,1)S(1)}, u32[]{:S(2)}, u32[]{:S(2)}) collective-permute-start(bf16[544,128]{1,0:T(8,128)(2,1)S(1)} %get-tuple-element.49), channel_id=1, source_target_pairs={{0,4},{1,5},{2,6},{3,7},{4,0},{5,1},{6,2},{7,3},{8,12},{9,13},{10,... | collective-permute-start | bytes 417800 | tf_op jit(solution)/shard_map/ppermute | solution.py:504
  10.1 1.7 %collective-permute-start.3 = (bf16[544,128]{1,0:T(8,128)(2,1)S(1)}, bf16[544,128]{1,0:T(8,128)(2,1)S(1)}, u32[]{:S(2)}, u32[]{:S(2)}) collective-permute-start(bf16[544,128]{1,0:T(8,128)(2,1)S(1)} %get-tuple-element.50), channel_id=1, source_target_pairs={{0,6},{1,7},{2,4},{3,5},{4,2},{5,3},{6,0},{7,1},{8,14},{9,15},{10,... | collective-permute-start | bytes 417800 | tf_op jit(solution)/shard_map/ppermute | solution.py:504
  11.8 1.0 %collective-permute-done.1.m1 = bf16[544,128]{1,0:T(8,128)(2,1)S(1)} collective-permute-done((bf16[544,128]{1,0:T(8,128)(2,1)S(1)}, bf16[544,128]{1,0:T(8,128)(2,1)S(1)}, u32[]{:S(2)}, u32[]{:S(2)}) %collective-permute-start.1) | collective-permute-done | bytes 139296 | tf_op jit(solution)/shard_map/ppermute | solution.py:504
  12.8 3.7 %collective-permute-done.2.m2 = bf16[544,128]{1,0:T(8,128)(2,1)S(1)} collective-permute-done((bf16[544,128]{1,0:T(8,128)(2,1)S(1)}, bf16[544,128]{1,0:T(8,128)(2,1)S(1)}, u32[]{:S(2)}, u32[]{:S(2)}) %collective-permute-start.2) | collective-permute-done | bytes 139296 | tf_op jit(solution)/shard_map/ppermute | solution.py:504
  16.6 2.5 %collective-permute-done.3.m3 = bf16[544,128]{1,0:T(8,128)(2,1)S(1)} collective-permute-done((bf16[544,128]{1,0:T(8,128)(2,1)S(1)}, bf16[544,128]{1,0:T(8,128)(2,1)S(1)}, u32[]{:S(2)}, u32[]{:S(2)}) %collective-permute-start.3) | collective-permute-done | bytes 139296 | tf_op jit(solution)/shard_map/ppermute | solution.py:504
  19.1 1.0 %near.1 = (f32[4,128,128]{2,1,0:T(8,128)S(1)}, f32[4,2,128,128]{3,2,1,0:T(8,128)S(1)}, bf16[544,128]{1,0:T(8,128)(2,1)S(1)}, bf16[4,64,128]{2,1,0:T(8,128)(2,1)S(1)}) custom-call(bf16[544,128]{1,0:T(8,128)(2,1)S(1)} %get-tuple-element.47.m0, bf16[544,128]{1,0:T(8,128)(2,1)S(1)} %collective-permute-done.1.m1, bf16[544,128]{1,0:T(8,128)(2,1)S(1)} %collective-permute-done.2.m2, ...), custom_call_target="tpu_custom_call" | custom-call | tf_op jit(solution)/shard_map/near/pallas_call | solution.py:491
  20.0 1.7 %collective-permute-start.4 = (bf16[544,128]{1,0:T(8,128)(2,1)S(1)}, bf16[544,128]{1,0:T(8,128)(2,1)S(1)}, u32[]{:S(2)}, u32[]{:S(2)}) collective-permute-start(bf16[544,128]{1,0:T(8,128)(2,1)S(1)} %get-tuple-element.53.g), channel_id=1, source_target_pairs={{0,8},{1,9},{2,10},{3,11},{4,12},{5,13},{6,14},{7,15},{8,0},{9,1},... | collective-permute-start | bytes 417800 | tf_op jit(solution)/shard_map/ppermute | solution.py:509
  21.7 3.0 %collective-permute-start.6 = (bf16[4,64,128]{2,1,0:T(8,128)(2,1)S(1)}, bf16[4,64,128]{2,1,0:T(8,128)(2,1)S(1)}, u32[]{:S(2)}, u32[]{:S(2)}) collective-permute-start(bf16[4,64,128]{2,1,0:T(8,128)(2,1)S(1)} %get-tuple-element.54), channel_id=1, source_target_pairs={{0,16},{1,17},{2,18},{3,19},{4,20},{5,21},{6,22},{7,23},{8,24},{9,... | collective-permute-start | bytes 196616 | tf_op jit(solution)/shard_map/ppermute | solution.py:509
  24.7 0.0 collective-permute-start.5
  24.7 0.0 collective-permute-done.4.a1
  24.7 0.6 %pair.1 = (f32[128,128]{1,0:T(8,128)S(1)}, f32[2,256,128]{2,1,0:T(8,128)S(1)}, f32[8,128]{1,0:T(8,128)S(1)}) custom-call(bf16[544,128]{1,0:T(8,128)(2,1)S(1)} %get-tuple-element.53.g, bf16[544,128]{1,0:T(8,128)(2,1)S(1)} %collective-permute-done.4.a1), custom_call_target="tpu_custom_call" | custom-call | tf_op jit(solution)/shard_map/pair/pallas_call | solution.py:491
  25.4 5.0 %collective-permute-start.7 = (f32[8,128]{1,0:T(8,128)S(1)}, f32[8,128]{1,0:T(8,128)S(1)}, u32[]{:S(2)}, u32[]{:S(2)}) collective-permute-start(f32[8,128]{1,0:T(8,128)S(1)} %get-tuple-element.55), channel_id=1, source_target_pairs={{0,24},{1,25},{2,26},{3,27},{4,28},{5,29},{6,30},{7,31},{8,16},{9,... | collective-permute-start | bytes 12296 | tf_op jit(solution)/shard_map/ppermute | solution.py:509
  30.4 0.0 collective-permute-done.6.a2
  30.4 0.1 collective-permute-done.5.a3
  30.5 1.2 %collective-permute-done.7.message3 = f32[8,128]{1,0:T(8,128)S(1)} collective-permute-done((f32[8,128]{1,0:T(8,128)S(1)}, f32[8,128]{1,0:T(8,128)S(1)}, u32[]{:S(2)}, u32[]{:S(2)}) %collective-permute-start.7) | collective-permute-done | bytes 4128 | tf_op jit(solution)/shard_map/ppermute | solution.py:509
  31.7 2.0 %collective-permute-start.8 = (bf16[4,4,32,128]{3,2,1,0:T(8,128)(2,1)S(1)}, bf16[4,4,32,128]{3,2,1,0:T(8,128)(2,1)S(1)}, u32[]{:S(2)}, u32[]{:S(2)}) collective-permute-start(bf16[4,4,32,128]{3,2,1,0:T(8,128)(2,1)S(1)} %top.1), channel_id=1, source_target_pairs={{0,48},{1,49},{2,50},{3,51},{4,52},{5,53},{6,54},{7,55},{8,56},{9,... | collective-permute-start | bytes 393224 | tf_op jit(solution)/shard_map/ppermute | solution.py:509
  33.7 0.7 %quad.1 = (f32[128,128]{1,0:T(8,128)S(1)}, f32[2,256,128]{2,1,0:T(8,128)S(1)}, f32[8,128]{1,0:T(8,128)S(1)}) custom-call(bf16[544,128]{1,0:T(8,128)(2,1)S(1)} %get-tuple-element.53.g, bf16[544,128]{1,0:T(8,128)(2,1)S(1)} %collective-permute-done.4.a1, bf16[4,64,128]{2,1,0:T(8,128)(2,1)S(1)} %collective-permute-done.5.a3, ...), custom_call_target="tpu_custom_call" | custom-call | tf_op jit(solution)/shard_map/quad/pallas_call | solution.py:491
  34.4 1.7 %collective-permute-start.9 = (f32[8,128]{1,0:T(8,128)S(1)}, f32[8,128]{1,0:T(8,128)S(1)}, u32[]{:S(2)}, u32[]{:S(2)}) collective-permute-start(f32[8,128]{1,0:T(8,128)S(1)} %get-tuple-element.63), channel_id=1, source_target_pairs={{0,48},{1,49},{2,50},{3,51},{4,52},{5,53},{6,54},{7,55},{8,56},{9,... | collective-permute-start | bytes 12296 | tf_op jit(solution)/shard_map/ppermute | solution.py:509
  36.1 0.7 %below.1 = f32[4,3,128,128]{3,2,1,0:T(8,128)S(1)} custom-call(bf16[544,128]{1,0:T(8,128)(2,1)S(1)} %get-tuple-element.47.m0, bf16[544,128]{1,0:T(8,128)(2,1)S(1)} %collective-permute-done.1.m1, bf16[544,128]{1,0:T(8,128)(2,1)S(1)} %collective-permute-done.2.m2, bf16[544,128]{1,0:T(8,128)(2,1)S(1)} %collective-permute-done.3.m3, ...), custom_call_target="tpu_custom_call" | custom-call | tf_op jit(solution)/shard_map/below/pallas_call | solution.py:491
  36.8 2.2 %collective-permute-done.9.message5 = f32[8,128]{1,0:T(8,128)S(1)} collective-permute-done((f32[8,128]{1,0:T(8,128)S(1)}, f32[8,128]{1,0:T(8,128)S(1)}, u32[]{:S(2)}, u32[]{:S(2)}) %collective-permute-start.9) | collective-permute-done | bytes 4128 | tf_op jit(solution)/shard_map/ppermute | solution.py:509
  39.0 0.0 collective-permute-done.8.far5
  39.0 1.3 %rest.1 = (bf16[544,128]{1,0:T(8,128)(2,1)S(1)}, bf16[544,128]{1,0:T(8,128)(2,1)S(1)}, bf16[544,128]{1,0:T(8,128)(2,1)S(1)}, bf16[544,128]{1,0:T(8,128)(2,1)S(1)}) custom-call(bf16[544,128]{1,0:T(8,128)(2,1)S(1)} %get-tuple-element.47.m0, bf16[544,128]{1,0:T(8,128)(2,1)S(1)} %collective-permute-done.1.m1, bf16[544,128]{1,0:T(8,128)(2,1)S(1)} %collective-permute-done.2.m2, ...), custom_call_target="tpu_custom_call" | custom-call | tf_op jit(solution)/shard_map/rest/pallas_call | solution.py:491
  40.3 0.1 collective-permute-start.10
  40.4 1.4 %collective-permute-start.12 = (bf16[544,128]{1,0:T(8,128)(2,1)S(1)}, bf16[544,128]{1,0:T(8,128)(2,1)S(1)}, u32[]{:S(2)}, u32[]{:S(2)}) collective-permute-start(bf16[544,128]{1,0:T(8,128)(2,1)S(1)} %get-tuple-element.68), channel_id=1, source_target_pairs={{0,4},{1,5},{2,6},{3,7},{4,0},{5,1},{6,2},{7,3},{8,12},{9,13},{10,... | collective-permute-start | bytes 417800 | tf_op jit(solution)/shard_map/ppermute | solution.py:504
  41.8 2.4 %collective-permute-start.13 = (bf16[544,128]{1,0:T(8,128)(2,1)S(1)}, bf16[544,128]{1,0:T(8,128)(2,1)S(1)}, u32[]{:S(2)}, u32[]{:S(2)}) collective-permute-start(bf16[544,128]{1,0:T(8,128)(2,1)S(1)} %get-tuple-element.69), channel_id=1, source_target_pairs={{0,6},{1,7},{2,4},{3,5},{4,2},{5,3},{6,0},{7,1},{8,14},{9,15},{10,... | collective-permute-start | bytes 417800 | tf_op jit(solution)/shard_map/ppermute | solution.py:504
  44.3 0.2 alone.1.others
  44.5 0.0 collective-permute-done.10.c1
  44.5 1.0 %finish.2 = (bf16[2,4,128,128]{3,2,1,0:T(8,128)(2,1)S(1)}, bf16[2,4,128,128]{3,2,1,0:T(8,128)(2,1)S(1)}) custom-call(bf16[128,1024]{1,0:T(8,128)(2,1)S(1)} %get-tuple-element.38.q, bf16[128,1024]{1,0:T(8,128)(2,1)S(1)} %get-tuple-element.39.k, bf16[128,1024]{1,0:T(8,128)(2,1)S(1)} %get-tuple-element.40.v, bf16[128,1024]{1,0:T(8,128)(2,1)S(1)} %get-tuple-element.41.do, ...), custom_call_target="tpu_custom_call" | custom-call | tf_op jit(solution)/shard_map/finish/pallas_call | solution.py:491
  45.5 6.8 %collective-permute-start.11 = (bf16[2,4,128,128]{3,2,1,0:T(8,128)(2,1)S(1)}, bf16[2,4,128,128]{3,2,1,0:T(8,128)(2,1)S(1)}, u32[]{:S(2)}, u32[]{:S(2)}) collective-permute-start(bf16[2,4,128,128]{3,2,1,0:T(8,128)(2,1)S(1)} %get-tuple-element.67), channel_id=1, source_target_pairs={{0,1},{1,0},{2,3},{3,2},{4,5},{5,4},{6,7},{7,6},{8,9},{9,8},{10,11... | collective-permute-start | bytes 786440 | tf_op jit(solution)/shard_map/ppermute | solution.py:504
  52.2 0.0 collective-permute-done.12.c0
  52.2 0.0 collective-permute-done.13.c1
  52.2 1.0 %finish.3 = (bf16[2,4,128,128]{3,2,1,0:T(8,128)(2,1)S(1)}, bf16[2,4,128,128]{3,2,1,0:T(8,128)(2,1)S(1)}) custom-call(bf16[128,1024]{1,0:T(8,128)(2,1)S(1)} %get-tuple-element.38.q, bf16[128,1024]{1,0:T(8,128)(2,1)S(1)} %get-tuple-element.39.k, bf16[128,1024]{1,0:T(8,128)(2,1)S(1)} %get-tuple-element.40.v, bf16[128,1024]{1,0:T(8,128)(2,1)S(1)} %get-tuple-element.41.do, ...), custom_call_target="tpu_custom_call" | custom-call | tf_op jit(solution)/shard_map/finish/pallas_call | solution.py:491
  53.2 2.2 %collective-permute-start.14 = (bf16[2,4,128,128]{3,2,1,0:T(8,128)(2,1)S(1)}, bf16[2,4,128,128]{3,2,1,0:T(8,128)(2,1)S(1)}, u32[]{:S(2)}, u32[]{:S(2)}) collective-permute-start(bf16[2,4,128,128]{3,2,1,0:T(8,128)(2,1)S(1)} %get-tuple-element.71), channel_id=1, source_target_pairs={{0,1},{1,0},{2,3},{3,2},{4,5},{5,4},{6,7},{7,6},{8,9},{9,8},{10,11... | collective-permute-start | bytes 786440 | tf_op jit(solution)/shard_map/ppermute | solution.py:504
  55.4 0.0 collective-permute-done.11.theirs0
  55.4 0.1 early.1
  55.5 1.0 %collective-permute-done.14.theirs1 = bf16[2,4,128,128]{3,2,1,0:T(8,128)(2,1)S(1)} collective-permute-done((bf16[2,4,128,128]{3,2,1,0:T(8,128)(2,1)S(1)}, bf16[2,4,128,128]{3,2,1,0:T(8,128)(2,1)S(1)}, u32[]{:S(2)}, u32[]{:S(2)}) %collective-permute-start.14) | collective-permute-done | bytes 262176 | tf_op jit(solution)/shard_map/ppermute | solution.py:504
  56.5 1.0 %place.1 = (bf16[128,1024]{1,0:T(8,128)(2,1)}, bf16[128,1024]{1,0:T(8,128)(2,1)}, bf16[128,1024]{1,0:T(8,128)(2,1)}, bf16[128,1024]{1,0:T(8,128)(2,1)}) custom-call(bf16[4,128,1024]{2,1,0:T(8,128)(2,1)S(1)} %early.1, bf16[2,4,128,128]{3,2,1,0:T(8,128)(2,1)S(1)} %get-tuple-element.70.mine1, bf16[2,4,128,128]{3,2,1,0:T(8,128)(2,1)S(1)} %collective-permute-done.14.theirs1), custom_call_target="tpu_custom_call" | custom-call | tf_op jit(solution)/shard_map/place/pallas_call | solution.py:491
  (1 shorter events, 0.0 us)
Async XLA Ops:
  1.9 4.9 %collective-permute-start = (bf16[4,4,128,128]{3,2,1,0:T(8,128)(2,1)S(1)}, bf16[4,4,128,128]{3,2,1,0:T(8,128)(2,1)S(1)}, u32[]{:S(2)}, u32[]{:S(2)}) collective-permute-start(bf16[4,4,128,128]{3,2,1,0:T(8,128)(2,1)S(1)} %get-tuple-element.42), channel_id=1, source_target_pairs={{0,1},{1,0},{2,3},{3,2},{4,5},{5,4},{6,7},{7,6},{8,9},{9,8},{10,11... | collective-permute-start | bytes 1572872 | tf_op jit(solution)/shard_map/ppermute | solution.py:504
  7.9 4.9 %collective-permute-start.1 = (bf16[544,128]{1,0:T(8,128)(2,1)S(1)}, bf16[544,128]{1,0:T(8,128)(2,1)S(1)}, u32[]{:S(2)}, u32[]{:S(2)}) collective-permute-start(bf16[544,128]{1,0:T(8,128)(2,1)S(1)} %get-tuple-element.48), channel_id=1, source_target_pairs={{0,2},{1,3},{2,0},{3,1},{4,6},{5,7},{6,4},{7,5},{8,10},{9,11},{10,... | collective-permute-start | bytes 417800 | tf_op jit(solution)/shard_map/ppermute | solution.py:504
  8.0 8.6 %collective-permute-start.2 = (bf16[544,128]{1,0:T(8,128)(2,1)S(1)}, bf16[544,128]{1,0:T(8,128)(2,1)S(1)}, u32[]{:S(2)}, u32[]{:S(2)}) collective-permute-start(bf16[544,128]{1,0:T(8,128)(2,1)S(1)} %get-tuple-element.49), channel_id=1, source_target_pairs={{0,4},{1,5},{2,6},{3,7},{4,0},{5,1},{6,2},{7,3},{8,12},{9,13},{10,... | collective-permute-start | bytes 417800 | tf_op jit(solution)/shard_map/ppermute | solution.py:504
  10.1 8.9 %collective-permute-start.3 = (bf16[544,128]{1,0:T(8,128)(2,1)S(1)}, bf16[544,128]{1,0:T(8,128)(2,1)S(1)}, u32[]{:S(2)}, u32[]{:S(2)}) collective-permute-start(bf16[544,128]{1,0:T(8,128)(2,1)S(1)} %get-tuple-element.50), channel_id=1, source_target_pairs={{0,6},{1,7},{2,4},{3,5},{4,2},{5,3},{6,0},{7,1},{8,14},{9,15},{10,... | collective-permute-start | bytes 417800 | tf_op jit(solution)/shard_map/ppermute | solution.py:504
  20.0 4.7 %collective-permute-start.4 = (bf16[544,128]{1,0:T(8,128)(2,1)S(1)}, bf16[544,128]{1,0:T(8,128)(2,1)S(1)}, u32[]{:S(2)}, u32[]{:S(2)}) collective-permute-start(bf16[544,128]{1,0:T(8,128)(2,1)S(1)} %get-tuple-element.53.g), channel_id=1, source_target_pairs={{0,8},{1,9},{2,10},{3,11},{4,12},{5,13},{6,14},{7,15},{8,0},{9,1},... | collective-permute-start | bytes 417800 | tf_op jit(solution)/shard_map/ppermute | solution.py:509
  21.7 8.6 %collective-permute-start.6 = (bf16[4,64,128]{2,1,0:T(8,128)(2,1)S(1)}, bf16[4,64,128]{2,1,0:T(8,128)(2,1)S(1)}, u32[]{:S(2)}, u32[]{:S(2)}) collective-permute-start(bf16[4,64,128]{2,1,0:T(8,128)(2,1)S(1)} %get-tuple-element.54), channel_id=1, source_target_pairs={{0,16},{1,17},{2,18},{3,19},{4,20},{5,21},{6,22},{7,23},{8,24},{9,... | collective-permute-start | bytes 196616 | tf_op jit(solution)/shard_map/ppermute | solution.py:509
  24.7 5.8 %collective-permute-start.5 = (bf16[4,64,128]{2,1,0:T(8,128)(2,1)S(1)}, bf16[4,64,128]{2,1,0:T(8,128)(2,1)S(1)}, u32[]{:S(2)}, u32[]{:S(2)}) collective-permute-start(bf16[4,64,128]{2,1,0:T(8,128)(2,1)S(1)} %get-tuple-element.54), channel_id=1, source_target_pairs={{0,24},{1,25},{2,26},{3,27},{4,28},{5,29},{6,30},{7,31},{8,16},{9,... | collective-permute-start | bytes 196616 | tf_op jit(solution)/shard_map/ppermute | solution.py:509
  25.4 6.3 %collective-permute-start.7 = (f32[8,128]{1,0:T(8,128)S(1)}, f32[8,128]{1,0:T(8,128)S(1)}, u32[]{:S(2)}, u32[]{:S(2)}) collective-permute-start(f32[8,128]{1,0:T(8,128)S(1)} %get-tuple-element.55), channel_id=1, source_target_pairs={{0,24},{1,25},{2,26},{3,27},{4,28},{5,29},{6,30},{7,31},{8,16},{9,... | collective-permute-start | bytes 12296 | tf_op jit(solution)/shard_map/ppermute | solution.py:509
  31.7 7.3 %collective-permute-start.8 = (bf16[4,4,32,128]{3,2,1,0:T(8,128)(2,1)S(1)}, bf16[4,4,32,128]{3,2,1,0:T(8,128)(2,1)S(1)}, u32[]{:S(2)}, u32[]{:S(2)}) collective-permute-start(bf16[4,4,32,128]{3,2,1,0:T(8,128)(2,1)S(1)} %top.1), channel_id=1, source_target_pairs={{0,48},{1,49},{2,50},{3,51},{4,52},{5,53},{6,54},{7,55},{8,56},{9,... | collective-permute-start | bytes 393224 | tf_op jit(solution)/shard_map/ppermute | solution.py:509
  34.4 4.6 %collective-permute-start.9 = (f32[8,128]{1,0:T(8,128)S(1)}, f32[8,128]{1,0:T(8,128)S(1)}, u32[]{:S(2)}, u32[]{:S(2)}) collective-permute-start(f32[8,128]{1,0:T(8,128)S(1)} %get-tuple-element.63), channel_id=1, source_target_pairs={{0,48},{1,49},{2,50},{3,51},{4,52},{5,53},{6,54},{7,55},{8,56},{9,... | collective-permute-start | bytes 12296 | tf_op jit(solution)/shard_map/ppermute | solution.py:509
  40.3 4.2 %collective-permute-start.10 = (bf16[544,128]{1,0:T(8,128)(2,1)S(1)}, bf16[544,128]{1,0:T(8,128)(2,1)S(1)}, u32[]{:S(2)}, u32[]{:S(2)}) collective-permute-start(bf16[544,128]{1,0:T(8,128)(2,1)S(1)} %get-tuple-element.65), channel_id=1, source_target_pairs={{0,2},{1,3},{2,0},{3,1},{4,6},{5,7},{6,4},{7,5},{8,10},{9,11},{10,... | collective-permute-start | bytes 417800 | tf_op jit(solution)/shard_map/ppermute | solution.py:504
  40.4 11.8 %collective-permute-start.12 = (bf16[544,128]{1,0:T(8,128)(2,1)S(1)}, bf16[544,128]{1,0:T(8,128)(2,1)S(1)}, u32[]{:S(2)}, u32[]{:S(2)}) collective-permute-start(bf16[544,128]{1,0:T(8,128)(2,1)S(1)} %get-tuple-element.68), channel_id=1, source_target_pairs={{0,4},{1,5},{2,6},{3,7},{4,0},{5,1},{6,2},{7,3},{8,12},{9,13},{10,... | collective-permute-start | bytes 417800 | tf_op jit(solution)/shard_map/ppermute | solution.py:504
  41.8 10.4 %collective-permute-start.13 = (bf16[544,128]{1,0:T(8,128)(2,1)S(1)}, bf16[544,128]{1,0:T(8,128)(2,1)S(1)}, u32[]{:S(2)}, u32[]{:S(2)}) collective-permute-start(bf16[544,128]{1,0:T(8,128)(2,1)S(1)} %get-tuple-element.69), channel_id=1, source_target_pairs={{0,6},{1,7},{2,4},{3,5},{4,2},{5,3},{6,0},{7,1},{8,14},{9,15},{10,... | collective-permute-start | bytes 417800 | tf_op jit(solution)/shard_map/ppermute | solution.py:504
  45.5 9.9 %collective-permute-start.11 = (bf16[2,4,128,128]{3,2,1,0:T(8,128)(2,1)S(1)}, bf16[2,4,128,128]{3,2,1,0:T(8,128)(2,1)S(1)}, u32[]{:S(2)}, u32[]{:S(2)}) collective-permute-start(bf16[2,4,128,128]{3,2,1,0:T(8,128)(2,1)S(1)} %get-tuple-element.67), channel_id=1, source_target_pairs={{0,1},{1,0},{2,3},{3,2},{4,5},{5,4},{6,7},{7,6},{8,9},{9,8},{10,11... | collective-permute-start | bytes 786440 | tf_op jit(solution)/shard_map/ppermute | solution.py:504
  53.2 3.4 %collective-permute-start.14 = (bf16[2,4,128,128]{3,2,1,0:T(8,128)(2,1)S(1)}, bf16[2,4,128,128]{3,2,1,0:T(8,128)(2,1)S(1)}, u32[]{:S(2)}, u32[]{:S(2)}) collective-permute-start(bf16[2,4,128,128]{3,2,1,0:T(8,128)(2,1)S(1)} %get-tuple-element.71), channel_id=1, source_target_pairs={{0,1},{1,0},{2,3},{3,2},{4,5},{5,4},{6,7},{7,6},{8,9},{9,8},{10,11... | collective-permute-start | bytes 786440 | tf_op jit(solution)/shard_map/ppermute | solution.py:504

commit v5 on v4

--- a/solution.py
+++ b/solution.py
@@ -189,32 +189,33 @@
         places[step] = placing(offs, own_head(step))
 
 
-def chip_kernel(q, k, v, do, theirs, picks, m0, m1, m2, m3, outs, stats):
-    messages = (m0, m1, m2, m3)
-    tensors = [chip_rows(step, (q, k, v, do), theirs) for step in range(CHIPS)]
+def chip_kernel(steps, q, k, v, do, theirs, picks, *refs):
+    messages, (outs, stats) = refs[:-2], refs[-2:]
+    tensors = [chip_rows(step, (q, k, v, do), theirs) for step in steps]
     found = attend(*(rows[:3] for rows in tensors))
-    picked = [nn(picks[step], side_by_side(tensors[step])) for step in range(CHIPS)]
-    deltas = [dotted(tensors[step][3], found[step][0]) for step in range(CHIPS)]
-    for step, message in enumerate(messages):
+    picked = [nn(picks[step], side_by_side(rows)) for step, rows in zip(steps, tensors)]
+    deltas = [dotted(rows[3], out) for rows, (out, _) in zip(tensors, found)]
+    for slot, message in enumerate(messages):
         for t in range(4):
-            rows = picked[step][:, t * WIDTH : (t + 1) * WIDTH]
+            rows = picked[slot][:, t * WIDTH : (t + 1) * WIDTH]
             message[t * ROWS : (t + 1) * ROWS] = rows.astype(BF16)
     lane = lax.broadcasted_iota(jnp.int32, (1, WIDTH), 1)
-    for step, message in enumerate(messages):
-        out, total = found[step]
-        outs[step] = out
-        stats[step, 0] = total
-        stats[step, 1] = deltas[step]
-        flat = jnp.where(lane & 4 == 0, total, deltas[step]).T[:8]
+    for slot, (step, message) in enumerate(zip(steps, messages)):
+        out, total = found[slot]
+        outs[slot] = out
+        stats[slot, 0] = total
+        stats[slot, 1] = deltas[slot]
+        flat = jnp.where(lane & 4 == 0, total, deltas[slot]).T[:8]
         flat = nt(join([term.astype(F32) for term in three_terms(flat)]).astype(BF16), picks[step])
         message[BODY:] = join([flat, jnp.zeros((8, WIDTH), F32)]).astype(BF16)
 
 
-def alone_kernel(places, stats, others):
+def alone_kernel(places, stats_own, stats_sent, others):
     for step in range(CHIPS):
         alone = 1.0 - nn(places[step], jnp.ones((ROWS, WIDTH), BF16))
         for i in range(2):
-            others[step, i] = stats[step, i] * alone
+            stat = stats_sent[step - 1, i] if step else stats_own[0, i]
+            others[step, i] = stat * alone
 
 
 def tensor(ref, t, rows=ROWS):
@@ -433,7 +434,8 @@
         )
 
 
-def finish_kernel(steps, q, k, v, do, theirs, places, outs, stats, others, c0, c1, *refs):
+def finish_kernel(steps, q, k, v, do, theirs, places, outs_own, outs_sent, stats_own,
+    stats_sent, others, c0, c1, *refs):
     mine_out, theirs_out = refs[-2:]
     messages = (c0, c1)
     tensors = [chip_rows(step, (q, k, v, do), theirs) for step in steps]
@@ -447,7 +449,11 @@
     ]
     found = scored(scores, grads, stat)
     own = [
-        [outs[step] * jnp.exp(stats[step, 0] - stat[slot][0]) for slot, step in enumerate(steps)],
+        [
+            (outs_sent[step - 1] if step else outs_own[0])
+            * jnp.exp((stats_sent[step - 1, 0] if step else stats_own[0, 0]) - stat[slot][0])
+            for slot, step in enumerate(steps)
+        ],
         [nn(score, rows[1]) for (_, score), rows in zip(found, tensors)],
         [tn(score, rows[0]) for (_, score), rows in zip(found, tensors)],
         [tn(chance, rows[3]) for (chance, _), rows in zip(found, tensors)],
@@ -530,10 +536,18 @@
         maps_kernel, "maps", [((CHIPS, ROWS, CHIP), BF16), ((CHIPS, CHIP, ROWS), BF16)], offsets,
         left=1, scratch=[pltpu.SMEM((6, HEADS), jnp.int32), pltpu.SemaphoreType.DMA((1,))],
     )
-    *sent, outs0, stats0 = call(
-        chip_kernel, "chip", [message] * 4 + [chips, chip_stats], *raw, theirs, picks
-    )
-    (others,) = call(alone_kernel, "alone", [chip_stats], places, stats0)
+    found = []
+    for steps in ((1, 2, 3), (0,)):
+        sizes = [((len(steps), CHIP, WIDTH), F32), ((len(steps), 2, CHIP, WIDTH), F32)]
+        found.append(
+            call(
+                functools.partial(chip_kernel, steps), "chip", [message] * len(steps) + sizes,
+                *raw, theirs, picks,
+            )
+        )
+    (*sent, outs_sent, stats_sent), (kept, outs_own, stats_own) = found
+    sent = [kept, *sent]
+    (others,) = call(alone_kernel, "alone", [chip_stats], places, stats_own, stats_sent)
     got = [sent[0]] + [in_plane(sent[step], 2 * step) for step in (1, 2, 3)]
     outs, stats, g, g4 = call(
         near_kernel, "near", [quads, quad_stats, message, ((4, 64, WIDTH), BF16)], *got
@@ -562,7 +576,7 @@
     for steps in ((0, 1), (2, 3)):
         mine, other = call(
             functools.partial(finish_kernel, steps), "finish", [pairs, pairs],
-            *raw, theirs, places, outs0, stats0, others, *(back[step] for step in steps), *after,
+            *raw, theirs, places, outs_own, outs_sent, stats_own, stats_sent, others, *(back[step] for step in steps), *after,
         )
         after = (mine,)
         halves.append((mine, in_plane(other, 1)))

time: 57.9 us -> 57.7 us (level)
  waiting for transfers between devices: 12.5 us -> 11.7 us
  Pallas kernels: 10.8 us -> 11.4 us
    ppermute x9, waiting for transfers between devices: 8.97 us -> 8.17 us  [in_plane(): return lax.ppermute(array, 'ctx', moves)]
    pallas_call x14 -> x15, Pallas kernels: 10.8 us -> 11.4 us  [call(): pl.pallas_call(kernel, name=name, out_shape=tuple((jax.ShapeDtypeStruct(s...]
  transfers between devices with their start and end apart: 15 -> 15, of which waited for: 8 -> 8; matrix products, arithmetic and copies ran while one was open for 0% -> 0% of each run, Pallas kernels for 9% -> 10%
where the time goes in v5:
time: 57.7 us; the launch traced here: 57.6 us
  starting transfers between devices  33.6 us (58%)
  waiting for transfers between devices  11.7 us (20%)
  Pallas kernels  11.4 us (20%)
  between operations  0.89 us (2%)
    ppermute x9, starting transfers between devices, in_plane(): return lax.ppermute(array, 'ctx', moves)  20.1 us
    ppermute x6, starting transfers between devices, across(): return lax.ppermute(array, 'ctx', moves)  13.5 us
    pallas_call x15, Pallas kernels, call(): pl.pallas_call(kernel, name=name, out_shape=tuple((jax.ShapeDtypeStruct(s...  11.4 us
    ppermute x9, waiting for transfers between devices, in_plane(): return lax.ppermute(array, 'ctx', moves)  8.17 us
    ppermute x6, waiting for transfers between devices, across(): return lax.ppermute(array, 'ctx', moves)  3.53 us
  transfers between devices with their start and end apart: 15, of which 8 were waited for; matrix products, arithmetic and copies ran while one was open for 0% of the time, Pallas kernels for 10%

profile of v5, /device:TPU:1, one launch (start us, length us, event | category | flops | bytes accessed | tf_op | source)
XLA Modules:
  0.0 57.6 jit_solution(11815981894369129980)
XLA Ops:
  0.6 1.3 %split.1 = (bf16[128,1024]{1,0:T(8,128)(2,1)S(1)}, bf16[128,1024]{1,0:T(8,128)(2,1)S(1)}, bf16[128,1024]{1,0:T(8,128)(2,1)S(1)}, bf16[128,1024]{1,0:T(8,128)(2,1)S(1)}, bf16[4,4,128,128]{3,2,1,0:T(8,128)(2,1)S(1)}) custom-call(bf16[128,1024]{1,0:T(8,128)(2,1)} %q.1, bf16[128,1024]{1,0:T(8,128)(2,1)} %k.1, bf16[128,1024]{1,0:T(8,128)(2,1)} %v.1, ...), custom_call_target="tpu_custom_call" | custom-call | tf_op jit(solution)/shard_map/split/pallas_call | solution.py:497
  1.9 3.3 %collective-permute-start = (bf16[4,4,128,128]{3,2,1,0:T(8,128)(2,1)S(1)}, bf16[4,4,128,128]{3,2,1,0:T(8,128)(2,1)S(1)}, u32[]{:S(2)}, u32[]{:S(2)}) collective-permute-start(bf16[4,4,128,128]{3,2,1,0:T(8,128)(2,1)S(1)} %get-tuple-element.44), channel_id=1, source_target_pairs={{0,1},{1,0},{2,3},{3,2},{4,5},{5,4},{6,7},{7,6},{8,9},{9,8},{10,11... | collective-permute-start | bytes 1572872 | tf_op jit(solution)/shard_map/ppermute | solution.py:510
  5.2 0.8 %maps.1 = (bf16[4,128,256]{2,1,0:T(8,128)(2,1)S(1)}, bf16[4,256,128]{2,1,0:T(8,128)(2,1)S(1)}) custom-call(s32[6,8]{1,0:T(8,128)} %offs_left.1), custom_call_target="tpu_custom_call" | custom-call | tf_op jit(solution)/shard_map/maps/pallas_call | solution.py:497
  6.1 0.7 %collective-permute-done.theirs = bf16[4,4,128,128]{3,2,1,0:T(8,128)(2,1)S(1)} collective-permute-done((bf16[4,4,128,128]{3,2,1,0:T(8,128)(2,1)S(1)}, bf16[4,4,128,128]{3,2,1,0:T(8,128)(2,1)S(1)}, u32[]{:S(2)}, u32[]{:S(2)}) %collective-permute-start) | collective-permute-done | bytes 524320 | tf_op jit(solution)/shard_map/ppermute | solution.py:510
  6.8 1.0 %chip.3 = (bf16[544,128]{1,0:T(8,128)(2,1)S(1)}, bf16[544,128]{1,0:T(8,128)(2,1)S(1)}, bf16[544,128]{1,0:T(8,128)(2,1)S(1)}, f32[3,256,128]{2,1,0:T(8,128)S(1)}, f32[3,2,256,128]{3,2,1,0:T(8,128)S(1)}) custom-call(bf16[128,1024]{1,0:T(8,128)(2,1)S(1)} %get-tuple-element.40.q, bf16[128,1024]{1,0:T(8,128)(2,1)S(1)} %get-tuple-element.41.k, ...), custom_call_target="tpu_custom_call" | custom-call | tf_op jit(solution)/shard_map/chip/pallas_call | solution.py:497
  7.8 0.0 collective-permute-start.1
  7.8 2.2 %collective-permute-start.2 = (bf16[544,128]{1,0:T(8,128)(2,1)S(1)}, bf16[544,128]{1,0:T(8,128)(2,1)S(1)}, u32[]{:S(2)}, u32[]{:S(2)}) collective-permute-start(bf16[544,128]{1,0:T(8,128)(2,1)S(1)} %get-tuple-element.53), channel_id=1, source_target_pairs={{0,4},{1,5},{2,6},{3,7},{4,0},{5,1},{6,2},{7,3},{8,12},{9,13},{10,... | collective-permute-start | bytes 417800 | tf_op jit(solution)/shard_map/ppermute | solution.py:510
  10.0 1.7 %collective-permute-start.3 = (bf16[544,128]{1,0:T(8,128)(2,1)S(1)}, bf16[544,128]{1,0:T(8,128)(2,1)S(1)}, u32[]{:S(2)}, u32[]{:S(2)}) collective-permute-start(bf16[544,128]{1,0:T(8,128)(2,1)S(1)} %get-tuple-element.54), channel_id=1, source_target_pairs={{0,6},{1,7},{2,4},{3,5},{4,2},{5,3},{6,0},{7,1},{8,14},{9,15},{10,... | collective-permute-start | bytes 417800 | tf_op jit(solution)/shard_map/ppermute | solution.py:510
  11.7 0.8 %chip.2 = (bf16[544,128]{1,0:T(8,128)(2,1)S(1)}, f32[1,256,128]{2,1,0:T(8,128)S(1)}, f32[1,2,256,128]{3,2,1,0:T(8,128)S(1)}) custom-call(bf16[128,1024]{1,0:T(8,128)(2,1)S(1)} %get-tuple-element.40.q, bf16[128,1024]{1,0:T(8,128)(2,1)S(1)} %get-tuple-element.41.k, bf16[128,1024]{1,0:T(8,128)(2,1)S(1)} %get-tuple-element.42.v, ...), custom_call_target="tpu_custom_call" | custom-call | tf_op jit(solution)/shard_map/chip/pallas_call | solution.py:497
  12.5 0.2 collective-permute-done.1.m1
  12.7 3.7 %collective-permute-done.2.m2 = bf16[544,128]{1,0:T(8,128)(2,1)S(1)} collective-permute-done((bf16[544,128]{1,0:T(8,128)(2,1)S(1)}, bf16[544,128]{1,0:T(8,128)(2,1)S(1)}, u32[]{:S(2)}, u32[]{:S(2)}) %collective-permute-start.2) | collective-permute-done | bytes 139296 | tf_op jit(solution)/shard_map/ppermute | solution.py:510
  16.4 2.5 %collective-permute-done.3.m3 = bf16[544,128]{1,0:T(8,128)(2,1)S(1)} collective-permute-done((bf16[544,128]{1,0:T(8,128)(2,1)S(1)}, bf16[544,128]{1,0:T(8,128)(2,1)S(1)}, u32[]{:S(2)}, u32[]{:S(2)}) %collective-permute-start.3) | collective-permute-done | bytes 139296 | tf_op jit(solution)/shard_map/ppermute | solution.py:510
  18.9 1.0 %near.1 = (f32[4,128,128]{2,1,0:T(8,128)S(1)}, f32[4,2,128,128]{3,2,1,0:T(8,128)S(1)}, bf16[544,128]{1,0:T(8,128)(2,1)S(1)}, bf16[4,64,128]{2,1,0:T(8,128)(2,1)S(1)}) custom-call(bf16[544,128]{1,0:T(8,128)(2,1)S(1)} %get-tuple-element.51.m0, bf16[544,128]{1,0:T(8,128)(2,1)S(1)} %collective-permute-done.1.m1, bf16[544,128]{1,0:T(8,128)(2,1)S(1)} %collective-permute-done.2.m2, ...), custom_call_target="tpu_custom_call" | custom-call | tf_op jit(solution)/shard_map/near/pallas_call | solution.py:497
  19.9 1.7 %collective-permute-start.4 = (bf16[544,128]{1,0:T(8,128)(2,1)S(1)}, bf16[544,128]{1,0:T(8,128)(2,1)S(1)}, u32[]{:S(2)}, u32[]{:S(2)}) collective-permute-start(bf16[544,128]{1,0:T(8,128)(2,1)S(1)} %get-tuple-element.57.g), channel_id=1, source_target_pairs={{0,8},{1,9},{2,10},{3,11},{4,12},{5,13},{6,14},{7,15},{8,0},{9,1},... | collective-permute-start | bytes 417800 | tf_op jit(solution)/shard_map/ppermute | solution.py:515
  21.6 3.0 %collective-permute-start.6 = (bf16[4,64,128]{2,1,0:T(8,128)(2,1)S(1)}, bf16[4,64,128]{2,1,0:T(8,128)(2,1)S(1)}, u32[]{:S(2)}, u32[]{:S(2)}) collective-permute-start(bf16[4,64,128]{2,1,0:T(8,128)(2,1)S(1)} %get-tuple-element.58), channel_id=1, source_target_pairs={{0,16},{1,17},{2,18},{3,19},{4,20},{5,21},{6,22},{7,23},{8,24},{9,... | collective-permute-start | bytes 196616 | tf_op jit(solution)/shard_map/ppermute | solution.py:515
  24.6 0.0 collective-permute-start.5
  24.6 0.0 collective-permute-done.4.a1
  24.6 0.6 %pair.1 = (f32[128,128]{1,0:T(8,128)S(1)}, f32[2,256,128]{2,1,0:T(8,128)S(1)}, f32[8,128]{1,0:T(8,128)S(1)}) custom-call(bf16[544,128]{1,0:T(8,128)(2,1)S(1)} %get-tuple-element.57.g, bf16[544,128]{1,0:T(8,128)(2,1)S(1)} %collective-permute-done.4.a1), custom_call_target="tpu_custom_call" | custom-call | tf_op jit(solution)/shard_map/pair/pallas_call | solution.py:497
  25.2 5.0 %collective-permute-start.7 = (f32[8,128]{1,0:T(8,128)S(1)}, f32[8,128]{1,0:T(8,128)S(1)}, u32[]{:S(2)}, u32[]{:S(2)}) collective-permute-start(f32[8,128]{1,0:T(8,128)S(1)} %get-tuple-element.59), channel_id=1, source_target_pairs={{0,24},{1,25},{2,26},{3,27},{4,28},{5,29},{6,30},{7,31},{8,16},{9,... | collective-permute-start | bytes 12296 | tf_op jit(solution)/shard_map/ppermute | solution.py:515
  30.2 0.0 collective-permute-done.6.a2
  30.3 0.1 collective-permute-done.5.a3
  30.4 1.2 %collective-permute-done.7.message3 = f32[8,128]{1,0:T(8,128)S(1)} collective-permute-done((f32[8,128]{1,0:T(8,128)S(1)}, f32[8,128]{1,0:T(8,128)S(1)}, u32[]{:S(2)}, u32[]{:S(2)}) %collective-permute-start.7) | collective-permute-done | bytes 4128 | tf_op jit(solution)/shard_map/ppermute | solution.py:515
  31.6 2.0 %collective-permute-start.8 = (bf16[4,4,32,128]{3,2,1,0:T(8,128)(2,1)S(1)}, bf16[4,4,32,128]{3,2,1,0:T(8,128)(2,1)S(1)}, u32[]{:S(2)}, u32[]{:S(2)}) collective-permute-start(bf16[4,4,32,128]{3,2,1,0:T(8,128)(2,1)S(1)} %top.1), channel_id=1, source_target_pairs={{0,48},{1,49},{2,50},{3,51},{4,52},{5,53},{6,54},{7,55},{8,56},{9,... | collective-permute-start | bytes 393224 | tf_op jit(solution)/shard_map/ppermute | solution.py:515
  33.6 0.7 %quad.1 = (f32[128,128]{1,0:T(8,128)S(1)}, f32[2,256,128]{2,1,0:T(8,128)S(1)}, f32[8,128]{1,0:T(8,128)S(1)}) custom-call(bf16[544,128]{1,0:T(8,128)(2,1)S(1)} %get-tuple-element.57.g, bf16[544,128]{1,0:T(8,128)(2,1)S(1)} %collective-permute-done.4.a1, bf16[4,64,128]{2,1,0:T(8,128)(2,1)S(1)} %collective-permute-done.5.a3, ...), custom_call_target="tpu_custom_call" | custom-call | tf_op jit(solution)/shard_map/quad/pallas_call | solution.py:497
  34.2 1.7 %collective-permute-start.9 = (f32[8,128]{1,0:T(8,128)S(1)}, f32[8,128]{1,0:T(8,128)S(1)}, u32[]{:S(2)}, u32[]{:S(2)}) collective-permute-start(f32[8,128]{1,0:T(8,128)S(1)} %get-tuple-element.67), channel_id=1, source_target_pairs={{0,48},{1,49},{2,50},{3,51},{4,52},{5,53},{6,54},{7,55},{8,56},{9,... | collective-permute-start | bytes 12296 | tf_op jit(solution)/shard_map/ppermute | solution.py:515
  36.0 0.7 %below.1 = f32[4,3,128,128]{3,2,1,0:T(8,128)S(1)} custom-call(bf16[544,128]{1,0:T(8,128)(2,1)S(1)} %get-tuple-element.51.m0, bf16[544,128]{1,0:T(8,128)(2,1)S(1)} %collective-permute-done.1.m1, bf16[544,128]{1,0:T(8,128)(2,1)S(1)} %collective-permute-done.2.m2, bf16[544,128]{1,0:T(8,128)(2,1)S(1)} %collective-permute-done.3.m3, ...), custom_call_target="tpu_custom_call" | custom-call | tf_op jit(solution)/shard_map/below/pallas_call | solution.py:497
  36.7 2.2 %collective-permute-done.9.message5 = f32[8,128]{1,0:T(8,128)S(1)} collective-permute-done((f32[8,128]{1,0:T(8,128)S(1)}, f32[8,128]{1,0:T(8,128)S(1)}, u32[]{:S(2)}, u32[]{:S(2)}) %collective-permute-start.9) | collective-permute-done | bytes 4128 | tf_op jit(solution)/shard_map/ppermute | solution.py:515
  38.9 0.0 collective-permute-done.8.far5
  38.9 1.3 %rest.1 = (bf16[544,128]{1,0:T(8,128)(2,1)S(1)}, bf16[544,128]{1,0:T(8,128)(2,1)S(1)}, bf16[544,128]{1,0:T(8,128)(2,1)S(1)}, bf16[544,128]{1,0:T(8,128)(2,1)S(1)}) custom-call(bf16[544,128]{1,0:T(8,128)(2,1)S(1)} %get-tuple-element.51.m0, bf16[544,128]{1,0:T(8,128)(2,1)S(1)} %collective-permute-done.1.m1, bf16[544,128]{1,0:T(8,128)(2,1)S(1)} %collective-permute-done.2.m2, ...), custom_call_target="tpu_custom_call" | custom-call | tf_op jit(solution)/shard_map/rest/pallas_call | solution.py:497
  40.2 0.1 collective-permute-start.10
  40.3 1.4 %collective-permute-start.12 = (bf16[544,128]{1,0:T(8,128)(2,1)S(1)}, bf16[544,128]{1,0:T(8,128)(2,1)S(1)}, u32[]{:S(2)}, u32[]{:S(2)}) collective-permute-start(bf16[544,128]{1,0:T(8,128)(2,1)S(1)} %get-tuple-element.72), channel_id=1, source_target_pairs={{0,4},{1,5},{2,6},{3,7},{4,0},{5,1},{6,2},{7,3},{8,12},{9,13},{10,... | collective-permute-start | bytes 417800 | tf_op jit(solution)/shard_map/ppermute | solution.py:510
  41.7 2.4 %collective-permute-start.13 = (bf16[544,128]{1,0:T(8,128)(2,1)S(1)}, bf16[544,128]{1,0:T(8,128)(2,1)S(1)}, u32[]{:S(2)}, u32[]{:S(2)}) collective-permute-start(bf16[544,128]{1,0:T(8,128)(2,1)S(1)} %get-tuple-element.73), channel_id=1, source_target_pairs={{0,6},{1,7},{2,4},{3,5},{4,2},{5,3},{6,0},{7,1},{8,14},{9,15},{10,... | collective-permute-start | bytes 417800 | tf_op jit(solution)/shard_map/ppermute | solution.py:510
  44.1 0.2 alone.1.others
  44.3 0.0 collective-permute-done.10.c1
  44.3 1.0 %finish.2 = (bf16[2,4,128,128]{3,2,1,0:T(8,128)(2,1)S(1)}, bf16[2,4,128,128]{3,2,1,0:T(8,128)(2,1)S(1)}) custom-call(bf16[128,1024]{1,0:T(8,128)(2,1)S(1)} %get-tuple-element.40.q, bf16[128,1024]{1,0:T(8,128)(2,1)S(1)} %get-tuple-element.41.k, bf16[128,1024]{1,0:T(8,128)(2,1)S(1)} %get-tuple-element.42.v, bf16[128,1024]{1,0:T(8,128)(2,1)S(1)} %get-tuple-element.43.do, ...), custom_call_target="tpu_custom_call" | custom-call | tf_op jit(solution)/shard_map/finish/pallas_call | solution.py:497
  45.3 6.8 %collective-permute-start.11 = (bf16[2,4,128,128]{3,2,1,0:T(8,128)(2,1)S(1)}, bf16[2,4,128,128]{3,2,1,0:T(8,128)(2,1)S(1)}, u32[]{:S(2)}, u32[]{:S(2)}) collective-permute-start(bf16[2,4,128,128]{3,2,1,0:T(8,128)(2,1)S(1)} %get-tuple-element.71), channel_id=1, source_target_pairs={{0,1},{1,0},{2,3},{3,2},{4,5},{5,4},{6,7},{7,6},{8,9},{9,8},{10,11... | collective-permute-start | bytes 786440 | tf_op jit(solution)/shard_map/ppermute | solution.py:510
  52.1 0.0 collective-permute-done.12.c0
  52.1 0.0 collective-permute-done.13.c1
  52.1 1.0 %finish.3 = (bf16[2,4,128,128]{3,2,1,0:T(8,128)(2,1)S(1)}, bf16[2,4,128,128]{3,2,1,0:T(8,128)(2,1)S(1)}) custom-call(bf16[128,1024]{1,0:T(8,128)(2,1)S(1)} %get-tuple-element.40.q, bf16[128,1024]{1,0:T(8,128)(2,1)S(1)} %get-tuple-element.41.k, bf16[128,1024]{1,0:T(8,128)(2,1)S(1)} %get-tuple-element.42.v, bf16[128,1024]{1,0:T(8,128)(2,1)S(1)} %get-tuple-element.43.do, ...), custom_call_target="tpu_custom_call" | custom-call | tf_op jit(solution)/shard_map/finish/pallas_call | solution.py:497
  53.0 2.2 %collective-permute-start.14 = (bf16[2,4,128,128]{3,2,1,0:T(8,128)(2,1)S(1)}, bf16[2,4,128,128]{3,2,1,0:T(8,128)(2,1)S(1)}, u32[]{:S(2)}, u32[]{:S(2)}) collective-permute-start(bf16[2,4,128,128]{3,2,1,0:T(8,128)(2,1)S(1)} %get-tuple-element.75), channel_id=1, source_target_pairs={{0,1},{1,0},{2,3},{3,2},{4,5},{5,4},{6,7},{7,6},{8,9},{9,8},{10,11... | collective-permute-start | bytes 786440 | tf_op jit(solution)/shard_map/ppermute | solution.py:510
  55.2 0.0 collective-permute-done.11.theirs0
  55.2 0.1 early.1
  55.4 1.0 %collective-permute-done.14.theirs1 = bf16[2,4,128,128]{3,2,1,0:T(8,128)(2,1)S(1)} collective-permute-done((bf16[2,4,128,128]{3,2,1,0:T(8,128)(2,1)S(1)}, bf16[2,4,128,128]{3,2,1,0:T(8,128)(2,1)S(1)}, u32[]{:S(2)}, u32[]{:S(2)}) %collective-permute-start.14) | collective-permute-done | bytes 262176 | tf_op jit(solution)/shard_map/ppermute | solution.py:510
  56.4 1.0 %place.1 = (bf16[128,1024]{1,0:T(8,128)(2,1)}, bf16[128,1024]{1,0:T(8,128)(2,1)}, bf16[128,1024]{1,0:T(8,128)(2,1)}, bf16[128,1024]{1,0:T(8,128)(2,1)}) custom-call(bf16[4,128,1024]{2,1,0:T(8,128)(2,1)S(1)} %early.1, bf16[2,4,128,128]{3,2,1,0:T(8,128)(2,1)S(1)} %get-tuple-element.74.mine1, bf16[2,4,128,128]{3,2,1,0:T(8,128)(2,1)S(1)} %collective-permute-done.14.theirs1), custom_call_target="tpu_custom_call" | custom-call | tf_op jit(solution)/shard_map/place/pallas_call | solution.py:497
  (1 shorter events, 0.0 us)
Async XLA Ops:
  1.9 4.9 %collective-permute-start = (bf16[4,4,128,128]{3,2,1,0:T(8,128)(2,1)S(1)}, bf16[4,4,128,128]{3,2,1,0:T(8,128)(2,1)S(1)}, u32[]{:S(2)}, u32[]{:S(2)}) collective-permute-start(bf16[4,4,128,128]{3,2,1,0:T(8,128)(2,1)S(1)} %get-tuple-element.44), channel_id=1, source_target_pairs={{0,1},{1,0},{2,3},{3,2},{4,5},{5,4},{6,7},{7,6},{8,9},{9,8},{10,11... | collective-permute-start | bytes 1572872 | tf_op jit(solution)/shard_map/ppermute | solution.py:510
  7.8 4.9 %collective-permute-start.1 = (bf16[544,128]{1,0:T(8,128)(2,1)S(1)}, bf16[544,128]{1,0:T(8,128)(2,1)S(1)}, u32[]{:S(2)}, u32[]{:S(2)}) collective-permute-start(bf16[544,128]{1,0:T(8,128)(2,1)S(1)} %get-tuple-element.52), channel_id=1, source_target_pairs={{0,2},{1,3},{2,0},{3,1},{4,6},{5,7},{6,4},{7,5},{8,10},{9,11},{10,... | collective-permute-start | bytes 417800 | tf_op jit(solution)/shard_map/ppermute | solution.py:510
  7.8 8.6 %collective-permute-start.2 = (bf16[544,128]{1,0:T(8,128)(2,1)S(1)}, bf16[544,128]{1,0:T(8,128)(2,1)S(1)}, u32[]{:S(2)}, u32[]{:S(2)}) collective-permute-start(bf16[544,128]{1,0:T(8,128)(2,1)S(1)} %get-tuple-element.53), channel_id=1, source_target_pairs={{0,4},{1,5},{2,6},{3,7},{4,0},{5,1},{6,2},{7,3},{8,12},{9,13},{10,... | collective-permute-start | bytes 417800 | tf_op jit(solution)/shard_map/ppermute | solution.py:510
  10.0 8.9 %collective-permute-start.3 = (bf16[544,128]{1,0:T(8,128)(2,1)S(1)}, bf16[544,128]{1,0:T(8,128)(2,1)S(1)}, u32[]{:S(2)}, u32[]{:S(2)}) collective-permute-start(bf16[544,128]{1,0:T(8,128)(2,1)S(1)} %get-tuple-element.54), channel_id=1, source_target_pairs={{0,6},{1,7},{2,4},{3,5},{4,2},{5,3},{6,0},{7,1},{8,14},{9,15},{10,... | collective-permute-start | bytes 417800 | tf_op jit(solution)/shard_map/ppermute | solution.py:510
  19.9 4.7 %collective-permute-start.4 = (bf16[544,128]{1,0:T(8,128)(2,1)S(1)}, bf16[544,128]{1,0:T(8,128)(2,1)S(1)}, u32[]{:S(2)}, u32[]{:S(2)}) collective-permute-start(bf16[544,128]{1,0:T(8,128)(2,1)S(1)} %get-tuple-element.57.g), channel_id=1, source_target_pairs={{0,8},{1,9},{2,10},{3,11},{4,12},{5,13},{6,14},{7,15},{8,0},{9,1},... | collective-permute-start | bytes 417800 | tf_op jit(solution)/shard_map/ppermute | solution.py:515
  21.6 8.7 %collective-permute-start.6 = (bf16[4,64,128]{2,1,0:T(8,128)(2,1)S(1)}, bf16[4,64,128]{2,1,0:T(8,128)(2,1)S(1)}, u32[]{:S(2)}, u32[]{:S(2)}) collective-permute-start(bf16[4,64,128]{2,1,0:T(8,128)(2,1)S(1)} %get-tuple-element.58), channel_id=1, source_target_pairs={{0,16},{1,17},{2,18},{3,19},{4,20},{5,21},{6,22},{7,23},{8,24},{9,... | collective-permute-start | bytes 196616 | tf_op jit(solution)/shard_map/ppermute | solution.py:515
  24.6 5.8 %collective-permute-start.5 = (bf16[4,64,128]{2,1,0:T(8,128)(2,1)S(1)}, bf16[4,64,128]{2,1,0:T(8,128)(2,1)S(1)}, u32[]{:S(2)}, u32[]{:S(2)}) collective-permute-start(bf16[4,64,128]{2,1,0:T(8,128)(2,1)S(1)} %get-tuple-element.58), channel_id=1, source_target_pairs={{0,24},{1,25},{2,26},{3,27},{4,28},{5,29},{6,30},{7,31},{8,16},{9,... | collective-permute-start | bytes 196616 | tf_op jit(solution)/shard_map/ppermute | solution.py:515
  25.2 6.3 %collective-permute-start.7 = (f32[8,128]{1,0:T(8,128)S(1)}, f32[8,128]{1,0:T(8,128)S(1)}, u32[]{:S(2)}, u32[]{:S(2)}) collective-permute-start(f32[8,128]{1,0:T(8,128)S(1)} %get-tuple-element.59), channel_id=1, source_target_pairs={{0,24},{1,25},{2,26},{3,27},{4,28},{5,29},{6,30},{7,31},{8,16},{9,... | collective-permute-start | bytes 12296 | tf_op jit(solution)/shard_map/ppermute | solution.py:515
  31.6 7.3 %collective-permute-start.8 = (bf16[4,4,32,128]{3,2,1,0:T(8,128)(2,1)S(1)}, bf16[4,4,32,128]{3,2,1,0:T(8,128)(2,1)S(1)}, u32[]{:S(2)}, u32[]{:S(2)}) collective-permute-start(bf16[4,4,32,128]{3,2,1,0:T(8,128)(2,1)S(1)} %top.1), channel_id=1, source_target_pairs={{0,48},{1,49},{2,50},{3,51},{4,52},{5,53},{6,54},{7,55},{8,56},{9,... | collective-permute-start | bytes 393224 | tf_op jit(solution)/shard_map/ppermute | solution.py:515
  34.2 4.6 %collective-permute-start.9 = (f32[8,128]{1,0:T(8,128)S(1)}, f32[8,128]{1,0:T(8,128)S(1)}, u32[]{:S(2)}, u32[]{:S(2)}) collective-permute-start(f32[8,128]{1,0:T(8,128)S(1)} %get-tuple-element.67), channel_id=1, source_target_pairs={{0,48},{1,49},{2,50},{3,51},{4,52},{5,53},{6,54},{7,55},{8,56},{9,... | collective-permute-start | bytes 12296 | tf_op jit(solution)/shard_map/ppermute | solution.py:515
  40.2 4.2 %collective-permute-start.10 = (bf16[544,128]{1,0:T(8,128)(2,1)S(1)}, bf16[544,128]{1,0:T(8,128)(2,1)S(1)}, u32[]{:S(2)}, u32[]{:S(2)}) collective-permute-start(bf16[544,128]{1,0:T(8,128)(2,1)S(1)} %get-tuple-element.69), channel_id=1, source_target_pairs={{0,2},{1,3},{2,0},{3,1},{4,6},{5,7},{6,4},{7,5},{8,10},{9,11},{10,... | collective-permute-start | bytes 417800 | tf_op jit(solution)/shard_map/ppermute | solution.py:510
  40.3 11.8 %collective-permute-start.12 = (bf16[544,128]{1,0:T(8,128)(2,1)S(1)}, bf16[544,128]{1,0:T(8,128)(2,1)S(1)}, u32[]{:S(2)}, u32[]{:S(2)}) collective-permute-start(bf16[544,128]{1,0:T(8,128)(2,1)S(1)} %get-tuple-element.72), channel_id=1, source_target_pairs={{0,4},{1,5},{2,6},{3,7},{4,0},{5,1},{6,2},{7,3},{8,12},{9,13},{10,... | collective-permute-start | bytes 417800 | tf_op jit(solution)/shard_map/ppermute | solution.py:510
  41.7 10.4 %collective-permute-start.13 = (bf16[544,128]{1,0:T(8,128)(2,1)S(1)}, bf16[544,128]{1,0:T(8,128)(2,1)S(1)}, u32[]{:S(2)}, u32[]{:S(2)}) collective-permute-start(bf16[544,128]{1,0:T(8,128)(2,1)S(1)} %get-tuple-element.73), channel_id=1, source_target_pairs={{0,6},{1,7},{2,4},{3,5},{4,2},{5,3},{6,0},{7,1},{8,14},{9,15},{10,... | collective-permute-start | bytes 417800 | tf_op jit(solution)/shard_map/ppermute | solution.py:510
  45.3 9.9 %collective-permute-start.11 = (bf16[2,4,128,128]{3,2,1,0:T(8,128)(2,1)S(1)}, bf16[2,4,128,128]{3,2,1,0:T(8,128)(2,1)S(1)}, u32[]{:S(2)}, u32[]{:S(2)}) collective-permute-start(bf16[2,4,128,128]{3,2,1,0:T(8,128)(2,1)S(1)} %get-tuple-element.71), channel_id=1, source_target_pairs={{0,1},{1,0},{2,3},{3,2},{4,5},{5,4},{6,7},{7,6},{8,9},{9,8},{10,11... | collective-permute-start | bytes 786440 | tf_op jit(solution)/shard_map/ppermute | solution.py:510
  53.0 3.3 %collective-permute-start.14 = (bf16[2,4,128,128]{3,2,1,0:T(8,128)(2,1)S(1)}, bf16[2,4,128,128]{3,2,1,0:T(8,128)(2,1)S(1)}, u32[]{:S(2)}, u32[]{:S(2)}) collective-permute-start(bf16[2,4,128,128]{3,2,1,0:T(8,128)(2,1)S(1)} %get-tuple-element.75), channel_id=1, source_target_pairs={{0,1},{1,0},{2,3},{3,2},{4,5},{5,4},{6,7},{7,6},{8,9},{9,8},{10,11... | collective-permute-start | bytes 786440 | tf_op jit(solution)/shard_map/ppermute | solution.py:510

commit v6 on v5

--- a/solution.py
+++ b/solution.py
@@ -238,17 +238,25 @@
     )
 
 
-def near_kernel(m0, m1, m2, m3, outs, stats, g, g4):
+def first_kernel(m0, m1, first, first_found):
+    q, k, v, do = (join([tensor(m0, t), tensor(m1, t)]) for t in range(4))
+    ((more, total),) = attend((q, k, v))
+    first[...] = more
+    first_found[0], first_found[1] = total, dotted(do, more)
+
+
+def near_kernel(m0, m1, m2, m3, first, first_found, outs, stats, g, g4):
     refs = (m0, m1, m2, m3)
     stat = [unpack(ref[BODY:]) for ref in refs]
     out = [None] * 4
     blocks = [
-        [join([tensor(refs[pair], t), tensor(refs[pair + 1], t)]) for t in range(4)]
-        for pair in (0, 2)
-    ]
-    blocks.append([join([tensor(ref, t, 64) for ref in refs]) for t in range(4)])
+        [join([tensor(m2, t), tensor(m3, t)]) for t in range(4)],
+        [join([tensor(ref, t, 64) for ref in refs]) for t in range(4)],
+    ]
     found = attend(*(block[:3] for block in blocks))
     deltas = [dotted(block[3], more) for block, (more, _) in zip(blocks, found)]
+    found = [(first[...], first_found[0]), *found]
+    deltas = [first_found[1], *deltas]
     for pair in (0, 2):
         more, total = found[pair // 2]
         joined, _, added = combine(stack(stat[pair : pair + 2]), total, deltas[pair // 2])
@@ -549,8 +557,9 @@
     sent = [kept, *sent]
     (others,) = call(alone_kernel, "alone", [chip_stats], places, stats_own, stats_sent)
     got = [sent[0]] + [in_plane(sent[step], 2 * step) for step in (1, 2, 3)]
+    first = call(first_kernel, "first", [((SEG, WIDTH), F32), seg_stats], *got[:2])
     outs, stats, g, g4 = call(
-        near_kernel, "near", [quads, quad_stats, message, ((4, 64, WIDTH), BF16)], *got
+        near_kernel, "near", [quads, quad_stats, message, ((4, 64, WIDTH), BF16)], *got, *first
     )
     (below,) = call(below_kernel, "below", [((4, 3, ROWS, WIDTH), F32)], *got, stats)
     a1 = across(g, 1)

time: 57.7 us -> 57.5 us (level)
  waiting for transfers between devices: 11.7 us -> 11.1 us
    ppermute x9, waiting for transfers between devices: 8.17 us -> 7.56 us  [in_plane(): return lax.ppermute(array, 'ctx', moves)]
    pallas_call x15 -> x16, Pallas kernels: 11.4 us -> 11.8 us  [call(): pl.pallas_call(kernel, name=name, out_shape=tuple((jax.ShapeDtypeStruct(s...]
  transfers between devices with their start and end apart: 15 -> 15, of which waited for: 8 -> 8; matrix products, arithmetic and copies ran while one was open for 0% -> 0% of each run, Pallas kernels for 10% -> 11%
where the time goes in v6:
time: 57.5 us; the launch traced here: 57.4 us
  starting transfers between devices  33.6 us (58%)
  Pallas kernels  11.8 us (21%)
  waiting for transfers between devices  11.1 us (19%)
  between operations  0.89 us (2%)
    ppermute x9, starting transfers between devices, in_plane(): return lax.ppermute(array, 'ctx', moves)  20.1 us
    ppermute x6, starting transfers between devices, across(): return lax.ppermute(array, 'ctx', moves)  13.5 us
    pallas_call x16, Pallas kernels, call(): pl.pallas_call(kernel, name=name, out_shape=tuple((jax.ShapeDtypeStruct(s...  11.8 us
    ppermute x9, waiting for transfers between devices, in_plane(): return lax.ppermute(array, 'ctx', moves)  7.56 us
    ppermute x6, waiting for transfers between devices, across(): return lax.ppermute(array, 'ctx', moves)  3.53 us
  transfers between devices with their start and end apart: 15, of which 8 were waited for; matrix products, arithmetic and copies ran while one was open for 0% of the time, Pallas kernels for 11%

profile of v6, /device:TPU:1, one launch (start us, length us, event | category | flops | bytes accessed | tf_op | source)
XLA Modules:
  0.0 57.4 jit_solution(5424850533892479011)
XLA Ops:
  0.6 1.3 %split.1 = (bf16[128,1024]{1,0:T(8,128)(2,1)S(1)}, bf16[128,1024]{1,0:T(8,128)(2,1)S(1)}, bf16[128,1024]{1,0:T(8,128)(2,1)S(1)}, bf16[128,1024]{1,0:T(8,128)(2,1)S(1)}, bf16[4,4,128,128]{3,2,1,0:T(8,128)(2,1)S(1)}) custom-call(bf16[128,1024]{1,0:T(8,128)(2,1)} %q.1, bf16[128,1024]{1,0:T(8,128)(2,1)} %k.1, bf16[128,1024]{1,0:T(8,128)(2,1)} %v.1, ...), custom_call_target="tpu_custom_call" | custom-call | tf_op jit(solution)/shard_map/split/pallas_call | solution.py:505
  1.9 3.3 %collective-permute-start = (bf16[4,4,128,128]{3,2,1,0:T(8,128)(2,1)S(1)}, bf16[4,4,128,128]{3,2,1,0:T(8,128)(2,1)S(1)}, u32[]{:S(2)}, u32[]{:S(2)}) collective-permute-start(bf16[4,4,128,128]{3,2,1,0:T(8,128)(2,1)S(1)} %get-tuple-element.46), channel_id=1, source_target_pairs={{0,1},{1,0},{2,3},{3,2},{4,5},{5,4},{6,7},{7,6},{8,9},{9,8},{10,11... | collective-permute-start | bytes 1572872 | tf_op jit(solution)/shard_map/ppermute | solution.py:518
  5.2 0.8 %maps.1 = (bf16[4,128,256]{2,1,0:T(8,128)(2,1)S(1)}, bf16[4,256,128]{2,1,0:T(8,128)(2,1)S(1)}) custom-call(s32[6,8]{1,0:T(8,128)} %offs_left.1), custom_call_target="tpu_custom_call" | custom-call | tf_op jit(solution)/shard_map/maps/pallas_call | solution.py:505
  6.1 0.7 %collective-permute-done.theirs = bf16[4,4,128,128]{3,2,1,0:T(8,128)(2,1)S(1)} collective-permute-done((bf16[4,4,128,128]{3,2,1,0:T(8,128)(2,1)S(1)}, bf16[4,4,128,128]{3,2,1,0:T(8,128)(2,1)S(1)}, u32[]{:S(2)}, u32[]{:S(2)}) %collective-permute-start) | collective-permute-done | bytes 524320 | tf_op jit(solution)/shard_map/ppermute | solution.py:518
  6.8 1.0 %chip.3 = (bf16[544,128]{1,0:T(8,128)(2,1)S(1)}, bf16[544,128]{1,0:T(8,128)(2,1)S(1)}, bf16[544,128]{1,0:T(8,128)(2,1)S(1)}, f32[3,256,128]{2,1,0:T(8,128)S(1)}, f32[3,2,256,128]{3,2,1,0:T(8,128)S(1)}) custom-call(bf16[128,1024]{1,0:T(8,128)(2,1)S(1)} %get-tuple-element.42.q, bf16[128,1024]{1,0:T(8,128)(2,1)S(1)} %get-tuple-element.43.k, ...), custom_call_target="tpu_custom_call" | custom-call | tf_op jit(solution)/shard_map/chip/pallas_call | solution.py:505
  7.8 0.0 collective-permute-start.1
  7.8 2.2 %collective-permute-start.2 = (bf16[544,128]{1,0:T(8,128)(2,1)S(1)}, bf16[544,128]{1,0:T(8,128)(2,1)S(1)}, u32[]{:S(2)}, u32[]{:S(2)}) collective-permute-start(bf16[544,128]{1,0:T(8,128)(2,1)S(1)} %get-tuple-element.55), channel_id=1, source_target_pairs={{0,4},{1,5},{2,6},{3,7},{4,0},{5,1},{6,2},{7,3},{8,12},{9,13},{10,... | collective-permute-start | bytes 417800 | tf_op jit(solution)/shard_map/ppermute | solution.py:518
  10.0 1.7 %collective-permute-start.3 = (bf16[544,128]{1,0:T(8,128)(2,1)S(1)}, bf16[544,128]{1,0:T(8,128)(2,1)S(1)}, u32[]{:S(2)}, u32[]{:S(2)}) collective-permute-start(bf16[544,128]{1,0:T(8,128)(2,1)S(1)} %get-tuple-element.56), channel_id=1, source_target_pairs={{0,6},{1,7},{2,4},{3,5},{4,2},{5,3},{6,0},{7,1},{8,14},{9,15},{10,... | collective-permute-start | bytes 417800 | tf_op jit(solution)/shard_map/ppermute | solution.py:518
  11.7 0.8 %chip.2 = (bf16[544,128]{1,0:T(8,128)(2,1)S(1)}, f32[1,256,128]{2,1,0:T(8,128)S(1)}, f32[1,2,256,128]{3,2,1,0:T(8,128)S(1)}) custom-call(bf16[128,1024]{1,0:T(8,128)(2,1)S(1)} %get-tuple-element.42.q, bf16[128,1024]{1,0:T(8,128)(2,1)S(1)} %get-tuple-element.43.k, bf16[128,1024]{1,0:T(8,128)(2,1)S(1)} %get-tuple-element.44.v, ...), custom_call_target="tpu_custom_call" | custom-call | tf_op jit(solution)/shard_map/chip/pallas_call | solution.py:505
  12.5 0.2 collective-permute-done.1.m1
  12.7 0.6 %first.1 = (f32[256,128]{1,0:T(8,128)S(1)}, f32[2,256,128]{2,1,0:T(8,128)S(1)}) custom-call(bf16[544,128]{1,0:T(8,128)(2,1)S(1)} %get-tuple-element.53.m0, bf16[544,128]{1,0:T(8,128)(2,1)S(1)} %collective-permute-done.1.m1), custom_call_target="tpu_custom_call" | custom-call | tf_op jit(solution)/shard_map/first/pallas_call | solution.py:505
  13.3 3.1 %collective-permute-done.2.m2 = bf16[544,128]{1,0:T(8,128)(2,1)S(1)} collective-permute-done((bf16[544,128]{1,0:T(8,128)(2,1)S(1)}, bf16[544,128]{1,0:T(8,128)(2,1)S(1)}, u32[]{:S(2)}, u32[]{:S(2)}) %collective-permute-start.2) | collective-permute-done | bytes 139296 | tf_op jit(solution)/shard_map/ppermute | solution.py:518
  16.4 2.5 %collective-permute-done.3.m3 = bf16[544,128]{1,0:T(8,128)(2,1)S(1)} collective-permute-done((bf16[544,128]{1,0:T(8,128)(2,1)S(1)}, bf16[544,128]{1,0:T(8,128)(2,1)S(1)}, u32[]{:S(2)}, u32[]{:S(2)}) %collective-permute-start.3) | collective-permute-done | bytes 139296 | tf_op jit(solution)/shard_map/ppermute | solution.py:518
  18.9 0.8 %near.1 = (f32[4,128,128]{2,1,0:T(8,128)S(1)}, f32[4,2,128,128]{3,2,1,0:T(8,128)S(1)}, bf16[544,128]{1,0:T(8,128)(2,1)S(1)}, bf16[4,64,128]{2,1,0:T(8,128)(2,1)S(1)}) custom-call(bf16[544,128]{1,0:T(8,128)(2,1)S(1)} %get-tuple-element.53.m0, bf16[544,128]{1,0:T(8,128)(2,1)S(1)} %collective-permute-done.1.m1, bf16[544,128]{1,0:T(8,128)(2,1)S(1)} %collective-permute-done.2.m2, ...), custom_call_target="tpu_custom_call" | custom-call | tf_op jit(solution)/shard_map/near/pallas_call | solution.py:505
  19.7 1.7 %collective-permute-start.4 = (bf16[544,128]{1,0:T(8,128)(2,1)S(1)}, bf16[544,128]{1,0:T(8,128)(2,1)S(1)}, u32[]{:S(2)}, u32[]{:S(2)}) collective-permute-start(bf16[544,128]{1,0:T(8,128)(2,1)S(1)} %get-tuple-element.61.g), channel_id=1, source_target_pairs={{0,8},{1,9},{2,10},{3,11},{4,12},{5,13},{6,14},{7,15},{8,0},{9,1},... | collective-permute-start | bytes 417800 | tf_op jit(solution)/shard_map/ppermute | solution.py:523
  21.4 3.0 %collective-permute-start.6 = (bf16[4,64,128]{2,1,0:T(8,128)(2,1)S(1)}, bf16[4,64,128]{2,1,0:T(8,128)(2,1)S(1)}, u32[]{:S(2)}, u32[]{:S(2)}) collective-permute-start(bf16[4,64,128]{2,1,0:T(8,128)(2,1)S(1)} %get-tuple-element.62), channel_id=1, source_target_pairs={{0,16},{1,17},{2,18},{3,19},{4,20},{5,21},{6,22},{7,23},{8,24},{9,... | collective-permute-start | bytes 196616 | tf_op jit(solution)/shard_map/ppermute | solution.py:523
  24.4 0.0 collective-permute-start.5
  24.4 0.0 collective-permute-done.4.a1
  24.4 0.6 %pair.1 = (f32[128,128]{1,0:T(8,128)S(1)}, f32[2,256,128]{2,1,0:T(8,128)S(1)}, f32[8,128]{1,0:T(8,128)S(1)}) custom-call(bf16[544,128]{1,0:T(8,128)(2,1)S(1)} %get-tuple-element.61.g, bf16[544,128]{1,0:T(8,128)(2,1)S(1)} %collective-permute-done.4.a1), custom_call_target="tpu_custom_call" | custom-call | tf_op jit(solution)/shard_map/pair/pallas_call | solution.py:505
  25.0 5.0 %collective-permute-start.7 = (f32[8,128]{1,0:T(8,128)S(1)}, f32[8,128]{1,0:T(8,128)S(1)}, u32[]{:S(2)}, u32[]{:S(2)}) collective-permute-start(f32[8,128]{1,0:T(8,128)S(1)} %get-tuple-element.63), channel_id=1, source_target_pairs={{0,24},{1,25},{2,26},{3,27},{4,28},{5,29},{6,30},{7,31},{8,16},{9,... | collective-permute-start | bytes 12296 | tf_op jit(solution)/shard_map/ppermute | solution.py:523
  30.0 0.0 collective-permute-done.6.a2
  30.0 0.1 collective-permute-done.5.a3
  30.2 1.2 %collective-permute-done.7.message3 = f32[8,128]{1,0:T(8,128)S(1)} collective-permute-done((f32[8,128]{1,0:T(8,128)S(1)}, f32[8,128]{1,0:T(8,128)S(1)}, u32[]{:S(2)}, u32[]{:S(2)}) %collective-permute-start.7) | collective-permute-done | bytes 4128 | tf_op jit(solution)/shard_map/ppermute | solution.py:523
  31.4 2.0 %collective-permute-start.8 = (bf16[4,4,32,128]{3,2,1,0:T(8,128)(2,1)S(1)}, bf16[4,4,32,128]{3,2,1,0:T(8,128)(2,1)S(1)}, u32[]{:S(2)}, u32[]{:S(2)}) collective-permute-start(bf16[4,4,32,128]{3,2,1,0:T(8,128)(2,1)S(1)} %top.1), channel_id=1, source_target_pairs={{0,48},{1,49},{2,50},{3,51},{4,52},{5,53},{6,54},{7,55},{8,56},{9,... | collective-permute-start | bytes 393224 | tf_op jit(solution)/shard_map/ppermute | solution.py:523
  33.4 0.7 %quad.1 = (f32[128,128]{1,0:T(8,128)S(1)}, f32[2,256,128]{2,1,0:T(8,128)S(1)}, f32[8,128]{1,0:T(8,128)S(1)}) custom-call(bf16[544,128]{1,0:T(8,128)(2,1)S(1)} %get-tuple-element.61.g, bf16[544,128]{1,0:T(8,128)(2,1)S(1)} %collective-permute-done.4.a1, bf16[4,64,128]{2,1,0:T(8,128)(2,1)S(1)} %collective-permute-done.5.a3, ...), custom_call_target="tpu_custom_call" | custom-call | tf_op jit(solution)/shard_map/quad/pallas_call | solution.py:505
  34.0 1.7 %collective-permute-start.9 = (f32[8,128]{1,0:T(8,128)S(1)}, f32[8,128]{1,0:T(8,128)S(1)}, u32[]{:S(2)}, u32[]{:S(2)}) collective-permute-start(f32[8,128]{1,0:T(8,128)S(1)} %get-tuple-element.71), channel_id=1, source_target_pairs={{0,48},{1,49},{2,50},{3,51},{4,52},{5,53},{6,54},{7,55},{8,56},{9,... | collective-permute-start | bytes 12296 | tf_op jit(solution)/shard_map/ppermute | solution.py:523
  35.8 0.7 %below.1 = f32[4,3,128,128]{3,2,1,0:T(8,128)S(1)} custom-call(bf16[544,128]{1,0:T(8,128)(2,1)S(1)} %get-tuple-element.53.m0, bf16[544,128]{1,0:T(8,128)(2,1)S(1)} %collective-permute-done.1.m1, bf16[544,128]{1,0:T(8,128)(2,1)S(1)} %collective-permute-done.2.m2, bf16[544,128]{1,0:T(8,128)(2,1)S(1)} %collective-permute-done.3.m3, ...), custom_call_target="tpu_custom_call" | custom-call | tf_op jit(solution)/shard_map/below/pallas_call | solution.py:505
  36.5 2.2 %collective-permute-done.9.message5 = f32[8,128]{1,0:T(8,128)S(1)} collective-permute-done((f32[8,128]{1,0:T(8,128)S(1)}, f32[8,128]{1,0:T(8,128)S(1)}, u32[]{:S(2)}, u32[]{:S(2)}) %collective-permute-start.9) | collective-permute-done | bytes 4128 | tf_op jit(solution)/shard_map/ppermute | solution.py:523
  38.7 0.0 collective-permute-done.8.far5
  38.7 1.3 %rest.1 = (bf16[544,128]{1,0:T(8,128)(2,1)S(1)}, bf16[544,128]{1,0:T(8,128)(2,1)S(1)}, bf16[544,128]{1,0:T(8,128)(2,1)S(1)}, bf16[544,128]{1,0:T(8,128)(2,1)S(1)}) custom-call(bf16[544,128]{1,0:T(8,128)(2,1)S(1)} %get-tuple-element.53.m0, bf16[544,128]{1,0:T(8,128)(2,1)S(1)} %collective-permute-done.1.m1, bf16[544,128]{1,0:T(8,128)(2,1)S(1)} %collective-permute-done.2.m2, ...), custom_call_target="tpu_custom_call" | custom-call | tf_op jit(solution)/shard_map/rest/pallas_call | solution.py:505
  39.9 0.1 collective-permute-start.10
  40.0 1.4 %collective-permute-start.12 = (bf16[544,128]{1,0:T(8,128)(2,1)S(1)}, bf16[544,128]{1,0:T(8,128)(2,1)S(1)}, u32[]{:S(2)}, u32[]{:S(2)}) collective-permute-start(bf16[544,128]{1,0:T(8,128)(2,1)S(1)} %get-tuple-element.76), channel_id=1, source_target_pairs={{0,4},{1,5},{2,6},{3,7},{4,0},{5,1},{6,2},{7,3},{8,12},{9,13},{10,... | collective-permute-start | bytes 417800 | tf_op jit(solution)/shard_map/ppermute | solution.py:518
  41.5 2.4 %collective-permute-start.13 = (bf16[544,128]{1,0:T(8,128)(2,1)S(1)}, bf16[544,128]{1,0:T(8,128)(2,1)S(1)}, u32[]{:S(2)}, u32[]{:S(2)}) collective-permute-start(bf16[544,128]{1,0:T(8,128)(2,1)S(1)} %get-tuple-element.77), channel_id=1, source_target_pairs={{0,6},{1,7},{2,4},{3,5},{4,2},{5,3},{6,0},{7,1},{8,14},{9,15},{10,... | collective-permute-start | bytes 417800 | tf_op jit(solution)/shard_map/ppermute | solution.py:518
  43.9 0.2 alone.1.others
  44.1 0.0 collective-permute-done.10.c1
  44.1 1.0 %finish.2 = (bf16[2,4,128,128]{3,2,1,0:T(8,128)(2,1)S(1)}, bf16[2,4,128,128]{3,2,1,0:T(8,128)(2,1)S(1)}) custom-call(bf16[128,1024]{1,0:T(8,128)(2,1)S(1)} %get-tuple-element.42.q, bf16[128,1024]{1,0:T(8,128)(2,1)S(1)} %get-tuple-element.43.k, bf16[128,1024]{1,0:T(8,128)(2,1)S(1)} %get-tuple-element.44.v, bf16[128,1024]{1,0:T(8,128)(2,1)S(1)} %get-tuple-element.45.do, ...), custom_call_target="tpu_custom_call" | custom-call | tf_op jit(solution)/shard_map/finish/pallas_call | solution.py:505
  45.1 6.8 %collective-permute-start.11 = (bf16[2,4,128,128]{3,2,1,0:T(8,128)(2,1)S(1)}, bf16[2,4,128,128]{3,2,1,0:T(8,128)(2,1)S(1)}, u32[]{:S(2)}, u32[]{:S(2)}) collective-permute-start(bf16[2,4,128,128]{3,2,1,0:T(8,128)(2,1)S(1)} %get-tuple-element.75), channel_id=1, source_target_pairs={{0,1},{1,0},{2,3},{3,2},{4,5},{5,4},{6,7},{7,6},{8,9},{9,8},{10,11... | collective-permute-start | bytes 786440 | tf_op jit(solution)/shard_map/ppermute | solution.py:518
  51.9 0.0 collective-permute-done.12.c0
  51.9 0.0 collective-permute-done.13.c1
  51.9 1.0 %finish.3 = (bf16[2,4,128,128]{3,2,1,0:T(8,128)(2,1)S(1)}, bf16[2,4,128,128]{3,2,1,0:T(8,128)(2,1)S(1)}) custom-call(bf16[128,1024]{1,0:T(8,128)(2,1)S(1)} %get-tuple-element.42.q, bf16[128,1024]{1,0:T(8,128)(2,1)S(1)} %get-tuple-element.43.k, bf16[128,1024]{1,0:T(8,128)(2,1)S(1)} %get-tuple-element.44.v, bf16[128,1024]{1,0:T(8,128)(2,1)S(1)} %get-tuple-element.45.do, ...), custom_call_target="tpu_custom_call" | custom-call | tf_op jit(solution)/shard_map/finish/pallas_call | solution.py:505
  52.8 2.2 %collective-permute-start.14 = (bf16[2,4,128,128]{3,2,1,0:T(8,128)(2,1)S(1)}, bf16[2,4,128,128]{3,2,1,0:T(8,128)(2,1)S(1)}, u32[]{:S(2)}, u32[]{:S(2)}) collective-permute-start(bf16[2,4,128,128]{3,2,1,0:T(8,128)(2,1)S(1)} %get-tuple-element.79), channel_id=1, source_target_pairs={{0,1},{1,0},{2,3},{3,2},{4,5},{5,4},{6,7},{7,6},{8,9},{9,8},{10,11... | collective-permute-start | bytes 786440 | tf_op jit(solution)/shard_map/ppermute | solution.py:518
  55.0 0.0 collective-permute-done.11.theirs0
  55.0 0.1 early.1
  55.2 1.0 %collective-permute-done.14.theirs1 = bf16[2,4,128,128]{3,2,1,0:T(8,128)(2,1)S(1)} collective-permute-done((bf16[2,4,128,128]{3,2,1,0:T(8,128)(2,1)S(1)}, bf16[2,4,128,128]{3,2,1,0:T(8,128)(2,1)S(1)}, u32[]{:S(2)}, u32[]{:S(2)}) %collective-permute-start.14) | collective-permute-done | bytes 262176 | tf_op jit(solution)/shard_map/ppermute | solution.py:518
  56.2 1.0 %place.1 = (bf16[128,1024]{1,0:T(8,128)(2,1)}, bf16[128,1024]{1,0:T(8,128)(2,1)}, bf16[128,1024]{1,0:T(8,128)(2,1)}, bf16[128,1024]{1,0:T(8,128)(2,1)}) custom-call(bf16[4,128,1024]{2,1,0:T(8,128)(2,1)S(1)} %early.1, bf16[2,4,128,128]{3,2,1,0:T(8,128)(2,1)S(1)} %get-tuple-element.78.mine1, bf16[2,4,128,128]{3,2,1,0:T(8,128)(2,1)S(1)} %collective-permute-done.14.theirs1), custom_call_target="tpu_custom_call" | custom-call | tf_op jit(solution)/shard_map/place/pallas_call | solution.py:505
  (1 shorter events, 0.0 us)
Async XLA Ops:
  1.9 4.9 %collective-permute-start = (bf16[4,4,128,128]{3,2,1,0:T(8,128)(2,1)S(1)}, bf16[4,4,128,128]{3,2,1,0:T(8,128)(2,1)S(1)}, u32[]{:S(2)}, u32[]{:S(2)}) collective-permute-start(bf16[4,4,128,128]{3,2,1,0:T(8,128)(2,1)S(1)} %get-tuple-element.46), channel_id=1, source_target_pairs={{0,1},{1,0},{2,3},{3,2},{4,5},{5,4},{6,7},{7,6},{8,9},{9,8},{10,11... | collective-permute-start | bytes 1572872 | tf_op jit(solution)/shard_map/ppermute | solution.py:518
  7.8 4.9 %collective-permute-start.1 = (bf16[544,128]{1,0:T(8,128)(2,1)S(1)}, bf16[544,128]{1,0:T(8,128)(2,1)S(1)}, u32[]{:S(2)}, u32[]{:S(2)}) collective-permute-start(bf16[544,128]{1,0:T(8,128)(2,1)S(1)} %get-tuple-element.54), channel_id=1, source_target_pairs={{0,2},{1,3},{2,0},{3,1},{4,6},{5,7},{6,4},{7,5},{8,10},{9,11},{10,... | collective-permute-start | bytes 417800 | tf_op jit(solution)/shard_map/ppermute | solution.py:518
  7.8 8.6 %collective-permute-start.2 = (bf16[544,128]{1,0:T(8,128)(2,1)S(1)}, bf16[544,128]{1,0:T(8,128)(2,1)S(1)}, u32[]{:S(2)}, u32[]{:S(2)}) collective-permute-start(bf16[544,128]{1,0:T(8,128)(2,1)S(1)} %get-tuple-element.55), channel_id=1, source_target_pairs={{0,4},{1,5},{2,6},{3,7},{4,0},{5,1},{6,2},{7,3},{8,12},{9,13},{10,... | collective-permute-start | bytes 417800 | tf_op jit(solution)/shard_map/ppermute | solution.py:518
  10.0 8.9 %collective-permute-start.3 = (bf16[544,128]{1,0:T(8,128)(2,1)S(1)}, bf16[544,128]{1,0:T(8,128)(2,1)S(1)}, u32[]{:S(2)}, u32[]{:S(2)}) collective-permute-start(bf16[544,128]{1,0:T(8,128)(2,1)S(1)} %get-tuple-element.56), channel_id=1, source_target_pairs={{0,6},{1,7},{2,4},{3,5},{4,2},{5,3},{6,0},{7,1},{8,14},{9,15},{10,... | collective-permute-start | bytes 417800 | tf_op jit(solution)/shard_map/ppermute | solution.py:518
  19.7 4.7 %collective-permute-start.4 = (bf16[544,128]{1,0:T(8,128)(2,1)S(1)}, bf16[544,128]{1,0:T(8,128)(2,1)S(1)}, u32[]{:S(2)}, u32[]{:S(2)}) collective-permute-start(bf16[544,128]{1,0:T(8,128)(2,1)S(1)} %get-tuple-element.61.g), channel_id=1, source_target_pairs={{0,8},{1,9},{2,10},{3,11},{4,12},{5,13},{6,14},{7,15},{8,0},{9,1},... | collective-permute-start | bytes 417800 | tf_op jit(solution)/shard_map/ppermute | solution.py:523
  21.4 8.7 %collective-permute-start.6 = (bf16[4,64,128]{2,1,0:T(8,128)(2,1)S(1)}, bf16[4,64,128]{2,1,0:T(8,128)(2,1)S(1)}, u32[]{:S(2)}, u32[]{:S(2)}) collective-permute-start(bf16[4,64,128]{2,1,0:T(8,128)(2,1)S(1)} %get-tuple-element.62), channel_id=1, source_target_pairs={{0,16},{1,17},{2,18},{3,19},{4,20},{5,21},{6,22},{7,23},{8,24},{9,... | collective-permute-start | bytes 196616 | tf_op jit(solution)/shard_map/ppermute | solution.py:523
  24.4 5.8 %collective-permute-start.5 = (bf16[4,64,128]{2,1,0:T(8,128)(2,1)S(1)}, bf16[4,64,128]{2,1,0:T(8,128)(2,1)S(1)}, u32[]{:S(2)}, u32[]{:S(2)}) collective-permute-start(bf16[4,64,128]{2,1,0:T(8,128)(2,1)S(1)} %get-tuple-element.62), channel_id=1, source_target_pairs={{0,24},{1,25},{2,26},{3,27},{4,28},{5,29},{6,30},{7,31},{8,16},{9,... | collective-permute-start | bytes 196616 | tf_op jit(solution)/shard_map/ppermute | solution.py:523
  25.0 6.4 %collective-permute-start.7 = (f32[8,128]{1,0:T(8,128)S(1)}, f32[8,128]{1,0:T(8,128)S(1)}, u32[]{:S(2)}, u32[]{:S(2)}) collective-permute-start(f32[8,128]{1,0:T(8,128)S(1)} %get-tuple-element.63), channel_id=1, source_target_pairs={{0,24},{1,25},{2,26},{3,27},{4,28},{5,29},{6,30},{7,31},{8,16},{9,... | collective-permute-start | bytes 12296 | tf_op jit(solution)/shard_map/ppermute | solution.py:523
  31.4 7.3 %collective-permute-start.8 = (bf16[4,4,32,128]{3,2,1,0:T(8,128)(2,1)S(1)}, bf16[4,4,32,128]{3,2,1,0:T(8,128)(2,1)S(1)}, u32[]{:S(2)}, u32[]{:S(2)}) collective-permute-start(bf16[4,4,32,128]{3,2,1,0:T(8,128)(2,1)S(1)} %top.1), channel_id=1, source_target_pairs={{0,48},{1,49},{2,50},{3,51},{4,52},{5,53},{6,54},{7,55},{8,56},{9,... | collective-permute-start | bytes 393224 | tf_op jit(solution)/shard_map/ppermute | solution.py:523
  34.0 4.6 %collective-permute-start.9 = (f32[8,128]{1,0:T(8,128)S(1)}, f32[8,128]{1,0:T(8,128)S(1)}, u32[]{:S(2)}, u32[]{:S(2)}) collective-permute-start(f32[8,128]{1,0:T(8,128)S(1)} %get-tuple-element.71), channel_id=1, source_target_pairs={{0,48},{1,49},{2,50},{3,51},{4,52},{5,53},{6,54},{7,55},{8,56},{9,... | collective-permute-start | bytes 12296 | tf_op jit(solution)/shard_map/ppermute | solution.py:523
  39.9 4.2 %collective-permute-start.10 = (bf16[544,128]{1,0:T(8,128)(2,1)S(1)}, bf16[544,128]{1,0:T(8,128)(2,1)S(1)}, u32[]{:S(2)}, u32[]{:S(2)}) collective-permute-start(bf16[544,128]{1,0:T(8,128)(2,1)S(1)} %get-tuple-element.73), channel_id=1, source_target_pairs={{0,2},{1,3},{2,0},{3,1},{4,6},{5,7},{6,4},{7,5},{8,10},{9,11},{10,... | collective-permute-start | bytes 417800 | tf_op jit(solution)/shard_map/ppermute | solution.py:518
  40.0 11.8 %collective-permute-start.12 = (bf16[544,128]{1,0:T(8,128)(2,1)S(1)}, bf16[544,128]{1,0:T(8,128)(2,1)S(1)}, u32[]{:S(2)}, u32[]{:S(2)}) collective-permute-start(bf16[544,128]{1,0:T(8,128)(2,1)S(1)} %get-tuple-element.76), channel_id=1, source_target_pairs={{0,4},{1,5},{2,6},{3,7},{4,0},{5,1},{6,2},{7,3},{8,12},{9,13},{10,... | collective-permute-start | bytes 417800 | tf_op jit(solution)/shard_map/ppermute | solution.py:518
  41.5 10.4 %collective-permute-start.13 = (bf16[544,128]{1,0:T(8,128)(2,1)S(1)}, bf16[544,128]{1,0:T(8,128)(2,1)S(1)}, u32[]{:S(2)}, u32[]{:S(2)}) collective-permute-start(bf16[544,128]{1,0:T(8,128)(2,1)S(1)} %get-tuple-element.77), channel_id=1, source_target_pairs={{0,6},{1,7},{2,4},{3,5},{4,2},{5,3},{6,0},{7,1},{8,14},{9,15},{10,... | collective-permute-start | bytes 417800 | tf_op jit(solution)/shard_map/ppermute | solution.py:518
  45.1 9.9 %collective-permute-start.11 = (bf16[2,4,128,128]{3,2,1,0:T(8,128)(2,1)S(1)}, bf16[2,4,128,128]{3,2,1,0:T(8,128)(2,1)S(1)}, u32[]{:S(2)}, u32[]{:S(2)}) collective-permute-start(bf16[2,4,128,128]{3,2,1,0:T(8,128)(2,1)S(1)} %get-tuple-element.75), channel_id=1, source_target_pairs={{0,1},{1,0},{2,3},{3,2},{4,5},{5,4},{6,7},{7,6},{8,9},{9,8},{10,11... | collective-permute-start | bytes 786440 | tf_op jit(solution)/shard_map/ppermute | solution.py:518
  52.8 3.4 %collective-permute-start.14 = (bf16[2,4,128,128]{3,2,1,0:T(8,128)(2,1)S(1)}, bf16[2,4,128,128]{3,2,1,0:T(8,128)(2,1)S(1)}, u32[]{:S(2)}, u32[]{:S(2)}) collective-permute-start(bf16[2,4,128,128]{3,2,1,0:T(8,128)(2,1)S(1)} %get-tuple-element.79), channel_id=1, source_target_pairs={{0,1},{1,0},{2,3},{3,2},{4,5},{5,4},{6,7},{7,6},{8,9},{9,8},{10,11... | collective-permute-start | bytes 786440 | tf_op jit(solution)/shard_map/ppermute | solution.py:518
